TPU v7x, 32 devices: a whole 2x2x4 slice. The times are simulated.
32 devices in a mesh: req: 8 (over z, x), kv: 4 (over y, core).
Axes of the slice: x: 2, y: 2, z: 4, core: 2. Of those that a mesh axis runs over, the one named last changes fastest.
Arguments:
- hidden_in: bfloat16 [1024, 1536], P('req'), may hold values from -6 to 6
- attn_gain: float32 [1536], replicated, may hold values from 0.1 to 1.9
- w_query: bfloat16 [1536, 1536], P('kv'), may hold values from -0.15625 to 0.15625
- w_key: bfloat16 [512, 1536], P('kv'), may hold values from -0.15625 to 0.15625
- w_value: bfloat16 [512, 1536], P('kv'), may hold values from -0.15625 to 0.15625
- w_out: bfloat16 [1536, 1536], P('kv'), may hold values from -0.75 to 0.75
- k_cache: bfloat16 [3072, 8, 8192], P('req', 'kv'), may hold values from -600 to 600
- v_cache: bfloat16 [3072, 8, 8192], P('req', 'kv'), may hold values from -6 to 6
- cache_len: int32 [1024], replicated, may hold values from 1 to 384, 196608 in all
- block_slot: int32 [3072], P('req'), may hold values from 0 to 3071, as said below
- moe_gain: float32 [1536], replicated, may hold values from 0.1 to 1.9
- w_router: bfloat16 [1536, 16], replicated, may hold values from -0.15625 to 0.15625
- w_gate_up: bfloat16 [16, 1536, 1024], P('req'), may hold values from -0.15625 to 0.15625
- w_down: bfloat16 [16, 512, 1536], P('req'), may hold values from -0.25 to 0.25
- routes: int32 [1024, 8], P(('req', 'kv')), may hold values from 0 to 15, all different within a row; in each aligned block of 32 rows (0 to 31, 32 to 63, ...) at most 32 rows name the same one
Outputs:
- layer_out: bfloat16 [1024, 1536], P(('req', 'kv'))
Inputs may be any that keep to these rules, and one draw needn't show every extreme that they name: `block_slot`: each value once; the block holds page v % 3 of request v // 3; the blocks of one index of req hold exactly 128 * 3 / 8 pages of the requests of each index of req. `routes`: each row names 8 different experts; in the 32 rows of one device an expert may be named by all of them.
All inputs are finite; a program needn't handle non-finite values.
Results may differ from a plain program's by a relative error of at most 0.02.
The roundings to bfloat16 on the way count: a program that leaves them out, or rounds other values in their place, can miss the bound.
Values may be sent and summed in bfloat16 or wider, within the bound.
No kernel may reach another device: no remote copies, remote signals or barrier semaphores. Data moves between devices by JAX's collectives and lax.ppermute only.
A program may use at most 192 MiB of HBM per device.

v0:
```python
import jax
import jax.numpy as jnp
from jax import lax
from jax.sharding import PartitionSpec as P

HD = 64
FFE = 512
BLK = 128
PAGES = 3


def merged_2(value, axis, join):
    pieces = jax.tree.map(lambda part: lax.all_gather(part, axis), value)
    head = jax.tree.map(lambda part: part[0], pieces)
    tail = jax.tree.map(lambda part: part[1:], pieces)
    so_far, _ = lax.scan(lambda so_far, share: (join(so_far, share), None), head, tail)
    return so_far


def rms_norm(values, gain):
    values = values.astype(jnp.float32)
    return values * lax.rsqrt(jnp.mean(values * values, -1, keepdims=True) + 1e-05) * gain


def rotate(values, positions):
    half_dim = values.shape[-1] // 2
    frequency = 10000.0 ** (-jnp.arange(half_dim, dtype=jnp.float32) / half_dim)
    angles = positions.astype(jnp.float32)[:, None, None] * frequency
    cosines = jnp.cos(angles)
    sines = jnp.sin(angles)
    first_half = values[..., :half_dim]
    second_half = values[..., half_dim:]
    return jnp.concatenate(
        [first_half * cosines - second_half * sines, first_half * sines + second_half * cosines], -1
    )


def project_rows(normed, weight):
    return lax.dot_general(
        normed, weight, (((1,), (1,)), ((), ())), preferred_element_type=jnp.float32
    )


def shards(
    hidden_in,
    attn_gain,
    w_query,
    w_key,
    w_value,
    w_out,
    k_cache,
    v_cache,
    cache_len,
    block_slot,
    moe_gain,
    w_router,
    w_gate_up,
    w_down,
    routes,
):
    req_index = lax.axis_index("req")
    kv_index = lax.axis_index("kv")
    row_count = hidden_in.shape[0]
    heads_dev = w_query.shape[0] // HD
    kv_dev = w_key.shape[0] // HD
    per_group = heads_dev // kv_dev
    block_count = k_cache.shape[0]
    request_count = cache_len.shape[0]
    home_start = req_index * row_count
    lengths_home = lax.dynamic_slice_in_dim(cache_len, home_start, row_count, 0)
    normed = rms_norm(hidden_in, attn_gain).astype(jnp.bfloat16)
    query = project_rows(normed, w_query).reshape(row_count, heads_dev, HD)
    query = (rotate(query, lengths_home) * 0.125).astype(jnp.bfloat16)
    key_new = project_rows(normed, w_key).reshape(row_count, kv_dev, HD)
    key_new = rotate(key_new, lengths_home).astype(jnp.bfloat16)
    value_new = project_rows(normed, w_value).astype(jnp.bfloat16).reshape(row_count, kv_dev, HD)
    queries = lax.all_gather(query.reshape(row_count, heads_dev * HD), "req", axis=0, tiled=True)
    owners = block_slot // PAGES
    pages_of = block_slot % PAGES
    query_blocks = queries[owners].reshape(block_count, kv_dev, per_group, HD)
    cache_keys = k_cache.reshape(block_count, kv_dev, BLK, HD)
    cache_values = v_cache.reshape(block_count, kv_dev, BLK, HD).astype(jnp.float32)
    scores = jnp.einsum(
        "bgqd,bgtd->bgqt", query_blocks, cache_keys, preferred_element_type=jnp.float32
    )
    limits = cache_len[owners]
    usable = pages_of[:, None] * BLK + jnp.arange(BLK, dtype=jnp.int32)[None, :] < limits[:, None]
    usable = usable[:, None, None, :]
    scores = jnp.where(usable, scores, -1e30)
    block_max = jnp.max(scores, -1).reshape(block_count, heads_dev)
    member = owners[None, :] == jnp.arange(request_count, dtype=jnp.int32)[:, None]
    member_float = member.astype(jnp.float32)
    local_max = jnp.max(jnp.where(member[:, :, None], block_max[None, :, :], -1e30), 1)

    def blend_parts(first, second):
        highest = jnp.maximum(first[0], second[0])
        first_scale = jnp.exp(first[0] - highest)
        second_scale = jnp.exp(second[0] - highest)
        first_numer = first[2].reshape(-1, heads_dev, HD) * first_scale[..., None]
        second_numer = second[2].reshape(-1, heads_dev, HD) * second_scale[..., None]
        return (
            highest,
            first[1] * first_scale + second[1] * second_scale,
            (first_numer + second_numer).reshape(-1, heads_dev * HD),
        )

    offsets = local_max[owners].reshape(block_count, kv_dev, per_group)
    weights = jnp.where(usable, jnp.exp(scores - offsets[..., None]), 0.0)
    totals = jnp.sum(weights, -1).reshape(block_count, heads_dev)
    numer = jnp.einsum(
        "bgqt,bgtd->bgqd", weights, cache_values, precision=lax.Precision.HIGHEST
    ).reshape(block_count, heads_dev * HD)
    totals, numer = (totals, numer)
    totals = jnp.dot(member_float, totals, precision=lax.Precision.HIGHEST)
    numer = jnp.dot(member_float, numer, precision=lax.Precision.HIGHEST)
    totals, numer = (totals, numer)
    merged = merged_2((local_max, totals, numer), "req", blend_parts)
    max_home = lax.dynamic_slice_in_dim(merged[0], home_start, row_count, 0)
    totals_home = lax.dynamic_slice_in_dim(merged[1], home_start, row_count, 0)
    numer_home = lax.dynamic_slice_in_dim(merged[2], home_start, row_count, 0)
    own_score = jnp.einsum(
        "rgqd,rgd->rgq",
        query.reshape(row_count, kv_dev, per_group, HD),
        key_new,
        preferred_element_type=jnp.float32,
    ).reshape(row_count, heads_dev)
    highest = jnp.maximum(max_home, own_score)
    old_scale = jnp.exp(max_home - highest)
    new_scale = jnp.exp(own_score - highest)
    total = totals_home * old_scale + new_scale
    spread_value = jnp.broadcast_to(
        value_new.astype(jnp.float32)[:, :, None, :], (row_count, kv_dev, per_group, HD)
    ).reshape(row_count, heads_dev, HD)
    numer_all = (
        numer_home.reshape(row_count, heads_dev, HD) * old_scale[..., None]
        + new_scale[..., None] * spread_value
    )
    attended = (
        (numer_all / total[..., None]).reshape(row_count, heads_dev * HD).astype(jnp.bfloat16)
    )
    projected = jnp.dot(attended, w_out, preferred_element_type=jnp.float32)
    attn_rows = lax.psum_scatter(
        projected.astype(jnp.bfloat16), "kv", scatter_dimension=0, tiled=True
    ).astype(jnp.float32)
    token_count = attn_rows.shape[0]
    rows_home = lax.dynamic_slice_in_dim(hidden_in, kv_index * token_count, token_count, 0)
    after_attn = rows_home.astype(jnp.float32) + attn_rows
    moe_in = rms_norm(after_attn, moe_gain).astype(jnp.bfloat16)
    logits = jnp.dot(moe_in, w_router, preferred_element_type=jnp.float32)
    gate_probs = jax.nn.softmax(jnp.take_along_axis(logits, routes, 1), -1)
    expert_count = w_router.shape[1]
    onehot = (
        routes[:, :, None] == jnp.arange(expert_count, dtype=jnp.int32)[None, None, :]
    ).astype(jnp.float32)
    combine_weight = jnp.sum(gate_probs[:, :, None] * onehot, 1)
    sources = lax.axis_size("req")
    local_experts = w_gate_up.shape[0]
    chosen_mask = jnp.sum(onehot, 1)
    outgoing = (chosen_mask.T[:, :, None] * moe_in[None, :, :].astype(jnp.float32)).astype(
        jnp.bfloat16
    )
    arrived = lax.all_to_all(outgoing, "req", split_axis=0, concat_axis=0, tiled=True)
    count = arrived.shape[1]
    grouped = arrived.reshape(sources, local_experts, count, arrived.shape[2])
    gate_up = jnp.einsum("sexd,edf->sexf", grouped, w_gate_up, preferred_element_type=jnp.float32)
    activated = (jax.nn.silu(gate_up[..., :FFE]) * gate_up[..., FFE:]).astype(jnp.bfloat16)
    produced = jnp.einsum(
        "sexf,efd->sexd", activated, w_down, preferred_element_type=jnp.float32
    ).astype(jnp.bfloat16)
    produced = produced.reshape(sources * local_experts, count, produced.shape[3])
    returned = lax.all_to_all(produced, "req", split_axis=0, concat_axis=0, tiled=True)
    mixture = jnp.einsum(
        "te,etd->td", combine_weight, returned.astype(jnp.float32), precision=lax.Precision.HIGHEST
    )
    return (after_attn + mixture).astype(jnp.bfloat16)


def solution(mesh):
    placed = (
        P("req", None),
        P(),
        P("kv", None),
        P("kv", None),
        P("kv", None),
        P("kv", None),
        P("req", "kv", None),
        P("req", "kv", None),
        P(),
        P("req"),
        P(),
        P(),
        P("req", None, None),
        P("req", None, None),
        P(("req", "kv"), None),
    )
    return jax.shard_map(
        shards, mesh=mesh, in_specs=placed, out_specs=P(("req", "kv"), None), check_vma=False
    )
```

profile of v0, /device:TPU:0, one launch (start us, length us, event | category | flops | bytes accessed | tf_op | source)
XLA Modules:
  0.0 607.8 jit_solution(15673589883562390273)
XLA Ops:
  11.6 36.0 %all_gather.21 = bf16[1024,384]{1,0:T(8,128)(2,1)} all-gather(bf16[128,384]{1,0:T(8,128)(2,1)S(1)} %copy.105), channel_id=1, replica_groups=mesh['req'=8,'kv'=4] {'req'}, dimensions={0}, use_global_device_ids=true | all-gather | bytes 884736 | tf_op jit(solution)/shard_map/all_gather | solution.py:77
  50.1 3.2 gather_fusion.1
  56.4 31.3 %copy.107 = bf16[384,2,8192]{0,2,1:T(8,128)(2,1)} copy(bf16[384,2,8192]{2,1,0:T(2,128)(2,1)} %param.23) | data formatting | bytes 25165824 | tf_op args[6]
  87.6 18.0 %copy.109 = bf16[384,2,128,64]{2,3,1,0:T(8,128)(2,1)} copy(bf16[384,2,128,64]{0,3,2,1:T(8,128)(2,1)} %bitcast.114) | data formatting | bytes 25165824 | tf_op jit(solution)/shard_map/reshape | solution.py:81
  105.8 9.7 %fusion.58 = (f32[384,2,3]{2,1,0:T(2,128)S(1)}, f32[384,2,3,128]{3,2,1,0:T(4,128)}) fusion(bf16[384,2,3,64]{3,2,1,0:T(4,128)(2,1)} %copy.108, bf16[384,2,128,64]{2,3,1,0:T(8,128)(2,1)} %copy.109, pred[384,128]{1,0:T(8,128)(4,1)S(1)} %add_compare_fusion), kind=kOutput, calls=%fused_computation.104 | convolution fusion | flops 38336256 | bytes 14115840 | tf_op jit(solution)/shard_map/bgqd,bgtd->bgqt/dot_general | solution.py:83
  124.3 31.3 %copy.115 = bf16[384,2,8192]{0,2,1:T(8,128)(2,1)} copy(bf16[384,2,8192]{2,1,0:T(2,128)(2,1)} %param.24) | data formatting | bytes 25165824 | tf_op args[7]
  155.5 18.0 %copy.116 = bf16[384,2,128,64]{2,3,1,0:T(8,128)(2,1)} copy(bf16[384,2,128,64]{0,3,2,1:T(8,128)(2,1)} %bitcast.115) | data formatting | bytes 25165824 | tf_op jit(solution)/shard_map/reshape | solution.py:82
  173.6 23.2 %fusion.20 = f32[384,2,3,64]{3,2,1,0:T(4,128)} fusion(bf16[384,2,128,64]{2,3,1,0:T(8,128)(2,1)} %copy.116, f32[384,2,3,128]{3,2,1,0:T(4,128)} %get-tuple-element.117, f32[384,2,3]{2,1,0:T(2,128)S(1)} %reshape.299, pred[384,128]{1,0:T(8,128)(4,1)} %copy-done.7), kind=kOutput, calls=%fused_computation.33 | convolution fusion | flops 227082240 | bytes 14410752 | tf_op jit(solution)/shard_map/bgqt,bgtd->bgqd/dot_general | solution.py:110
  199.0 3.9 fusion.22
  203.0 3.9 fusion.21
  211.6 31.9 %all-gather.1 = f32[8192,6]{0,1:T(8,128)S(1)} all-gather(f32[1024,6]{0,1:T(8,128)S(1)} %fusion.23), channel_id=3, replica_groups=mesh['req'=8,'kv'=4] {'req'}, dimensions={0}, use_global_device_ids=true | all-gather | bytes 221184 | tf_op jit(solution)/shard_map/all_gather | solution.py:13
  244.8 31.9 %all-gather = f32[8192,6]{0,1:T(8,128)S(1)} all-gather(f32[1024,6]{0,1:T(8,128)} %copy-done.8), channel_id=2, replica_groups=mesh['req'=8,'kv'=4] {'req'}, dimensions={0}, use_global_device_ids=true | all-gather | bytes 221184 | tf_op jit(solution)/shard_map/all_gather | solution.py:13
  283.2 100.9 %all-gather.5.cloned.1.call-done = f32[8192,384]{1,0:T(8,128)} async-done(((f32[1024,384]{1,0:T(8,128)}), f32[8192,384]{1,0:T(8,128)}) %all-gather.5.cloned.1.call-update) | async-done | bytes 12582928 | tf_op jit(solution)/shard_map/all_gather | solution.py:13
  389.9 8.9 %slice.69 = f32[7168,384]{1,0:T(8,128)} slice(f32[8192,384]{1,0:T(8,128)} %all-gather.5.cloned.1.call-done), slice={[1024:8192], [0:384]} | slice | bytes 22020096 | tf_op jit(solution)/shard_map/slice | solution.py:15
  398.7 74.3 %while.14 = (s32[]{:T(128)}, f32[1024,6]{0,1:T(8,128)}, f32[1024,6]{0,1:T(8,128)}, f32[1024,384]{0,1:T(8,128)}, f32[7,1024,6]{1,2,0:T(8,128)}, /*index=5*/f32[7,1024,6]{1,2,0:T(8,128)}, f32[7,1024,384]{2,1,0:T(8,128)}, s32[]{:T(128)}) while((s32[]{:T(128)}, f32[1024,6]{0,1:T(8,128)}, f32[1024,6]{0,1:T(8,128)}, f32[1024,384]{0,1:T(8,128)}, ...), condition=%wide.region_5.6_spmd, body=%wide.region_4.5_spmd.sunk | while | flops 1216514 | bytes 11255901 | solution.py:16
  402.8 3.0 copy.146
  405.9 3.5 fusion.76
  413.4 3.0 copy.146
  416.5 3.5 fusion.76
  424.1 3.0 copy.146
  427.1 3.5 fusion.76
  434.7 3.0 copy.146
  437.7 3.5 fusion.76
  445.3 3.0 copy.146
  448.3 3.5 fusion.76
  458.9 3.5 fusion.76
  469.5 3.5 fusion.76
  478.7 17.7 %reduce-scatter.2.cloned.1.call-done = bf16[32,1536]{1,0:T(8,128)(2,1)} async-done(((bf16[128,1536]{1,0:T(8,128)(2,1)}), bf16[32,1536]{1,0:T(8,128)(2,1)}) %reduce-scatter.2.cloned.1.call-update) | async-done | bytes 98320 | tf_op jit(solution)/shard_map/reduce_scatter | solution.py:142
  507.6 42.3 %all_to_all.10 = bf16[16,32,1536]{2,1,0:T(8,128)(2,1)S(1)} all-to-all(bf16[16,32,1536]{2,1,0:T(8,128)(2,1)S(1)} %multiply_convert_fusion), channel_id=1, replica_groups=mesh['req'=8,'kv'=4] {'req'}, dimensions={0} | all-to-all | bytes 3145728 | tf_op jit(solution)/shard_map/all_to_all | solution.py:162
  549.9 4.7 fusion.13
  556.9 4.3 all-to-all-start.1
  561.9 35.5 %all-to-all-done.1 = bf16[16,32,1536]{2,1,0:T(8,128)(2,1)} async-done(((bf16[16,32,1536]{2,1,0:T(8,128)(2,1)}), bf16[16,32,1536]{2,1,0:T(8,128)(2,1)}, u32[]{:S(2)}, u32[]{:S(2)}) %all-to-all-start.1) | async-done | bytes 1572896 | tf_op jit(solution)/shard_map/all_to_all | solution.py:171
  (110 shorter events, 98.0 us)
Async XLA Ops:
  6.5 548.0 %copy-start = (bf16[2,512,1536]{2,1,0:T(8,128)(2,1)S(1)}, bf16[2,512,1536]{2,1,0:T(8,128)(2,1)}, u32[]{:S(2)}) copy-start(bf16[2,512,1536]{2,1,0:T(8,128)(2,1)} %param.30) | copy-start | bytes 9437188
  6.5 377.6 %all-gather.5.cloned.1.call-start = ((), (), s32[]{:S(2)}) async-start(), calls=%async_computation.4 | async-start | bytes 14155776 | tf_op jit(solution)/shard_map/all_gather | solution.py:13
  7.9 39.7 %copy-start.13 = (f32[128]{0:T(128)}, f32[128]{0:T(128)S(1)}, u32[]{:S(2)}) copy-start(f32[128]{0:T(128)S(1)} %add_rsqrt_fusion.1) | copy-start | bytes 1540
  8.8 2.7 copy-start.9
  8.8 38.8 %copy-start.12 = (s32[384]{0:T(512)S(1)}, s32[384]{0:T(512)}, u32[]{:S(2)}) copy-start(s32[384]{0:T(512)} %param.26) | copy-start | bytes 4612
  8.8 39.4 %copy-start.1 = (s32[1024]{0:T(1024)S(1)}, s32[1024]{0:T(1024)}, u32[]{:S(2)}) copy-start(s32[1024]{0:T(1024)} %param.25) | copy-start | bytes 12292
  10.8 0.6 copy-start.4
  10.8 0.7 copy-start.5
  48.2 5.2 copy-start.11
  105.8 9.7 %copy-start.7 = (pred[384,128]{1,0:T(8,128)(4,1)}, pred[384,128]{1,0:T(8,128)(4,1)S(1)}, u32[]{:S(2)}) copy-start(pred[384,128]{1,0:T(8,128)(4,1)S(1)} %add_compare_fusion) | copy-start | bytes 147460
  119.3 1.0 copy-start.8
  203.0 293.4 %reduce-scatter.2.cloned.1.call-start = ((), (), s32[]{:S(2)}) async-start(), calls=%async_computation.3 | async-start | bytes 491520 | tf_op jit(solution)/shard_map/reduce_scatter | solution.py:142
  206.9 71.0 %copy-start.2 = (bf16[128,1536]{1,0:T(8,128)(2,1)S(1)}, bf16[128,1536]{1,0:T(8,128)(2,1)}, u32[]{:S(2)}) copy-start(bf16[128,1536]{1,0:T(8,128)(2,1)} %param.17) | copy-start | bytes 1179652
  473.0 4.2 copy-start.10
  473.0 23.3 %copy-start.3 = (bf16[128,1536]{1,0:T(8,128)(2,1)S(1)}, bf16[128,1536]{1,0:T(8,128)(2,1)}, u32[]{:S(2)}) copy-start(bf16[128,1536]{1,0:T(8,128)(2,1)} %param.17) | copy-start | bytes 1179652
  556.9 40.5 %all-to-all-start.1 = ((bf16[16,32,1536]{2,1,0:T(8,128)(2,1)}), bf16[16,32,1536]{2,1,0:T(8,128)(2,1)}, u32[]{:S(2)}, u32[]{:S(2)}) async-start(bf16[16,32,1536]{2,1,0:T(8,128)(2,1)} %bitcast.117), calls=%async_computation.2 | async-start | bytes 3145728 | tf_op jit(solution)/shard_map/all_to_all | solution.py:171
  597.4 2.9 copy-start.6
Sparse Core Ops, SparseCore 0:
  203.1 181.0 all-gather.4
  477.3 19.0 reduce-scatter.1
where the time goes:
time: 613 us; the launch traced here: 608 us
  local copies, waits for them, and re-layouts  183 us (30%)
  waiting for transfers between devices  154 us (25%)
  blocking collectives  142 us (23%)
  other arithmetic  55.3 us (9%)
  matrix products  55 us (9%)
  between operations  13.7 us (2%)
    all_gather x1, waiting for transfers between devices, merged_2(): pieces = jax.tree.map(lambda part: lax.all_gather(part, axis), value)  101 us
    all_gather x2, blocking collectives, merged_2(): pieces = jax.tree.map(lambda part: lax.all_gather(part, axis), value)  63.8 us
    unnamed x30, local copies, waits for them, and re-layouts  63.2 us
    all_to_all x1, blocking collectives, shards(): lax.all_to_all(outgoing, 'req', split_axis=0, concat_axis=0, tiled=True)  42.3 us
    dynamic_slice x14, local copies, waits for them, and re-layouts, merged_2(): lax.scan(lambda so_far, share: (join(so_far, share), None), head, tail)  39.8 us
    all_gather x1, blocking collectives, shards(): lax.all_gather(query.reshape(row_count, heads_dev * HD), 'req', axis=0, t...  36 us
    all_to_all x1, waiting for transfers between devices, shards(): lax.all_to_all(produced, 'req', split_axis=0, concat_axis=0, tiled=True)  35.5 us
    add x7, other arithmetic, blend_parts(): first_numer + second_numer  24.5 us
  transfers between devices with their start and end apart: 3, of which 3 were waited for; matrix products, arithmetic and copies ran while one was open for 3% of the time, Pallas kernels for 0%

commit v1 on v0

v1 whole, which is shorter than its diff:
```python
import functools

import jax
import jax.numpy as jnp
from jax import lax
from jax.experimental import pallas as pl
from jax.experimental.pallas import tpu as pltpu
from jax.sharding import PartitionSpec as P

HD = 64
FFE = 512
BLK = 128
PAGES = 3
NEG = -1e30
BF = jnp.bfloat16
F32 = jnp.float32


def iota(shape, dim):
    return lax.broadcasted_iota(jnp.int32, shape, dim)


def swap(value, axis, distance):
    size = lax.axis_size(axis)
    return lax.ppermute(value, axis, [(source, source ^ distance) for source in range(size)])


def rms_norm(values, gain):
    values = values.astype(F32)
    return values * lax.rsqrt(jnp.mean(values * values, -1, keepdims=True) + 1e-05) * gain


def rotate(values, positions):
    half_dim = values.shape[-1] // 2
    frequency = 10000.0 ** (-jnp.arange(half_dim, dtype=F32) / half_dim)
    angles = positions.astype(F32)[:, None, None] * frequency
    cosines = jnp.cos(angles)
    sines = jnp.sin(angles)
    first_half = values[..., :half_dim]
    second_half = values[..., half_dim:]
    return jnp.concatenate(
        [first_half * cosines - second_half * sines, first_half * sines + second_half * cosines], -1
    )


def project_rows(normed, weight):
    return lax.dot_general(normed, weight, (((1,), (1,)), ((), ())), preferred_element_type=F32)


def dot(left, right):
    return jnp.dot(left, right, preferred_element_type=F32)


def attend_kernel(heads, groups, chunk, qrow_ref, left_ref, slot_ref, local_ref, query_ref,
                  key_ref, value_ref, out_ref, rows_ref):
    blocks = key_ref.shape[0]
    lanes = key_ref.shape[1]
    width = out_ref.shape[1]
    per_group = heads // groups
    feature = heads * HD

    row = iota((chunk * 16, 1), 0)
    parity = (row // 8) % 2
    head = row % 8
    keep_head = iota((chunk * 16, feature), 1) // HD == head
    keep_half = iota((chunk * 16, 2 * HD), 1) // HD == parity
    fold = (iota((feature, 2 * HD), 0) % HD == iota((feature, 2 * HD), 1) % HD).astype(BF)
    spread = (iota((chunk * 16, chunk), 0) // 16 == iota((chunk * 16, chunk), 1)).astype(BF)
    gather = (iota((chunk, chunk * 8), 1) // 8 == iota((chunk, chunk * 8), 0)).astype(BF)
    cell_row = iota((16, lanes), 0)
    cell_lane = iota((16, lanes), 1)
    position = jnp.where(
        cell_lane % groups == (cell_row % 8) // per_group,
        2 * (cell_lane // groups) + cell_row // 8,
        1 << 20,
    )[None]
    out_head = iota((chunk * 8, 1), 0) % 8
    out_lane = iota((chunk * 8, width), 1)
    own_lanes = out_lane // HD == out_head
    extra = out_lane - feature
    part_at = [jnp.logical_and(extra == out_head * 4 + part, out_head < heads) for part in range(3)]

    def step(index, carry):
        base = pl.multiple_of(index * chunk, chunk)
        rows = pl.ds(base, chunk)
        picked = (iota((chunk, query_ref.shape[0]), 1) == qrow_ref[rows, :]).astype(BF)
        query = dot(picked, query_ref[...]).astype(BF)
        query = jnp.where(keep_head, dot(spread, query), 0.0).astype(BF)
        query = jnp.where(keep_half, dot(query, fold), 0.0).astype(BF).reshape(chunk, 16, 2 * HD)
        scores = lax.dot_general(
            query, key_ref[rows], (((2,), (2,)), ((0,), (0,))), preferred_element_type=F32
        )
        usable = position < left_ref[rows]
        scores = jnp.where(usable, scores, NEG)
        highest = jnp.max(scores, -1, keepdims=True)
        highest = jnp.maximum(highest[:, :8], highest[:, 8:])
        weights = jnp.where(usable, jnp.exp(scores - jnp.concatenate([highest, highest], 1)), 0.0)
        total = jnp.sum(weights, -1, keepdims=True)
        total = total[:, :8] + total[:, 8:]
        numer = lax.dot_general(
            weights.astype(BF), value_ref[rows], (((2,), (1,)), ((0,), (0,))), preferred_element_type=F32
        )
        numer = jnp.where(iota((1, 8, 2 * HD), 2) < HD, numer[:, :8], numer[:, 8:])
        numer = numer.reshape(chunk * 8, 2 * HD)
        numer = numer + pltpu.roll(numer, HD, 1)
        total = total.reshape(chunk * 8, 1)
        highest = highest.reshape(chunk * 8, 1)
        some = total > 0.0
        safe = jnp.where(some, total, 1.0)
        mean = numer / safe
        level = jnp.where(some, highest + jnp.log(safe), NEG)
        first = level.astype(BF).astype(F32)
        second = (level - first).astype(BF).astype(F32)
        third = level - first - second
        wide = jnp.concatenate([mean] * (width // (2 * HD)), 1)
        wide = jnp.where(own_lanes, wide, 0.0)
        for here, part in zip(part_at, (first, second, third)):
            wide = jnp.where(here, part, wide)
        packed = dot(gather, wide.astype(BF))
        lane = iota((chunk, width), 1)
        packed = jnp.where(lane == feature + HD - 1, local_ref[rows, :].astype(F32), packed)
        rows_ref[rows, :] = packed.astype(BF)
        return carry

    lax.fori_loop(0, blocks // chunk, step, 0)
    order = (slot_ref[...] == iota((blocks, blocks), 0)).astype(BF)
    out_ref[...] = dot(order, rows_ref[...]).astype(BF)


def merge_kernel(heads, groups, part_ref, query_ref, key_ref, value_ref, weight_ref, out_ref):
    rows = query_ref.shape[0]
    blocks, width = part_ref.shape
    per_group = heads // groups
    feature = heads * HD
    row = iota((32, width), 0)
    column = iota((32, width), 1) - feature
    wanted = jnp.where(row < 24, (row % 8) * 4 + row // 8, HD - 1)
    pick = jnp.logical_and(column == wanted, jnp.logical_or(row == 24, row % 8 < heads))
    pick = jnp.logical_and(pick, row <= 24).astype(BF)
    parts = part_ref[...]
    extras = lax.dot_general(pick, parts, (((1,), (1,)), ((), ())), preferred_element_type=F32)
    levels = extras[0:8] + extras[8:16] + extras[16:24]
    local = extras[24:25].astype(jnp.int32)
    member = local == iota((rows, blocks), 0)

    source = iota((groups * HD, width), 0)
    target = iota((groups * HD, width), 1)
    same = jnp.logical_and(source // HD == target // (HD * per_group), source % HD == target % HD)
    widen = same.astype(BF)
    key = dot(key_ref[...], widen)
    value = dot(value_ref[...], widen)
    products = query_ref[...].astype(F32) * key[:, :feature]
    lane_head = iota((rows, width), 1) // HD
    joined = jnp.zeros((rows, width), F32)
    for head in range(heads):
        own = jnp.sum(jnp.where(lane_head[:, :feature] == head, products, 0.0), -1, keepdims=True)
        level = levels[head : head + 1]
        highest = jnp.max(jnp.where(member, level, NEG), -1, keepdims=True)
        highest = jnp.maximum(highest, own)
        weights = jnp.where(member, jnp.exp(level - highest), 0.0).astype(BF)
        own_weight = jnp.exp(own - highest)
        total = jnp.sum(weights.astype(F32), -1, keepdims=True) + own_weight
        numer = dot(weights, parts) + own_weight * value
        joined = jnp.where(lane_head == head, numer / total, joined)
    attended = joined[:, :feature].astype(BF)
    out_ref[...] = dot(attended, weight_ref[...]).astype(BF)


def shards(
    hidden_in,
    attn_gain,
    w_query,
    w_key,
    w_value,
    w_out,
    k_cache,
    v_cache,
    cache_len,
    block_slot,
    moe_gain,
    w_router,
    w_gate_up,
    w_down,
    routes,
):
    req_index = lax.axis_index("req")
    kv_index = lax.axis_index("kv")
    sources = lax.axis_size("req")
    kv_size = lax.axis_size("kv")
    row_count, model = hidden_in.shape
    heads = w_query.shape[0] // HD
    groups = w_key.shape[0] // HD
    blocks = k_cache.shape[0]
    requests = cache_len.shape[0]
    share = blocks // sources
    width = -(-(heads * HD + HD) // 128) * 128

    lengths_home = lax.dynamic_slice_in_dim(cache_len, req_index * row_count, row_count, 0)
    normed = rms_norm(hidden_in, attn_gain).astype(BF)
    query = project_rows(normed, w_query).reshape(row_count, heads, HD)
    query = (rotate(query, lengths_home) * 0.125).astype(BF).reshape(row_count, heads * HD)
    key_new = project_rows(normed, w_key).reshape(row_count, groups, HD)
    key_new = rotate(key_new, lengths_home).astype(BF).reshape(row_count, groups * HD)
    value_new = project_rows(normed, w_value).astype(BF)
    queries = jnp.concatenate(
        [query] + [swap(query, "req", distance) for distance in range(1, sources)], 0
    )

    owners = block_slot // PAGES
    home = owners // row_count
    local = owners % row_count
    owned = owners[:, None] == jnp.arange(requests, dtype=jnp.int32)[None, :]
    lengths = jnp.sum(jnp.where(owned, cache_len[None, :], 0), 1)
    left = lengths - (block_slot % PAGES) * BLK
    left = jnp.broadcast_to(left[:, None, None], (blocks, 1, groups * HD))
    number = jnp.arange(blocks, dtype=jnp.int32)
    earlier = jnp.logical_and(home[:, None] == home[None, :], number[:, None] < number[None, :])
    rank = jnp.sum(earlier.astype(jnp.int32), 0)
    slot = home * share + rank
    query_row = jnp.bitwise_xor(home, req_index) * row_count + local

    def pairs(cache):
        cache = cache.reshape(blocks, groups, HD, 2 * HD).transpose(0, 2, 1, 3)
        return cache.reshape(blocks, HD * groups, 2 * HD)

    chunk = 48
    vmem = pl.BlockSpec(memory_space=pltpu.VMEM)
    partial = pl.pallas_call(
        functools.partial(attend_kernel, heads, groups, chunk),
        out_shape=jax.ShapeDtypeStruct((blocks, width), BF),
        in_specs=[vmem] * 7,
        out_specs=vmem,
        scratch_shapes=[pltpu.VMEM((blocks, width), BF)],
        compiler_params=pltpu.CompilerParams(vmem_limit_bytes=48 << 20),
        name="attend",
    )(
        query_row[:, None],
        left,
        slot[None, :],
        local[:, None],
        queries,
        pairs(k_cache),
        pairs(v_cache),
    )
    parts = lax.all_to_all(partial, "req", split_axis=0, concat_axis=0, tiled=True)
    projected = pl.pallas_call(
        functools.partial(merge_kernel, heads, groups),
        out_shape=jax.ShapeDtypeStruct((row_count, model), BF),
        in_specs=[vmem] * 5,
        out_specs=vmem,
        compiler_params=pltpu.CompilerParams(vmem_limit_bytes=32 << 20),
        name="merge",
    )(parts, query, key_new, value_new, w_out)

    token_count = row_count // kv_size
    attn_rows = jnp.zeros((token_count, model), F32)
    for distance in range(kv_size):
        start = jnp.bitwise_xor(kv_index, distance) * token_count
        piece = lax.dynamic_slice_in_dim(projected, start, token_count, 0)
        if distance:
            piece = swap(piece, "kv", distance)
        attn_rows = attn_rows + piece.astype(F32)
    rows_home = lax.dynamic_slice_in_dim(hidden_in, kv_index * token_count, token_count, 0)
    after_attn = rows_home.astype(F32) + attn_rows
    moe_in = rms_norm(after_attn, moe_gain).astype(BF)
    logits = dot(moe_in, w_router)
    experts = w_router.shape[1]
    named = routes[:, :, None] == jnp.arange(experts, dtype=jnp.int32)[None, None, :]
    chosen = jnp.any(named, 1)
    gates = jax.nn.softmax(jnp.where(chosen, logits, -jnp.inf), -1)
    gates_high = gates.astype(BF)
    gates_low = (gates - gates_high.astype(F32)).astype(BF)
    outgoing = jnp.concatenate(
        [moe_in, gates_high, gates_low, jnp.zeros((token_count, 128 - 2 * experts), BF)], 1
    )
    arrived = jnp.concatenate(
        [outgoing] + [swap(outgoing, "req", distance) for distance in range(1, sources)], 0
    )
    tokens = arrived[:, :model]
    local_experts = w_gate_up.shape[0]
    first = model + req_index * local_experts
    high = lax.dynamic_slice_in_dim(arrived, first, local_experts, 1).astype(F32)
    low = lax.dynamic_slice_in_dim(arrived, first + experts, local_experts, 1).astype(F32)
    gate_here = high + low
    gate_up = jnp.einsum("td,edf->etf", tokens, w_gate_up, preferred_element_type=F32)
    activated = (jax.nn.silu(gate_up[..., :FFE]) * gate_up[..., FFE:]).astype(BF)
    produced = jnp.einsum("etf,efd->etd", activated, w_down, preferred_element_type=F32)
    produced = produced.astype(BF).astype(F32)
    mixed = jnp.sum(produced * gate_here.T[:, :, None], 0).astype(BF)
    mixture = mixed[:token_count].astype(F32)
    for distance in range(1, sources):
        piece = mixed[distance * token_count : (distance + 1) * token_count]
        mixture = mixture + swap(piece, "req", distance).astype(F32)
    return (after_attn + mixture).astype(BF)


def solution(mesh):
    placed = (
        P("req", None),
        P(),
        P("kv", None),
        P("kv", None),
        P("kv", None),
        P("kv", None),
        P("req", "kv", None),
        P("req", "kv", None),
        P(),
        P("req"),
        P(),
        P(),
        P("req", None, None),
        P("req", None, None),
        P(("req", "kv"), None),
    )
    return jax.shard_map(
        shards, mesh=mesh, in_specs=placed, out_specs=P(("req", "kv"), None), check_vma=False
    )
```

time: 613 us -> 147 us (0.24)
  local copies, waits for them, and re-layouts: 183 us -> 11 us
  blocking collectives: 142 us -> 0 us
  waiting for transfers between devices: 154 us -> 37.1 us
  other arithmetic: 55.3 us -> 9.28 us
  starting transfers between devices: 4.33 us -> 47 us
  matrix products: 55 us -> 13.1 us
  Pallas kernels: 0 us -> 28.5 us
  between operations: 13.7 us -> 0.39 us
    all_gather x1 -> x0, waiting for transfers between devices: 101 us -> none  [merged_2(): pieces = jax.tree.map(lambda part: lax.all_gather(part, axis), value)]
    all_gather x3 -> x0, blocking collectives: 99.7 us -> none  [the longest x2 63.8 us: merged_2(): pieces = jax.tree.map(lambda part: lax.all_gather(part, axis), value)]
    unnamed x30 -> x40, local copies, waits for them, and re-layouts: 63.2 us -> 6.3 us
    dot_general x9 -> x3, matrix products: 50.2 us -> 7 us  [the longest x1 4.84 us: shards(): jnp.einsum('td,edf->etf', tokens, w_gate_up, preferred_element_type=F32)]
    all_to_all x1 -> x0, blocking collectives: 42.3 us -> none  [shards(): lax.all_to_all(outgoing, 'req', split_axis=0, concat_axis=0, tiled=True)]
    reshape x5 -> x0, local copies, waits for them, and re-layouts: 39.5 us -> none  [the longest x1 18 us: shards(): cache_keys = k_cache.reshape(block_count, kv_dev, BLK, HD)]
    ppermute x0 -> x24, starting transfers between devices: none -> 39.3 us  [swap(): lax.ppermute(value, axis, [(source, source ^ distance) for source in rang...]
    dynamic_slice x14 -> x1, local copies, waits for them, and re-layouts: 39.8 us -> 0.66 us  [shards(): piece = lax.dynamic_slice_in_dim(projected, start, token_count, 0)]
  transfers between devices with their start and end apart: 3 -> 25, of which waited for: 3 -> 13; matrix products, arithmetic and copies ran while one was open for 3% -> 7% of each run, Pallas kernels for 0% -> 0%
where the time goes in v1:
time: 147 us; the launch traced here: 146 us
  starting transfers between devices  47 us (32%)
  waiting for transfers between devices  37.1 us (25%)
  Pallas kernels  28.5 us (19%)
  matrix products  13.1 us (9%)
  local copies, waits for them, and re-layouts  11 us (7%)
  other arithmetic  9.28 us (6%)
    ppermute x24, starting transfers between devices, swap(): lax.ppermute(value, axis, [(source, source ^ distance) for source in rang...  39.3 us
    ppermute x24, waiting for transfers between devices, swap(): lax.ppermute(value, axis, [(source, source ^ distance) for source in rang...  34.9 us
    pallas_call x1, Pallas kernels, shards(): pl.pallas_call(functools.partial(attend_kernel, heads, groups, chunk), ou...  27.1 us
    all_to_all x1, starting transfers between devices, shards(): lax.all_to_all(partial, 'req', split_axis=0, concat_axis=0, tiled=True)  7.68 us
    unnamed x40, local copies, waits for them, and re-layouts  6.3 us
    dot_general x3, matrix products, project_rows(): lax.dot_general(normed, weight, (((1,), (1,)), ((), ())), preferred_eleme...  6.1 us
    dot_general x1, matrix products, shards(): jnp.einsum('td,edf->etf', tokens, w_gate_up, preferred_element_type=F32)  4.84 us
  transfers between devices with their start and end apart: 25, of which 13 were waited for; matrix products, arithmetic and copies ran while one was open for 7% of the time, Pallas kernels for 0%

profile of v1, /device:TPU:0, one launch (start us, length us, event | category | flops | bytes accessed | tf_op | source)
XLA Modules:
  0.0 146.3 jit_solution(16449222669331252167)
XLA Ops:
  0.0 1.3 fusion.1
  2.3 1.9 %fusion.20 = f32[128,384]{0,1:T(8,128)S(1)} fusion(bf16[384,1536]{1,0:T(8,128)(2,1)} %param.17, bf16[128,1536]{1,0:T(8,128)(2,1)} %param.15, f32[1536]{0:T(1024)} %param.16, f32[128]{0:T(128)S(1)} %add_rsqrt_fusion.1), kind=kOutput, calls=%fused_computation.82 | convolution fusion | flops 151781376 | bytes 1776128 | tf_op jit(solution)/shard_map/dot_general | solution.py:47
  4.4 6.0 %collective-permute-start.6 = (bf16[128,384]{1,0:T(8,128)(2,1)S(1)}, bf16[128,384]{1,0:T(8,128)(2,1)S(1)}, u32[]{:S(2)}, u32[]{:S(2)}) collective-permute-start(bf16[128,384]{1,0:T(8,128)(2,1)S(1)} %copy.49.query_ref), channel_id=1, source_target_pairs={{0,28},{4,24},{8,20},{12,16},{16,12},{20,8},{24,4},{28,0},{1,29},{... | collective-permute-start | bytes 294920 | tf_op jit(solution)/shard_map/ppermute | solution.py:25
  11.5 2.0 %collective-permute-start.3 = (bf16[128,384]{1,0:T(8,128)(2,1)S(1)}, bf16[128,384]{1,0:T(8,128)(2,1)S(1)}, u32[]{:S(2)}, u32[]{:S(2)}) collective-permute-start(bf16[128,384]{1,0:T(8,128)(2,1)S(1)} %copy.49.query_ref), channel_id=1, source_target_pairs={{0,16},{4,20},{8,24},{12,28},{16,0},{20,4},{24,8},{28,12},{1,17},{... | collective-permute-start | bytes 294920 | tf_op jit(solution)/shard_map/ppermute | solution.py:25
  13.5 1.6 %collective-permute-start = (bf16[128,384]{1,0:T(8,128)(2,1)S(1)}, bf16[128,384]{1,0:T(8,128)(2,1)S(1)}, u32[]{:S(2)}, u32[]{:S(2)}) collective-permute-start(bf16[128,384]{1,0:T(8,128)(2,1)S(1)} %copy.49.query_ref), channel_id=1, source_target_pairs={{0,4},{4,0},{8,12},{12,8},{16,20},{20,16},{24,28},{28,24},{1,5},{5... | collective-permute-start | bytes 294920 | tf_op jit(solution)/shard_map/ppermute | solution.py:25
  18.1 2.3 %collective-permute-start.1 = (bf16[128,384]{1,0:T(8,128)(2,1)S(1)}, bf16[128,384]{1,0:T(8,128)(2,1)S(1)}, u32[]{:S(2)}, u32[]{:S(2)}) collective-permute-start(bf16[128,384]{1,0:T(8,128)(2,1)S(1)} %copy.49.query_ref), channel_id=1, source_target_pairs={{0,8},{4,12},{8,0},{12,4},{16,24},{20,28},{24,16},{28,20},{1,9},{5... | collective-permute-start | bytes 294920 | tf_op jit(solution)/shard_map/ppermute | solution.py:25
  20.4 3.5 %collective-permute-done.1 = bf16[128,384]{1,0:T(8,128)(2,1)S(1)} collective-permute-done((bf16[128,384]{1,0:T(8,128)(2,1)S(1)}, bf16[128,384]{1,0:T(8,128)(2,1)S(1)}, u32[]{:S(2)}, u32[]{:S(2)}) %collective-permute-start.1) | collective-permute-done | bytes 98336 | tf_op jit(solution)/shard_map/ppermute | solution.py:25
  23.9 4.0 %collective-permute-start.2 = (bf16[128,384]{1,0:T(8,128)(2,1)S(1)}, bf16[128,384]{1,0:T(8,128)(2,1)S(1)}, u32[]{:S(2)}, u32[]{:S(2)}) collective-permute-start(bf16[128,384]{1,0:T(8,128)(2,1)S(1)} %copy.49.query_ref), channel_id=1, source_target_pairs={{0,12},{4,8},{8,4},{12,0},{16,28},{20,24},{24,20},{28,16},{1,13},{... | collective-permute-start | bytes 294920 | tf_op jit(solution)/shard_map/ppermute | solution.py:25
  27.9 2.6 %collective-permute-done.2 = bf16[128,384]{1,0:T(8,128)(2,1)S(1)} collective-permute-done((bf16[128,384]{1,0:T(8,128)(2,1)S(1)}, bf16[128,384]{1,0:T(8,128)(2,1)S(1)}, u32[]{:S(2)}, u32[]{:S(2)}) %collective-permute-start.2) | collective-permute-done | bytes 98336 | tf_op jit(solution)/shard_map/ppermute | solution.py:25
  31.8 27.1 %attend.1 = bf16[384,512]{1,0:T(8,128)(2,1)S(1)} custom-call(s32[384,1]{1,0:T(8,128)S(1)} %broadcast_in_dim.33.qrow_ref, s32[384,1,128]{2,1,0:T(1,128)S(1)} %broadcast_in_dim.28.left_ref, s32[1,384]{1,0:T(1,128)S(1)} %broadcast_in_dim.29.slot_ref, s32[384,1]{1,0:T(8,128)S(1)} %broadcast_in_dim.35.local_ref, ...), custom_call_target="tpu_custom_call" | custom-call | tf_op jit(solution)/shard_map/attend/pallas_call | solution.py:228
  59.7 7.7 %all-to-all-start = ((bf16[8,48,512]{2,1,0:T(8,128)(2,1)}), bf16[8,48,512]{2,1,0:T(8,128)(2,1)S(1)}, u32[]{:S(2)}, u32[]{:S(2)}) async-start(bf16[8,48,512]{2,1,0:T(8,128)(2,1)} %bitcast.31), calls=%async_computation | async-start | bytes 786432 | tf_op jit(solution)/shard_map/all_to_all | solution.py:245
  67.4 2.1 %fusion.18 = f32[128,128]{0,1:T(8,128)} fusion(bf16[128,1536]{1,0:T(8,128)(2,1)} %param.18, bf16[128,1536]{1,0:T(8,128)(2,1)} %param.15, f32[1536]{0:T(1024)} %param.16, f32[128]{0:T(128)} %copy-done.12), kind=kOutput, calls=%fused_computation.81 | convolution fusion | flops 51118080 | bytes 858624 | tf_op jit(solution)/shard_map/dot_general | solution.py:47
  70.9 1.5 copy.55.key_ref
  72.3 2.1 %convolution_convert_fusion.1.value_ref = bf16[128,128]{1,0:T(8,128)(2,1)} fusion(bf16[128,1536]{1,0:T(8,128)(2,1)} %param.19, bf16[128,1536]{1,0:T(8,128)(2,1)} %param.15, f32[1536]{0:T(1024)} %param.16, f32[128]{0:T(128)} %copy-done.12), kind=kOutput, calls=%fused_computation.5 | convolution fusion | flops 51134464 | bytes 825856 | tf_op jit(solution)/shard_map/dot_general | solution.py:47
  74.4 2.2 %all-to-all-done = bf16[8,48,512]{2,1,0:T(8,128)(2,1)S(1)} async-done(((bf16[8,48,512]{2,1,0:T(8,128)(2,1)}), bf16[8,48,512]{2,1,0:T(8,128)(2,1)S(1)}, u32[]{:S(2)}, u32[]{:S(2)}) %all-to-all-start) | async-done | bytes 393248 | tf_op jit(solution)/shard_map/all_to_all | solution.py:245
  80.2 1.4 merge.1
  83.0 1.6 %collective-permute-start.9 = (bf16[32,1536]{1,0:T(8,128)(2,1)S(1)}, bf16[32,1536]{1,0:T(8,128)(2,1)S(1)}, u32[]{:S(2)}, u32[]{:S(2)}) collective-permute-start(bf16[32,1536]{1,0:T(8,128)(2,1)S(1)} %get-tuple-element.19), channel_id=1, source_target_pairs={{0,3},{1,2},{2,1},{3,0},{4,7},{5,6},{6,5},{7,4},{8,11},{9,10},{10,... | collective-permute-start | bytes 294920 | tf_op jit(solution)/shard_map/ppermute | solution.py:25
  85.3 2.5 %collective-permute-done.9 = bf16[32,1536]{1,0:T(8,128)(2,1)S(1)} collective-permute-done((bf16[32,1536]{1,0:T(8,128)(2,1)S(1)}, bf16[32,1536]{1,0:T(8,128)(2,1)S(1)}, u32[]{:S(2)}, u32[]{:S(2)}) %collective-permute-start.9) | collective-permute-done | bytes 98336 | tf_op jit(solution)/shard_map/ppermute | solution.py:25
  87.8 2.5 %collective-permute-done.8 = bf16[32,1536]{1,0:T(8,128)(2,1)} collective-permute-done((bf16[32,1536]{1,0:T(8,128)(2,1)S(1)}, bf16[32,1536]{1,0:T(8,128)(2,1)}, u32[]{:S(2)}, u32[]{:S(2)}) %collective-permute-start.8) | collective-permute-done | bytes 98336 | tf_op jit(solution)/shard_map/ppermute | solution.py:25
  94.4 2.6 %collective-permute-start.16 = (bf16[32,1664]{1,0:T(8,128)(2,1)S(1)}, bf16[32,1664]{1,0:T(8,128)(2,1)S(1)}, u32[]{:S(2)}, u32[]{:S(2)}) collective-permute-start(bf16[32,1664]{1,0:T(8,128)(2,1)S(1)} %concatenate.19), channel_id=1, source_target_pairs={{0,28},{4,24},{8,20},{12,16},{16,12},{20,8},{24,4},{28,0},{1,29},{... | collective-permute-start | bytes 319496 | tf_op jit(solution)/shard_map/ppermute | solution.py:25
  97.0 1.8 %collective-permute-start.15 = (bf16[32,1664]{1,0:T(8,128)(2,1)S(1)}, bf16[32,1664]{1,0:T(8,128)(2,1)S(1)}, u32[]{:S(2)}, u32[]{:S(2)}) collective-permute-start(bf16[32,1664]{1,0:T(8,128)(2,1)S(1)} %concatenate.19), channel_id=1, source_target_pairs={{0,24},{4,28},{8,16},{12,20},{16,8},{20,12},{24,0},{28,4},{1,25},{... | collective-permute-start | bytes 319496 | tf_op jit(solution)/shard_map/ppermute | solution.py:25
  98.9 3.2 %collective-permute-start.13 = (bf16[32,1664]{1,0:T(8,128)(2,1)S(1)}, bf16[32,1664]{1,0:T(8,128)(2,1)S(1)}, u32[]{:S(2)}, u32[]{:S(2)}) collective-permute-start(bf16[32,1664]{1,0:T(8,128)(2,1)S(1)} %concatenate.19), channel_id=1, source_target_pairs={{0,16},{4,20},{8,24},{12,28},{16,0},{20,4},{24,8},{28,12},{1,17},{... | collective-permute-start | bytes 319496 | tf_op jit(solution)/shard_map/ppermute | solution.py:25
  103.3 3.6 %collective-permute-done.10 = bf16[32,1664]{1,0:T(8,128)(2,1)S(1)} collective-permute-done((bf16[32,1664]{1,0:T(8,128)(2,1)S(1)}, bf16[32,1664]{1,0:T(8,128)(2,1)S(1)}, u32[]{:S(2)}, u32[]{:S(2)}) %collective-permute-start.10) | collective-permute-done | bytes 106528 | tf_op jit(solution)/shard_map/ppermute | solution.py:25
  107.0 9.3 %collective-permute-done.11 = bf16[32,1664]{1,0:T(8,128)(2,1)S(1)} collective-permute-done((bf16[32,1664]{1,0:T(8,128)(2,1)S(1)}, bf16[32,1664]{1,0:T(8,128)(2,1)S(1)}, u32[]{:S(2)}, u32[]{:S(2)}) %collective-permute-start.11) | collective-permute-done | bytes 106528 | tf_op jit(solution)/shard_map/ppermute | solution.py:25
  116.3 5.6 %collective-permute-done.12 = bf16[32,1664]{1,0:T(8,128)(2,1)S(1)} collective-permute-done((bf16[32,1664]{1,0:T(8,128)(2,1)S(1)}, bf16[32,1664]{1,0:T(8,128)(2,1)S(1)}, u32[]{:S(2)}, u32[]{:S(2)}) %collective-permute-start.12) | collective-permute-done | bytes 106528 | tf_op jit(solution)/shard_map/ppermute | solution.py:25
  123.1 4.8 %convolution_bitcast_fusion = f32[2,256,1024]{2,1,0:T(8,128)S(1)} fusion(bf16[2,1536,1024]{2,1,0:T(8,128)(2,1)} %param.27, bf16[256,1664]{1,0:T(8,128)(2,1)} %copy-done.8), kind=kOutput, calls=%fused_computation.2 | convolution fusion | flops 1610612736 | bytes 9175040 | tf_op jit(solution)/shard_map/td,edf->etf/dot_general | solution.py:285
  130.1 2.2 %collective-permute-start.22 = (bf16[32,1536]{1,0:T(8,128)(2,1)S(1)}, bf16[32,1536]{1,0:T(8,128)(2,1)S(1)}, u32[]{:S(2)}, u32[]{:S(2)}) collective-permute-start(bf16[32,1536]{1,0:T(8,128)(2,1)S(1)} %get-tuple-element.12), channel_id=1, source_target_pairs={{0,24},{4,28},{8,16},{12,20},{16,8},{20,12},{24,0},{28,4},{1,25},{... | collective-permute-start | bytes 294920 | tf_op jit(solution)/shard_map/ppermute | solution.py:25
  132.3 3.0 %collective-permute-start.20 = (bf16[32,1536]{1,0:T(8,128)(2,1)S(1)}, bf16[32,1536]{1,0:T(8,128)(2,1)S(1)}, u32[]{:S(2)}, u32[]{:S(2)}) collective-permute-start(bf16[32,1536]{1,0:T(8,128)(2,1)S(1)} %get-tuple-element.14), channel_id=1, source_target_pairs={{0,16},{4,20},{8,24},{12,28},{16,0},{20,4},{24,8},{28,12},{1,17},{... | collective-permute-start | bytes 294920 | tf_op jit(solution)/shard_map/ppermute | solution.py:25
  135.4 2.8 %collective-permute-start.18 = (bf16[32,1536]{1,0:T(8,128)(2,1)S(1)}, bf16[32,1536]{1,0:T(8,128)(2,1)S(1)}, u32[]{:S(2)}, u32[]{:S(2)}) collective-permute-start(bf16[32,1536]{1,0:T(8,128)(2,1)S(1)} %get-tuple-element.16), channel_id=1, source_target_pairs={{0,8},{4,12},{8,0},{12,4},{16,24},{20,28},{24,16},{28,20},{1,9},{5... | collective-permute-start | bytes 294920 | tf_op jit(solution)/shard_map/ppermute | solution.py:25
  138.2 2.2 %collective-permute-start.23 = (bf16[32,1536]{1,0:T(8,128)(2,1)S(1)}, bf16[32,1536]{1,0:T(8,128)(2,1)S(1)}, u32[]{:S(2)}, u32[]{:S(2)}) collective-permute-start(bf16[32,1536]{1,0:T(8,128)(2,1)S(1)} %get-tuple-element.17), channel_id=1, source_target_pairs={{0,28},{4,24},{8,20},{12,16},{16,12},{20,8},{24,4},{28,0},{1,29},{... | collective-permute-start | bytes 294920 | tf_op jit(solution)/shard_map/ppermute | solution.py:25
  140.4 2.0 %collective-permute-done.21 = bf16[32,1536]{1,0:T(8,128)(2,1)S(1)} collective-permute-done((bf16[32,1536]{1,0:T(8,128)(2,1)S(1)}, bf16[32,1536]{1,0:T(8,128)(2,1)S(1)}, u32[]{:S(2)}, u32[]{:S(2)}) %collective-permute-start.21) | collective-permute-done | bytes 98336 | tf_op jit(solution)/shard_map/ppermute | solution.py:25
  143.1 1.8 %collective-permute-done.18 = bf16[32,1536]{1,0:T(8,128)(2,1)S(1)} collective-permute-done((bf16[32,1536]{1,0:T(8,128)(2,1)S(1)}, bf16[32,1536]{1,0:T(8,128)(2,1)S(1)}, u32[]{:S(2)}, u32[]{:S(2)}) %collective-permute-start.18) | collective-permute-done | bytes 98336 | tf_op jit(solution)/shard_map/ppermute | solution.py:25
  (103 shorter events, 25.2 us)
Async XLA Ops:
  0.0 128.0 %copy-start = (bf16[2,512,1536]{2,1,0:T(8,128)(2,1)S(1)}, bf16[2,512,1536]{2,1,0:T(8,128)(2,1)}, u32[]{:S(2)}) copy-start(bf16[2,512,1536]{2,1,0:T(8,128)(2,1)} %param.28) | copy-start | bytes 9437188
  1.3 2.9 %copy-start.12 = (f32[128]{0:T(128)}, f32[128]{0:T(128)S(1)}, u32[]{:S(2)}) copy-start(f32[128]{0:T(128)S(1)} %add_rsqrt_fusion.1) | copy-start | bytes 1540
  2.3 2.0 %copy-start.9 = (f32[128,32]{0,1:T(8,128)}, f32[128,32]{0,1:T(8,128)S(1)}, u32[]{:S(2)}) copy-start(f32[128,32]{0,1:T(8,128)S(1)} %get-tuple-element.28) | copy-start | bytes 49156
  4.4 54.5 %copy-start.4 = (bf16[128,384]{1,0:T(8,128)(2,1)}, bf16[128,384]{1,0:T(8,128)(2,1)S(1)}, u32[]{:S(2)}) copy-start(bf16[128,384]{1,0:T(8,128)(2,1)S(1)} %copy.49.query_ref) | copy-start | bytes 294916
  4.4 26.2 %collective-permute-start.6 = (bf16[128,384]{1,0:T(8,128)(2,1)S(1)}, bf16[128,384]{1,0:T(8,128)(2,1)S(1)}, u32[]{:S(2)}, u32[]{:S(2)}) collective-permute-start(bf16[128,384]{1,0:T(8,128)(2,1)S(1)} %copy.49.query_ref), channel_id=1, source_target_pairs={{0,28},{4,24},{8,20},{12,16},{16,12},{20,8},{24,4},{28,0},{1,29},{... | collective-permute-start | bytes 294920 | tf_op jit(solution)/shard_map/ppermute | solution.py:25
  10.5 20.1 %collective-permute-start.5 = (bf16[128,384]{1,0:T(8,128)(2,1)S(1)}, bf16[128,384]{1,0:T(8,128)(2,1)S(1)}, u32[]{:S(2)}, u32[]{:S(2)}) collective-permute-start(bf16[128,384]{1,0:T(8,128)(2,1)S(1)} %copy.49.query_ref), channel_id=1, source_target_pairs={{0,24},{4,28},{8,16},{12,20},{16,8},{20,12},{24,0},{28,4},{1,25},{... | collective-permute-start | bytes 294920 | tf_op jit(solution)/shard_map/ppermute | solution.py:25
  10.7 19.8 %collective-permute-start.4 = (bf16[128,384]{1,0:T(8,128)(2,1)S(1)}, bf16[128,384]{1,0:T(8,128)(2,1)S(1)}, u32[]{:S(2)}, u32[]{:S(2)}) collective-permute-start(bf16[128,384]{1,0:T(8,128)(2,1)S(1)} %copy.49.query_ref), channel_id=1, source_target_pairs={{0,20},{4,16},{8,28},{12,24},{16,4},{20,0},{24,12},{28,8},{1,21},{... | collective-permute-start | bytes 294920 | tf_op jit(solution)/shard_map/ppermute | solution.py:25
  11.5 19.0 %collective-permute-start.3 = (bf16[128,384]{1,0:T(8,128)(2,1)S(1)}, bf16[128,384]{1,0:T(8,128)(2,1)S(1)}, u32[]{:S(2)}, u32[]{:S(2)}) collective-permute-start(bf16[128,384]{1,0:T(8,128)(2,1)S(1)} %copy.49.query_ref), channel_id=1, source_target_pairs={{0,16},{4,20},{8,24},{12,28},{16,0},{20,4},{24,8},{28,12},{1,17},{... | collective-permute-start | bytes 294920 | tf_op jit(solution)/shard_map/ppermute | solution.py:25
  13.5 4.6 %collective-permute-start = (bf16[128,384]{1,0:T(8,128)(2,1)S(1)}, bf16[128,384]{1,0:T(8,128)(2,1)S(1)}, u32[]{:S(2)}, u32[]{:S(2)}) collective-permute-start(bf16[128,384]{1,0:T(8,128)(2,1)S(1)} %copy.49.query_ref), channel_id=1, source_target_pairs={{0,4},{4,0},{8,12},{12,8},{16,20},{20,16},{24,28},{28,24},{1,5},{5... | collective-permute-start | bytes 294920 | tf_op jit(solution)/shard_map/ppermute | solution.py:25
  18.1 5.8 %collective-permute-start.1 = (bf16[128,384]{1,0:T(8,128)(2,1)S(1)}, bf16[128,384]{1,0:T(8,128)(2,1)S(1)}, u32[]{:S(2)}, u32[]{:S(2)}) collective-permute-start(bf16[128,384]{1,0:T(8,128)(2,1)S(1)} %copy.49.query_ref), channel_id=1, source_target_pairs={{0,8},{4,12},{8,0},{12,4},{16,24},{20,28},{24,16},{28,20},{1,9},{5... | collective-permute-start | bytes 294920 | tf_op jit(solution)/shard_map/ppermute | solution.py:25
  23.9 6.6 %collective-permute-start.2 = (bf16[128,384]{1,0:T(8,128)(2,1)S(1)}, bf16[128,384]{1,0:T(8,128)(2,1)S(1)}, u32[]{:S(2)}, u32[]{:S(2)}) collective-permute-start(bf16[128,384]{1,0:T(8,128)(2,1)S(1)} %copy.49.query_ref), channel_id=1, source_target_pairs={{0,12},{4,8},{8,4},{12,0},{16,28},{20,24},{24,20},{28,16},{1,13},{... | collective-permute-start | bytes 294920 | tf_op jit(solution)/shard_map/ppermute | solution.py:25
  59.7 16.9 %all-to-all-start = ((bf16[8,48,512]{2,1,0:T(8,128)(2,1)}), bf16[8,48,512]{2,1,0:T(8,128)(2,1)S(1)}, u32[]{:S(2)}, u32[]{:S(2)}) async-start(bf16[8,48,512]{2,1,0:T(8,128)(2,1)} %bitcast.31), calls=%async_computation | async-start | bytes 786432 | tf_op jit(solution)/shard_map/all_to_all | solution.py:245
  70.2 14.9 %copy-start.11 = (s32[32,8]{0,1:T(8,128)S(1)}, s32[32,8]{0,1:T(8,128)}, u32[]{:S(2)}) copy-start(s32[32,8]{0,1:T(8,128)} %param.29) | copy-start | bytes 3076
  72.3 19.2 %copy-start.10 = (f32[1536]{0:T(1024)S(1)}, f32[1536]{0:T(1024)}, u32[]{:S(2)}) copy-start(f32[1536]{0:T(1024)} %param.25) | copy-start | bytes 18436
  76.6 1.3 copy-start.3
  83.0 2.3 %collective-permute-start.7 = (bf16[32,1536]{1,0:T(8,128)(2,1)}, bf16[32,1536]{1,0:T(8,128)(2,1)S(1)}, u32[]{:S(2)}, u32[]{:S(2)}) collective-permute-start(bf16[32,1536]{1,0:T(8,128)(2,1)} %get-tuple-element.18), channel_id=1, source_target_pairs={{0,1},{1,0},{2,3},{3,2},{4,5},{5,4},{6,7},{7,6},{8,9},{9,8},{10,11... | collective-permute-start | bytes 294920 | tf_op jit(solution)/shard_map/ppermute | solution.py:25
  83.0 4.8 %collective-permute-start.9 = (bf16[32,1536]{1,0:T(8,128)(2,1)S(1)}, bf16[32,1536]{1,0:T(8,128)(2,1)S(1)}, u32[]{:S(2)}, u32[]{:S(2)}) collective-permute-start(bf16[32,1536]{1,0:T(8,128)(2,1)S(1)} %get-tuple-element.19), channel_id=1, source_target_pairs={{0,3},{1,2},{2,1},{3,0},{4,7},{5,6},{6,5},{7,4},{8,11},{9,10},{10,... | collective-permute-start | bytes 294920 | tf_op jit(solution)/shard_map/ppermute | solution.py:25
  84.7 5.7 %collective-permute-start.8 = (bf16[32,1536]{1,0:T(8,128)(2,1)S(1)}, bf16[32,1536]{1,0:T(8,128)(2,1)}, u32[]{:S(2)}, u32[]{:S(2)}) collective-permute-start(bf16[32,1536]{1,0:T(8,128)(2,1)S(1)} %get-tuple-element.20), channel_id=1, source_target_pairs={{0,2},{1,3},{2,0},{3,1},{4,6},{5,7},{6,4},{7,5},{8,10},{9,11},{10,... | collective-permute-start | bytes 294920 | tf_op jit(solution)/shard_map/ppermute | solution.py:25
  94.4 27.6 %collective-permute-start.16 = (bf16[32,1664]{1,0:T(8,128)(2,1)S(1)}, bf16[32,1664]{1,0:T(8,128)(2,1)S(1)}, u32[]{:S(2)}, u32[]{:S(2)}) collective-permute-start(bf16[32,1664]{1,0:T(8,128)(2,1)S(1)} %concatenate.19), channel_id=1, source_target_pairs={{0,28},{4,24},{8,20},{12,16},{16,12},{20,8},{24,4},{28,0},{1,29},{... | collective-permute-start | bytes 319496 | tf_op jit(solution)/shard_map/ppermute | solution.py:25
  97.0 25.0 %collective-permute-start.15 = (bf16[32,1664]{1,0:T(8,128)(2,1)S(1)}, bf16[32,1664]{1,0:T(8,128)(2,1)S(1)}, u32[]{:S(2)}, u32[]{:S(2)}) collective-permute-start(bf16[32,1664]{1,0:T(8,128)(2,1)S(1)} %concatenate.19), channel_id=1, source_target_pairs={{0,24},{4,28},{8,16},{12,20},{16,8},{20,12},{24,0},{28,4},{1,25},{... | collective-permute-start | bytes 319496 | tf_op jit(solution)/shard_map/ppermute | solution.py:25
  98.8 23.1 %collective-permute-start.14 = (bf16[32,1664]{1,0:T(8,128)(2,1)S(1)}, bf16[32,1664]{1,0:T(8,128)(2,1)S(1)}, u32[]{:S(2)}, u32[]{:S(2)}) collective-permute-start(bf16[32,1664]{1,0:T(8,128)(2,1)S(1)} %concatenate.19), channel_id=1, source_target_pairs={{0,20},{4,16},{8,28},{12,24},{16,4},{20,0},{24,12},{28,8},{1,21},{... | collective-permute-start | bytes 319496 | tf_op jit(solution)/shard_map/ppermute | solution.py:25
  98.9 23.1 %collective-permute-start.13 = (bf16[32,1664]{1,0:T(8,128)(2,1)S(1)}, bf16[32,1664]{1,0:T(8,128)(2,1)S(1)}, u32[]{:S(2)}, u32[]{:S(2)}) collective-permute-start(bf16[32,1664]{1,0:T(8,128)(2,1)S(1)} %concatenate.19), channel_id=1, source_target_pairs={{0,16},{4,20},{8,24},{12,28},{16,0},{20,4},{24,8},{28,12},{1,17},{... | collective-permute-start | bytes 319496 | tf_op jit(solution)/shard_map/ppermute | solution.py:25
  102.1 4.7 %collective-permute-start.10 = (bf16[32,1664]{1,0:T(8,128)(2,1)S(1)}, bf16[32,1664]{1,0:T(8,128)(2,1)S(1)}, u32[]{:S(2)}, u32[]{:S(2)}) collective-permute-start(bf16[32,1664]{1,0:T(8,128)(2,1)S(1)} %concatenate.19), channel_id=1, source_target_pairs={{0,4},{4,0},{8,12},{12,8},{16,20},{20,16},{24,28},{28,24},{1,5},{5... | collective-permute-start | bytes 319496 | tf_op jit(solution)/shard_map/ppermute | solution.py:25
  106.8 9.5 %collective-permute-start.11 = (bf16[32,1664]{1,0:T(8,128)(2,1)S(1)}, bf16[32,1664]{1,0:T(8,128)(2,1)S(1)}, u32[]{:S(2)}, u32[]{:S(2)}) collective-permute-start(bf16[32,1664]{1,0:T(8,128)(2,1)S(1)} %concatenate.19), channel_id=1, source_target_pairs={{0,8},{4,12},{8,0},{12,4},{16,24},{20,28},{24,16},{28,20},{1,9},{5... | collective-permute-start | bytes 319496 | tf_op jit(solution)/shard_map/ppermute | solution.py:25
  116.3 5.6 %collective-permute-start.12 = (bf16[32,1664]{1,0:T(8,128)(2,1)S(1)}, bf16[32,1664]{1,0:T(8,128)(2,1)S(1)}, u32[]{:S(2)}, u32[]{:S(2)}) collective-permute-start(bf16[32,1664]{1,0:T(8,128)(2,1)S(1)} %concatenate.19), channel_id=1, source_target_pairs={{0,12},{4,8},{8,4},{12,0},{16,28},{20,24},{24,20},{28,16},{1,13},{... | collective-permute-start | bytes 319496 | tf_op jit(solution)/shard_map/ppermute | solution.py:25
  129.1 6.3 %collective-permute-start.17 = (bf16[32,1536]{1,0:T(8,128)(2,1)S(1)}, bf16[32,1536]{1,0:T(8,128)(2,1)S(1)}, u32[]{:S(2)}, u32[]{:S(2)}) collective-permute-start(bf16[32,1536]{1,0:T(8,128)(2,1)S(1)} %get-tuple-element.11), channel_id=1, source_target_pairs={{0,4},{4,0},{8,12},{12,8},{16,20},{20,16},{24,28},{28,24},{1,5},{5... | collective-permute-start | bytes 294920 | tf_op jit(solution)/shard_map/ppermute | solution.py:25
  130.1 8.1 %collective-permute-start.22 = (bf16[32,1536]{1,0:T(8,128)(2,1)S(1)}, bf16[32,1536]{1,0:T(8,128)(2,1)S(1)}, u32[]{:S(2)}, u32[]{:S(2)}) collective-permute-start(bf16[32,1536]{1,0:T(8,128)(2,1)S(1)} %get-tuple-element.12), channel_id=1, source_target_pairs={{0,24},{4,28},{8,16},{12,20},{16,8},{20,12},{24,0},{28,4},{1,25},{... | collective-permute-start | bytes 294920 | tf_op jit(solution)/shard_map/ppermute | solution.py:25
  132.3 10.0 %collective-permute-start.21 = (bf16[32,1536]{1,0:T(8,128)(2,1)S(1)}, bf16[32,1536]{1,0:T(8,128)(2,1)S(1)}, u32[]{:S(2)}, u32[]{:S(2)}) collective-permute-start(bf16[32,1536]{1,0:T(8,128)(2,1)S(1)} %get-tuple-element.13), channel_id=1, source_target_pairs={{0,20},{4,16},{8,28},{12,24},{16,4},{20,0},{24,12},{28,8},{1,21},{... | collective-permute-start | bytes 294920 | tf_op jit(solution)/shard_map/ppermute | solution.py:25
  132.3 10.8 %collective-permute-start.20 = (bf16[32,1536]{1,0:T(8,128)(2,1)S(1)}, bf16[32,1536]{1,0:T(8,128)(2,1)S(1)}, u32[]{:S(2)}, u32[]{:S(2)}) collective-permute-start(bf16[32,1536]{1,0:T(8,128)(2,1)S(1)} %get-tuple-element.14), channel_id=1, source_target_pairs={{0,16},{4,20},{8,24},{12,28},{16,0},{20,4},{24,8},{28,12},{1,17},{... | collective-permute-start | bytes 294920 | tf_op jit(solution)/shard_map/ppermute | solution.py:25
  135.3 7.8 %collective-permute-start.19 = (bf16[32,1536]{1,0:T(8,128)(2,1)S(1)}, bf16[32,1536]{1,0:T(8,128)(2,1)S(1)}, u32[]{:S(2)}, u32[]{:S(2)}) collective-permute-start(bf16[32,1536]{1,0:T(8,128)(2,1)S(1)} %get-tuple-element.15), channel_id=1, source_target_pairs={{0,12},{4,8},{8,4},{12,0},{16,28},{20,24},{24,20},{28,16},{1,13},{... | collective-permute-start | bytes 294920 | tf_op jit(solution)/shard_map/ppermute | solution.py:25
  135.4 9.5 %collective-permute-start.18 = (bf16[32,1536]{1,0:T(8,128)(2,1)S(1)}, bf16[32,1536]{1,0:T(8,128)(2,1)S(1)}, u32[]{:S(2)}, u32[]{:S(2)}) collective-permute-start(bf16[32,1536]{1,0:T(8,128)(2,1)S(1)} %get-tuple-element.16), channel_id=1, source_target_pairs={{0,8},{4,12},{8,0},{12,4},{16,24},{20,28},{24,16},{28,20},{1,9},{5... | collective-permute-start | bytes 294920 | tf_op jit(solution)/shard_map/ppermute | solution.py:25
  138.2 7.3 %collective-permute-start.23 = (bf16[32,1536]{1,0:T(8,128)(2,1)S(1)}, bf16[32,1536]{1,0:T(8,128)(2,1)S(1)}, u32[]{:S(2)}, u32[]{:S(2)}) collective-permute-start(bf16[32,1536]{1,0:T(8,128)(2,1)S(1)} %get-tuple-element.17), channel_id=1, source_target_pairs={{0,28},{4,24},{8,20},{12,16},{16,12},{20,8},{24,4},{28,0},{1,29},{... | collective-permute-start | bytes 294920 | tf_op jit(solution)/shard_map/ppermute | solution.py:25
  (6 other events, 4.8 us)

commit v2 on v1

v2 whole, which is shorter than its diff:
```python
import functools

import jax
import jax.numpy as jnp
import numpy as np
from jax import lax
from jax.experimental import pallas as pl
from jax.experimental.pallas import tpu as pltpu
from jax.sharding import PartitionSpec as P

HD = 64
FFE = 512
BLK = 128
PAGES = 3
CHUNK = 96
COSTS = (12.0, 3.0, 12.0, 12.0, 12.0, 4.0, 12.0)
NEG = -1e30
BF = jnp.bfloat16
F32 = jnp.float32


def iota(shape, dim):
    return lax.broadcasted_iota(jnp.int32, shape, dim)


def swap(value, axis, distance):
    size = lax.axis_size(axis)
    return lax.ppermute(value, axis, [(source, source ^ distance) for source in range(size)])


def gather_rows(value, axis):
    size = lax.axis_size(axis)
    held = {0: value}
    far = size // 2
    for distance in list(range(far, size, 2)) + list(range(2, far, 2)) + list(range(1, far, 2)):
        held[distance] = swap(value, axis, distance)
    for distance in range(far + 1, size, 2):
        held[distance] = swap(held[distance - 1], axis, 1)
    return [held[distance] for distance in range(size)]


def send_rows(values, axis):
    size = lax.axis_size(axis)
    held = {0: values[0]}
    far = size // 2
    for start in list(range(size - 2, far - 1, -2)) + list(range(2, far, 2)) + [0]:
        for distance in (start, start + 1):
            if distance:
                held[distance] = swap(values[distance], axis, distance)
    return [held[distance] for distance in range(size)]


def sum_rows(values, axis):
    size = lax.axis_size(axis)
    far = size // 2
    beside = {distance: swap(values[distance], axis, 1) for distance in range(far + 1, size, 2)}
    arrived = [swap(values[distance], axis, distance) for distance in list(range(2, far, 2)) + list(range(1, far, 2))]
    for distance in range(far, size, 2):
        joined = values[distance].astype(F32) + beside[distance + 1].astype(F32)
        arrived.append(swap(joined.astype(BF), axis, distance))
    total = values[0].astype(F32)
    for value in arrived:
        total = total + value.astype(F32)
    return total


def cost(micros):
    return pl.CostEstimate(flops=int(micros * 1e9), bytes_accessed=int(micros * 3e6), transcendentals=0)


def project_rows(normed, weight):
    return lax.dot_general(normed, weight, (((1,), (1,)), ((), ())), preferred_element_type=F32)


def dot(left, right):
    return jnp.dot(left, right, preferred_element_type=F32)


def rotate(values, cosines, sines):
    width = values.shape[1]
    low = iota((1, 2 * HD), 1) % HD < HD // 2
    pieces = []
    for start in range(0, width, 2 * HD):
        tile = values[:, start : start + 2 * HD]
        short = 2 * HD - tile.shape[1]
        if short:
            tile = jnp.concatenate([tile, tile], 1)
        turned = jnp.where(low, pltpu.roll(tile, 2 * HD - HD // 2, 1), pltpu.roll(tile, HD // 2, 1))
        pieces.append((tile * cosines + turned * sines)[:, : 2 * HD - short])
    return pieces[0] if len(pieces) == 1 else jnp.concatenate(pieces, 1)


def table_kernel(req_ref, length_ref, frequency_ref, cosines_ref, sines_ref):
    rows, width = cosines_ref.shape
    lengths = jnp.broadcast_to(length_ref[pl.ds(req_ref[0], 1), :].astype(F32), (rows, rows))
    lengths = jnp.where(iota((rows, rows), 0) == iota((rows, rows), 1), lengths, 0.0)
    angles = jnp.sum(lengths, -1, keepdims=True) * frequency_ref[...]
    cosines_ref[...] = jnp.cos(angles)
    sines = jnp.sin(angles)
    sines_ref[...] = jnp.where(iota((rows, width), 1) % HD < HD // 2, -sines, sines)


def query_kernel(hidden_ref, gain_ref, weight_ref, cosines_ref, sines_ref, query_ref, normed_ref):
    hidden = hidden_ref[...].astype(F32)
    scale = lax.rsqrt(jnp.mean(hidden * hidden, -1, keepdims=True) + 1e-05)
    normed = (hidden * scale * gain_ref[...]).astype(BF)
    normed_ref[...] = normed
    query = project_rows(normed, weight_ref[...])
    query_ref[...] = (rotate(query, cosines_ref[...], sines_ref[...]) * 0.125).astype(BF)


def fresh_kernel(normed_ref, key_weight_ref, value_weight_ref, cosines_ref, sines_ref, key_ref, value_ref):
    key = project_rows(normed_ref[...], key_weight_ref[...])
    key_ref[...] = rotate(key, cosines_ref[...], sines_ref[...]).astype(BF)
    value_ref[...] = project_rows(normed_ref[...], value_weight_ref[...]).astype(BF)


def attend_kernel(heads, groups, chunk, nq, *refs):
    qrow_ref, left_ref, slot_ref, local_ref = refs[:4]
    query_refs = refs[4:4+nq]
    key_ref, value_ref = refs[4 + nq : 6 + nq]
    out_refs = refs[6 + nq : -5]
    asked_ref, laid_ref, mean_ref, level_ref, rows_ref = refs[-5:]
    blocks = qrow_ref.shape[0]
    lanes = key_ref.shape[1]
    share, width = out_refs[0].shape
    per_group = heads // groups
    feature = heads * HD
    index = pl.program_id(0)

    @pl.when(index == 0)
    def _():
        total = None
        for place, query_ref in enumerate(query_refs):
            count = query_ref.shape[0]
            picked = (iota((blocks, count), 1) + place * count == qrow_ref[...]).astype(BF)
            part = dot(picked, query_ref[...])
            total = part if total is None else total + part
        asked_ref[...] = total
        laid_ref[...] = jnp.zeros(laid_ref.shape, F32)

    base = pl.multiple_of(index * chunk, chunk)
    rows = pl.ds(base, chunk)
    low = iota((chunk, 2 * HD), 1) < HD
    for pair in range((heads + 1) // 2):
        stop = min(feature, (pair + 1) * 2 * HD)
        tile = asked_ref[rows, pair * 2 * HD : stop]
        if tile.shape[1] < 2 * HD:
            tile = jnp.concatenate([tile, tile], 1)
        turned = pltpu.roll(tile, HD, 1)
        for odd in range(2):
            head = 2 * pair + odd
            if head < heads:
                first, second = (turned, tile) if odd else (tile, turned)
                laid_ref[pl.ds(head, chunk, 16), :] = jnp.where(low, first, 0.0)
                laid_ref[pl.ds(head + 8, chunk, 16), :] = jnp.where(low, 0.0, second)
    query = laid_ref[...].astype(BF)
    scores = lax.dot_general(
        query.reshape(chunk // 2, 32, 2 * HD), key_ref[...].reshape(chunk // 2, 2 * lanes, 2 * HD),
        (((2,), (2,)), ((0,), (0,))), preferred_element_type=F32)
    scores = jnp.concatenate([scores[:, None, :16, :lanes], scores[:, None, 16:, lanes:]], 1).reshape(chunk, 16, lanes)
    cell_row = iota((8, lanes), 0)
    cell_lane = iota((8, lanes), 1)
    position = jnp.where(cell_lane % groups == cell_row // per_group, 2 * (cell_lane // groups), 1 << 20)
    position = position.astype(F32)[None]
    spread = (iota((chunk * 8, chunk), 0) // 8 == iota((chunk * 8, chunk), 1)).astype(BF)
    remaining = jnp.broadcast_to(left_ref[...].astype(F32), (chunk, lanes)).astype(BF)
    remaining = dot(spread, remaining).reshape(chunk, 8, lanes)
    usable = jnp.concatenate([position < remaining, position + 1.0 < remaining], 1)
    scores = jnp.where(usable, scores, NEG)
    highest = jnp.max(jnp.maximum(scores[:, :8], scores[:, 8:]), -1, keepdims=True)
    weights = jnp.where(usable, jnp.exp(scores - jnp.concatenate([highest, highest], 1)), 0.0)
    total = jnp.sum(weights[:, :8] + weights[:, 8:], -1, keepdims=True)
    weights = weights.astype(BF).reshape(chunk // 2, 2, 16, lanes)
    none = jnp.zeros((chunk // 2, 16, lanes), BF)
    weights = jnp.concatenate([jnp.concatenate([weights[:, 0], none], 2), jnp.concatenate([none, weights[:, 1]], 2)], 1)
    numer = lax.dot_general(weights, value_ref[...].reshape(chunk // 2, 2 * lanes, 2 * HD), (((2,), (1,)), ((0,), (0,))), preferred_element_type=F32)
    numer = numer.reshape(chunk, 16, 2 * HD)
    numer = jnp.where(iota((1, 8, 2 * HD), 2) < HD, numer[:, :8], numer[:, 8:]).reshape(chunk * 8, 2 * HD)
    numer = numer + pltpu.roll(numer, HD, 1)
    total = total.reshape(chunk * 8, 1)
    highest = highest.reshape(chunk * 8, 1)
    some = total > 0.0
    safe = jnp.where(some, total, 1.0)
    mean_ref[...] = numer / safe
    level_ref[...] = jnp.broadcast_to(jnp.where(some, highest + jnp.log(safe), NEG), (chunk * 8, 2 * HD))
    lane = iota((chunk, 2 * HD), 1)
    means = [mean_ref[pl.ds(head, chunk, 8), :] for head in range(heads)]
    extras = jnp.zeros((chunk, 2 * HD), F32)
    start = feature % (2 * HD)
    for head in range(heads):
        level = level_ref[pl.ds(head, chunk, 8), :]
        first = level.astype(BF).astype(F32)
        second = (level - first).astype(BF).astype(F32)
        third = level - first - second
        for part, piece in enumerate((first, second, third)):
            extras = jnp.where(lane == start + 4 * head + part, piece, extras)
    extras = jnp.where(lane == start + HD - 1, local_ref[...].astype(F32), extras)
    for pair in range(width // (2 * HD)):
        left = means[2 * pair] if 2 * pair < heads else extras
        right = means[2 * pair + 1] if 2 * pair + 1 < heads else extras
        rows_ref[rows, pair * 2 * HD : (pair + 1) * 2 * HD] = jnp.where(low, left, right).astype(BF)

    @pl.when(index == blocks // chunk - 1)
    def _():
        order = (slot_ref[...] == iota((blocks, blocks), 0)).astype(BF)
        sorted_rows = dot(order, rows_ref[...])
        for place, out_ref in enumerate(out_refs):
            out_ref[...] = sorted_rows[place * share : (place + 1) * share].astype(BF)

def attend(heads, groups, chunk, width, qrow, left, slot, local, queries, keys, values, limit=24):
    blocks, lanes = keys.shape[:2]
    whole = pl.BlockSpec(memory_space=pltpu.VMEM)
    block = lambda *shape: pl.BlockSpec(shape, lambda i: (i,) + (0,) * (len(shape) - 1))
    return pl.pallas_call(
        functools.partial(attend_kernel, heads, groups, chunk, len(queries)),
        grid=(blocks // chunk,),
        out_shape=[jax.ShapeDtypeStruct((blocks // len(queries), width), BF)] * len(queries),
        in_specs=[whole, block(chunk, 1), whole, block(chunk, 1)] + [whole] * len(queries)
        + [block(chunk, lanes, 2 * HD)] * 2,
        out_specs=[whole] * len(queries),
        scratch_shapes=[
            pltpu.VMEM((blocks, heads * HD), F32),
            pltpu.VMEM((chunk * 16, 2 * HD), F32),
            pltpu.VMEM((chunk * 8, 2 * HD), F32),
            pltpu.VMEM((chunk * 8, 2 * HD), F32),
            pltpu.VMEM((blocks, width), BF),
        ],
        compiler_params=pltpu.CompilerParams(vmem_limit_bytes=limit << 20),
        cost_estimate=cost(COSTS[2]),
        name="attend",
    )(qrow, left, slot, local, *queries, keys, values)


def merge_kernel(heads, groups, tokens, *refs):
    kv_ref, query_ref, key_ref, value_ref, weight_ref = refs[:5]
    out_refs = refs[-1 - tokens : -1]
    result_ref = refs[-1]
    part_refs = refs[5 : -1 - tokens]
    parts = jnp.concatenate([part_ref[...] for part_ref in part_refs], 0)
    rows = query_ref.shape[0]
    blocks, width = parts.shape
    per_group = heads // groups
    feature = heads * HD
    row = iota((32, width), 0)
    column = iota((32, width), 1) - feature
    wanted = jnp.where(row < 24, (row % 8) * 4 + row // 8, HD - 1)
    pick = jnp.logical_and(column == wanted, jnp.logical_or(row == 24, row % 8 < heads))
    pick = jnp.logical_and(pick, row <= 24).astype(BF)
    extras = lax.dot_general(pick, parts, (((1,), (1,)), ((), ())), preferred_element_type=F32)
    levels = extras[0:8] + extras[8:16] + extras[16:24]
    local = extras[24:25].astype(jnp.int32)
    member = local == iota((rows, blocks), 0)

    source = iota((groups * HD, width), 0)
    target = iota((groups * HD, width), 1)
    same = jnp.logical_and(source // HD == target // (HD * per_group), source % HD == target % HD)
    widen = same.astype(BF)
    key = dot(key_ref[...], widen)
    value = dot(value_ref[...], widen)
    products = query_ref[...].astype(F32) * key[:, :feature]
    lane_head = iota((rows, width), 1) // HD
    joined = jnp.zeros((rows, width), F32)
    for head in range(heads):
        own = jnp.sum(jnp.where(lane_head[:, :feature] == head, products, 0.0), -1, keepdims=True)
        level = levels[head : head + 1]
        highest = jnp.max(jnp.where(member, level, NEG), -1, keepdims=True)
        highest = jnp.maximum(highest, own)
        weights = jnp.where(member, jnp.exp(level - highest), 0.0).astype(BF)
        own_weight = jnp.exp(own - highest)
        total = jnp.sum(weights.astype(F32), -1, keepdims=True) + own_weight
        numer = dot(weights, parts) + own_weight * value
        joined = jnp.where(lane_head == head, numer / total, joined)
    attended = joined[:, :feature].astype(BF)
    result_ref[...] = dot(attended, weight_ref[...])
    count = rows // tokens
    for place, out_ref in enumerate(out_refs):
        start = pl.multiple_of(jnp.bitwise_xor(kv_ref[0], place) * count, count)
        out_ref[...] = result_ref[pl.ds(start, count), :].astype(BF)


def route_kernel(kv_ref, hidden_ref, gain_ref, router_ref, routes_ref, *refs):
    piece_refs = refs[:-2]
    after_ref, out_ref = refs[-2:]
    count, model = after_ref.shape
    start = pl.multiple_of(kv_ref[0] * count, count)
    total = piece_refs[0][...].astype(F32)
    for piece_ref in piece_refs[1:]:
        total = total + piece_ref[...].astype(F32)
    after = hidden_ref[pl.ds(start, count), :].astype(F32) + total
    after_ref[...] = after
    scale = lax.rsqrt(jnp.mean(after * after, -1, keepdims=True) + 1e-05)
    normed = (after * scale * gain_ref[...]).astype(BF)
    out_ref[:, :model] = normed
    experts = router_ref.shape[1]
    logits = dot(normed, router_ref[...])
    expert = iota((count, experts), 1)
    chosen = expert == routes_ref[:, 0:1]
    for turn in range(1, routes_ref.shape[1]):
        chosen = jnp.logical_or(chosen, expert == routes_ref[:, turn : turn + 1])
    logits = jnp.where(chosen, logits, NEG)
    gates = jnp.where(chosen, jnp.exp(logits - jnp.max(logits, -1, keepdims=True)), 0.0)
    gates = gates / jnp.sum(gates, -1, keepdims=True)
    high = gates.astype(BF).astype(F32)
    spare = jnp.zeros((count, 128 - 2 * experts), F32)
    out_ref[:, model:] = jnp.concatenate([high, gates - high, spare], 1).astype(BF)


def expert_kernel(sources, experts, req_ref, *refs):
    token_refs = refs[:sources]
    up_ref, down_ref = refs[sources : sources + 2]
    out_refs = refs[sources + 2 : -2]
    tokens_ref, mixed_ref = refs[-2:]
    index = pl.program_id(0)
    count, model = out_refs[0].shape
    hidden = down_ref.shape[1]

    @pl.when(index == 0)
    def _():
        for place, token_ref in enumerate(token_refs):
            tokens_ref[place * count : (place + 1) * count, :] = token_ref[...]

    lane = iota((sources * count, 128), 1)
    mine = req_ref[0] * pl.num_programs(0) + index
    gates = tokens_ref[:, model:].astype(F32)
    picked = jnp.logical_or(lane == mine, lane == mine + experts)
    gate = jnp.sum(jnp.where(picked, gates, 0.0), -1, keepdims=True)
    both = dot(tokens_ref[:, :model], up_ref[0])
    active = (jax.nn.silu(both[:, :hidden]) * both[:, hidden:]).astype(BF)
    produced = dot(active, down_ref[0]).astype(BF).astype(F32) * gate

    @pl.when(index == 0)
    def _():
        mixed_ref[...] = produced

    @pl.when(index > 0)
    def _():
        mixed_ref[...] += produced

    @pl.when(index == pl.num_programs(0) - 1)
    def _():
        for place, out_ref in enumerate(out_refs):
            out_ref[...] = mixed_ref[place * count : (place + 1) * count, :].astype(BF)


def shards(
    hidden_in,
    attn_gain,
    w_query,
    w_key,
    w_value,
    w_out,
    k_cache,
    v_cache,
    cache_len,
    block_slot,
    moe_gain,
    w_router,
    w_gate_up,
    w_down,
    routes,
):
    req_index = lax.axis_index("req")
    kv_index = lax.axis_index("kv")
    sources = lax.axis_size("req")
    kv_size = lax.axis_size("kv")
    row_count, model = hidden_in.shape
    heads = w_query.shape[0] // HD
    groups = w_key.shape[0] // HD
    blocks = k_cache.shape[0]
    requests = cache_len.shape[0]
    share = blocks // sources
    width = -(-(heads * HD + HD) // 128) * 128

    vmem = pl.BlockSpec(memory_space=pltpu.VMEM)
    scalar = pl.BlockSpec(memory_space=pltpu.SMEM)
    req_scalar = jnp.reshape(req_index, (1,)).astype(jnp.int32)
    frequency = 10000.0 ** (-(np.arange(2 * HD) % (HD // 2)) / (HD // 2))
    cosines, sines = pl.pallas_call(
        table_kernel,
        out_shape=[jax.ShapeDtypeStruct((row_count, 2 * HD), F32)] * 2,
        in_specs=[scalar, vmem, vmem],
        out_specs=[vmem] * 2,
        compiler_params=pltpu.CompilerParams(vmem_limit_bytes=4 << 20),
        cost_estimate=cost(COSTS[6]),
        name="tables",
    )(req_scalar, cache_len.reshape(sources, row_count), jnp.asarray(frequency[None, :], F32))
    query, normed = pl.pallas_call(
        query_kernel,
        out_shape=[
            jax.ShapeDtypeStruct((row_count, heads * HD), BF),
            jax.ShapeDtypeStruct((row_count, model), BF),
        ],
        in_specs=[vmem] * 5,
        out_specs=[vmem] * 2,
        cost_estimate=cost(COSTS[0]),
        compiler_params=pltpu.CompilerParams(vmem_limit_bytes=8 << 20),
        name="query",
    )(hidden_in, attn_gain[None, :], w_query, cosines, sines)
    key_new, value_new = pl.pallas_call(
        fresh_kernel,
        out_shape=[jax.ShapeDtypeStruct((row_count, groups * HD), BF)] * 2,
        in_specs=[vmem] * 5,
        out_specs=[vmem] * 2,
        cost_estimate=cost(COSTS[1]),
        compiler_params=pltpu.CompilerParams(vmem_limit_bytes=8 << 20),
        name="fresh",
    )(normed, w_key, w_value, cosines, sines)
    queries = gather_rows(query, "req")

    owners = block_slot // PAGES
    home = owners // row_count
    local = owners % row_count
    owned = owners[:, None] == jnp.arange(requests, dtype=jnp.int32)[None, :]
    lengths = jnp.sum(jnp.where(owned, cache_len[None, :], 0), 1)
    left = lengths - (block_slot % PAGES) * BLK
    left = jnp.clip(left, 0, BLK)
    number = jnp.arange(blocks, dtype=jnp.int32)
    earlier = jnp.logical_and(home[:, None] == home[None, :], number[:, None] < number[None, :])
    rank = jnp.sum(earlier.astype(jnp.int32), 0)
    place = jnp.bitwise_xor(home, req_index)
    slot = place * share + rank
    query_row = place * row_count + local

    def pairs(cache):
        cache = cache.reshape(blocks, groups, HD, 2 * HD).transpose(0, 2, 1, 3)
        return cache.reshape(blocks, HD * groups, 2 * HD)

    partial = attend(
        heads, groups, CHUNK, width, query_row[:, None], left[:, None], slot[None, :], local[:, None],
        queries, pairs(k_cache), pairs(v_cache),
    )
    parts = send_rows(partial, "req")
    kv_scalar = jnp.reshape(kv_index, (1,)).astype(jnp.int32)
    token_count = row_count // kv_size
    projected = pl.pallas_call(
        functools.partial(merge_kernel, heads, groups, kv_size),
        out_shape=[jax.ShapeDtypeStruct((token_count, model), BF)] * kv_size,
        in_specs=[scalar] + [vmem] * (4 + sources),
        out_specs=[vmem] * kv_size,
        scratch_shapes=[pltpu.VMEM((row_count, model), F32)],
        compiler_params=pltpu.CompilerParams(vmem_limit_bytes=10 << 20),
        cost_estimate=cost(COSTS[3]),
        name="merge",
    )(kv_scalar, query, key_new, value_new, w_out, *parts)
    pieces = [projected[0]]
    for distance in range(1, kv_size):
        pieces.append(swap(projected[distance], "kv", distance))
    after_attn, outgoing = pl.pallas_call(
        route_kernel,
        out_shape=[
            jax.ShapeDtypeStruct((token_count, model), F32),
            jax.ShapeDtypeStruct((token_count, model + 128), BF),
        ],
        in_specs=[scalar] + [vmem] * (4 + kv_size),
        out_specs=[vmem, vmem],
        compiler_params=pltpu.CompilerParams(vmem_limit_bytes=10 << 20),
        cost_estimate=cost(COSTS[4]),
        name="route",
    )(kv_scalar, hidden_in, moe_gain[None, :], w_router, routes, *pieces)
    arrived = gather_rows(outgoing, "req")
    local_experts = w_gate_up.shape[0]
    mixed = pl.pallas_call(
        functools.partial(expert_kernel, sources, w_router.shape[1]),
        grid=(local_experts,),
        out_shape=[jax.ShapeDtypeStruct((token_count, model), BF)] * sources,
        in_specs=[scalar]
        + [vmem] * sources
        + [
            pl.BlockSpec((1,) + w_gate_up.shape[1:], lambda i: (i, 0, 0)),
            pl.BlockSpec((1,) + w_down.shape[1:], lambda i: (i, 0, 0)),
        ],
        out_specs=[vmem] * sources,
        scratch_shapes=[
            pltpu.VMEM((sources * token_count, model + 128), BF),
            pltpu.VMEM((sources * token_count, model), F32),
        ],
        compiler_params=pltpu.CompilerParams(vmem_limit_bytes=24 << 20),
        cost_estimate=cost(COSTS[5]),
        name="experts",
    )(req_scalar, *arrived, w_gate_up, w_down)
    mixture = sum_rows(mixed, "req")
    return (after_attn + mixture).astype(BF)


def solution(mesh):
    placed = (
        P("req", None),
        P(),
        P("kv", None),
        P("kv", None),
        P("kv", None),
        P("kv", None),
        P("req", "kv", None),
        P("req", "kv", None),
        P(),
        P("req"),
        P(),
        P(),
        P("req", None, None),
        P("req", None, None),
        P(("req", "kv"), None),
    )
    return jax.shard_map(
        shards, mesh=mesh, in_specs=placed, out_specs=P(("req", "kv"), None), check_vma=False
    )
```

time: 147 us -> 99.5 us (0.68)
  matrix products: 13.1 us -> 0 us
  Pallas kernels: 28.5 us -> 17.2 us
  starting transfers between devices: 47 us -> 38.2 us
  other arithmetic: 9.28 us -> 1.31 us
  local copies, waits for them, and re-layouts: 11 us -> 6.51 us
    dot_general x6 -> x0, matrix products: 13.1 us -> none  [the longest x3 6.1 us: project_rows(): lax.dot_general(normed, weight, (((1,), (1,)), ((), ())), preferred_eleme...]
    pallas_call x2 -> x7, Pallas kernels: 28.5 us -> 17.2 us  [the longest x1 10.4 us: attend(): pl.pallas_call(functools.partial(attend_kernel, heads, groups, chunk, len...]
    all_to_all x1 -> x0, starting transfers between devices: 7.68 us -> none  [shards(): lax.all_to_all(partial, 'req', split_axis=0, concat_axis=0, tiled=True)]
    reduce_sum x3 -> x0, other arithmetic: 2.66 us -> none  [the longest x2 2.47 us: rms_norm(): jnp.mean(values * values, -1, keepdims=True) + 1e-05]
    all_to_all x1 -> x0, waiting for transfers between devices: 2.17 us -> none  [shards(): lax.all_to_all(partial, 'req', split_axis=0, concat_axis=0, tiled=True)]
    convert_element_type x2 -> x0, local copies, waits for them, and re-layouts: 1.58 us -> none  [the longest x1 1.46 us: shards(): rotate(key_new, lengths_home).astype(BF).reshape(row_count, groups * HD)]
    convert_element_type x4 -> x2, other arithmetic: 1.57 us -> 0.05 us  [sum_rows(): arrived.append(swap(joined.astype(BF), axis, distance))]
    ppermute x24 -> x31, starting transfers between devices: 39.3 us -> 38.2 us  [swap(): lax.ppermute(value, axis, [(source, source ^ distance) for source in rang...]
  transfers between devices with their start and end apart: 25 -> 31, of which waited for: 13 -> 14; matrix products, arithmetic and copies ran while one was open for 7% -> 1% of each run, Pallas kernels for 0% -> 0%
where the time goes in v2:
time: 99.5 us; the launch traced here: 99.3 us
  starting transfers between devices  38.2 us (38%)
  waiting for transfers between devices  35.7 us (36%)
  Pallas kernels  17.2 us (17%)
  local copies, waits for them, and re-layouts  6.51 us (7%)
  other arithmetic  1.31 us (1%)
    ppermute x31, starting transfers between devices, swap(): lax.ppermute(value, axis, [(source, source ^ distance) for source in rang...  38.2 us
    ppermute x31, waiting for transfers between devices, swap(): lax.ppermute(value, axis, [(source, source ^ distance) for source in rang...  35.7 us
    pallas_call x1, Pallas kernels, attend(): pl.pallas_call(functools.partial(attend_kernel, heads, groups, chunk, len...  10.4 us
    unnamed x42, local copies, waits for them, and re-layouts  5.48 us
    pallas_call x1, Pallas kernels, shards(): pl.pallas_call(functools.partial(expert_kernel, sources, w_router.shape[1...  3.44 us
  transfers between devices with their start and end apart: 31, of which 14 were waited for; matrix products, arithmetic and copies ran while one was open for 1% of the time, Pallas kernels for 0%

profile of v2, /device:TPU:0, one launch (start us, length us, event | category | flops | bytes accessed | tf_op | source)
XLA Modules:
  0.0 99.3 jit_solution(10363809754355795251)
XLA Ops:
  4.1 5.1 %collective-permute-start.5 = (bf16[128,384]{1,0:T(8,128)(2,1)S(1)}, bf16[128,384]{1,0:T(8,128)(2,1)S(1)}, u32[]{:S(2)}, u32[]{:S(2)}) collective-permute-start(bf16[128,384]{1,0:T(8,128)(2,1)S(1)} %get-tuple-element.35.refs_4_.refs_1_), channel_id=1, source_target_pairs={{0,24},{4,28},{8,16},{12,20},{16,8},{20,12},{24,0},{28,4},{1,25},{... | collective-permute-start | bytes 294920 | tf_op jit(solution)/shard_map/ppermute | solution.py:28
  9.2 1.7 %collective-permute-start.2 = (bf16[128,384]{1,0:T(8,128)(2,1)S(1)}, bf16[128,384]{1,0:T(8,128)(2,1)S(1)}, u32[]{:S(2)}, u32[]{:S(2)}) collective-permute-start(bf16[128,384]{1,0:T(8,128)(2,1)S(1)} %get-tuple-element.35.refs_4_.refs_1_), channel_id=1, source_target_pairs={{0,12},{4,8},{8,4},{12,0},{16,28},{20,24},{24,20},{28,16},{1,13},{... | collective-permute-start | bytes 294920 | tf_op jit(solution)/shard_map/ppermute | solution.py:28
  10.9 1.2 %collective-permute-start.1 = (bf16[128,384]{1,0:T(8,128)(2,1)S(1)}, bf16[128,384]{1,0:T(8,128)(2,1)S(1)}, u32[]{:S(2)}, u32[]{:S(2)}) collective-permute-start(bf16[128,384]{1,0:T(8,128)(2,1)S(1)} %get-tuple-element.35.refs_4_.refs_1_), channel_id=1, source_target_pairs={{0,8},{4,12},{8,0},{12,4},{16,24},{20,28},{24,16},{28,20},{1,9},{5... | collective-permute-start | bytes 294920 | tf_op jit(solution)/shard_map/ppermute | solution.py:28
  13.2 1.6 %collective-permute-start.6 = (bf16[128,384]{1,0:T(8,128)(2,1)S(1)}, bf16[128,384]{1,0:T(8,128)(2,1)S(1)}, u32[]{:S(2)}, u32[]{:S(2)}) collective-permute-start(bf16[128,384]{1,0:T(8,128)(2,1)S(1)} %collective-permute-done.5.refs_10_), channel_id=1, source_target_pairs={{0,4},{4,0},{8,12},{12,8},{16,20},{20,16},{24,28},{28,24},{1,5},{5... | collective-permute-start | bytes 294920 | tf_op jit(solution)/shard_map/ppermute | solution.py:28
  14.8 2.8 %collective-permute-done.3.refs_8_ = bf16[128,384]{1,0:T(8,128)(2,1)S(1)} collective-permute-done((bf16[128,384]{1,0:T(8,128)(2,1)S(1)}, bf16[128,384]{1,0:T(8,128)(2,1)S(1)}, u32[]{:S(2)}, u32[]{:S(2)}) %collective-permute-start.3) | collective-permute-done | bytes 98336 | tf_op jit(solution)/shard_map/ppermute | solution.py:28
  17.6 1.5 %collective-permute-start.4 = (bf16[128,384]{1,0:T(8,128)(2,1)S(1)}, bf16[128,384]{1,0:T(8,128)(2,1)S(1)}, u32[]{:S(2)}, u32[]{:S(2)}) collective-permute-start(bf16[128,384]{1,0:T(8,128)(2,1)S(1)} %collective-permute-done.3.refs_8_), channel_id=1, source_target_pairs={{0,4},{4,0},{8,12},{12,8},{16,20},{20,16},{24,28},{28,24},{1,5},{5... | collective-permute-start | bytes 294920 | tf_op jit(solution)/shard_map/ppermute | solution.py:28
  19.4 2.7 %collective-permute-done.4.refs_9_ = bf16[128,384]{1,0:T(8,128)(2,1)S(1)} collective-permute-done((bf16[128,384]{1,0:T(8,128)(2,1)S(1)}, bf16[128,384]{1,0:T(8,128)(2,1)S(1)}, u32[]{:S(2)}, u32[]{:S(2)}) %collective-permute-start.4) | collective-permute-done | bytes 98336 | tf_op jit(solution)/shard_map/ppermute | solution.py:28
  22.2 10.4 %attend.1 = (bf16[48,512]{1,0:T(8,128)(2,1)S(1)}, bf16[48,512]{1,0:T(8,128)(2,1)S(1)}, bf16[48,512]{1,0:T(8,128)(2,1)S(1)}, bf16[48,512]{1,0:T(8,128)(2,1)S(1)},...) custom-call(s32[384,1]{1,0:T(8,128)S(1)} %broadcast_in_dim.45.refs_0, ...), custom_call_target="tpu_custom_call" | custom-call | flops 12000000000 | bytes 36000000 | tf_op jit(solution)/shard_map/attend/pallas_call | solution.py:215
  32.6 1.6 %collective-permute-start.7 = (bf16[48,512]{1,0:T(8,128)(2,1)S(1)}, bf16[48,512]{1,0:T(8,128)(2,1)S(1)}, u32[]{:S(2)}, u32[]{:S(2)}) collective-permute-start(bf16[48,512]{1,0:T(8,128)(2,1)S(1)} %get-tuple-element.40), channel_id=1, source_target_pairs={{0,4},{4,0},{8,12},{12,8},{16,20},{20,16},{24,28},{28,24},{1,5},{5... | collective-permute-start | bytes 147464 | tf_op jit(solution)/shard_map/ppermute | solution.py:28
  34.6 1.6 %collective-permute-start.9 = (bf16[48,512]{1,0:T(8,128)(2,1)S(1)}, bf16[48,512]{1,0:T(8,128)(2,1)S(1)}, u32[]{:S(2)}, u32[]{:S(2)}) collective-permute-start(bf16[48,512]{1,0:T(8,128)(2,1)S(1)} %get-tuple-element.42), channel_id=1, source_target_pairs={{0,12},{4,8},{8,4},{12,0},{16,28},{20,24},{24,20},{28,16},{1,13},{... | collective-permute-start | bytes 147464 | tf_op jit(solution)/shard_map/ppermute | solution.py:28
  36.2 2.0 %collective-permute-start.10 = (bf16[48,512]{1,0:T(8,128)(2,1)S(1)}, bf16[48,512]{1,0:T(8,128)(2,1)S(1)}, u32[]{:S(2)}, u32[]{:S(2)}) collective-permute-start(bf16[48,512]{1,0:T(8,128)(2,1)S(1)} %get-tuple-element.43), channel_id=1, source_target_pairs={{0,16},{4,20},{8,24},{12,28},{16,0},{20,4},{24,8},{28,12},{1,17},{... | collective-permute-start | bytes 147464 | tf_op jit(solution)/shard_map/ppermute | solution.py:28
  38.2 1.9 %collective-permute-start.11 = (bf16[48,512]{1,0:T(8,128)(2,1)S(1)}, bf16[48,512]{1,0:T(8,128)(2,1)S(1)}, u32[]{:S(2)}, u32[]{:S(2)}) collective-permute-start(bf16[48,512]{1,0:T(8,128)(2,1)S(1)} %get-tuple-element.44), channel_id=1, source_target_pairs={{0,20},{4,16},{8,28},{12,24},{16,4},{20,0},{24,12},{28,8},{1,21},{... | collective-permute-start | bytes 147464 | tf_op jit(solution)/shard_map/ppermute | solution.py:28
  40.1 2.5 %collective-permute-start.12 = (bf16[48,512]{1,0:T(8,128)(2,1)S(1)}, bf16[48,512]{1,0:T(8,128)(2,1)S(1)}, u32[]{:S(2)}, u32[]{:S(2)}) collective-permute-start(bf16[48,512]{1,0:T(8,128)(2,1)S(1)} %get-tuple-element.45), channel_id=1, source_target_pairs={{0,24},{4,28},{8,16},{12,20},{16,8},{20,12},{24,0},{28,4},{1,25},{... | collective-permute-start | bytes 147464 | tf_op jit(solution)/shard_map/ppermute | solution.py:28
  42.5 1.3 %collective-permute-start.13 = (bf16[48,512]{1,0:T(8,128)(2,1)S(1)}, bf16[48,512]{1,0:T(8,128)(2,1)S(1)}, u32[]{:S(2)}, u32[]{:S(2)}) collective-permute-start(bf16[48,512]{1,0:T(8,128)(2,1)S(1)} %get-tuple-element.46), channel_id=1, source_target_pairs={{0,28},{4,24},{8,20},{12,16},{16,12},{20,8},{24,4},{28,0},{1,29},{... | collective-permute-start | bytes 147464 | tf_op jit(solution)/shard_map/ppermute | solution.py:28
  44.3 1.7 %collective-permute-done.12.refs_11_ = bf16[48,512]{1,0:T(8,128)(2,1)S(1)} collective-permute-done((bf16[48,512]{1,0:T(8,128)(2,1)S(1)}, bf16[48,512]{1,0:T(8,128)(2,1)S(1)}, u32[]{:S(2)}, u32[]{:S(2)}) %collective-permute-start.12) | collective-permute-done | bytes 49184 | tf_op jit(solution)/shard_map/ppermute | solution.py:28
  46.0 3.3 %collective-permute-done.13.refs_12_ = bf16[48,512]{1,0:T(8,128)(2,1)S(1)} collective-permute-done((bf16[48,512]{1,0:T(8,128)(2,1)S(1)}, bf16[48,512]{1,0:T(8,128)(2,1)S(1)}, u32[]{:S(2)}, u32[]{:S(2)}) %collective-permute-start.13) | collective-permute-done | bytes 49184 | tf_op jit(solution)/shard_map/ppermute | solution.py:28
  49.3 1.4 %merge.1 = (bf16[32,1536]{1,0:T(8,128)(2,1)S(1)}, bf16[32,1536]{1,0:T(8,128)(2,1)S(1)}, bf16[32,1536]{1,0:T(8,128)(2,1)S(1)}, bf16[32,1536]{1,0:T(8,128)(2,1)S(1)}) custom-call(s32[1]{0:T(128)} %bitcast.refs_0_.kv_ref, bf16[128,384]{1,0:T(8,128)(2,1)S(1)} %get-tuple-element.35.refs_4_.refs_1_, bf16[128,128]{1,0:T(8,128)(2,1)S(1)} %get-tuple-element.37.refs_2_, ...), custom_call_target="tpu_custom_call" | custom-call | flops 12000000000 | bytes 36000000 | tf_op jit(solution)/shard_map/merge/pallas_call | solution.py:436
  50.9 1.6 %collective-permute-start.15 = (bf16[32,1536]{1,0:T(8,128)(2,1)S(1)}, bf16[32,1536]{1,0:T(8,128)(2,1)S(1)}, u32[]{:S(2)}, u32[]{:S(2)}) collective-permute-start(bf16[32,1536]{1,0:T(8,128)(2,1)S(1)} %get-tuple-element.49), channel_id=1, source_target_pairs={{0,2},{1,3},{2,0},{3,1},{4,6},{5,7},{6,4},{7,5},{8,10},{9,11},{10,... | collective-permute-start | bytes 294920 | tf_op jit(solution)/shard_map/ppermute | solution.py:28
  53.1 3.5 %collective-permute-done.15.refs_2_ = bf16[32,1536]{1,0:T(8,128)(2,1)S(1)} collective-permute-done((bf16[32,1536]{1,0:T(8,128)(2,1)S(1)}, bf16[32,1536]{1,0:T(8,128)(2,1)S(1)}, u32[]{:S(2)}, u32[]{:S(2)}) %collective-permute-start.15) | collective-permute-done | bytes 98336 | tf_op jit(solution)/shard_map/ppermute | solution.py:28
  58.3 1.4 %collective-permute-start.22 = (bf16[32,1664]{1,0:T(8,128)(2,1)S(1)}, bf16[32,1664]{1,0:T(8,128)(2,1)S(1)}, u32[]{:S(2)}, u32[]{:S(2)}) collective-permute-start(bf16[32,1664]{1,0:T(8,128)(2,1)S(1)} %get-tuple-element.52.refs_0_), channel_id=1, source_target_pairs={{0,24},{4,28},{8,16},{12,20},{16,8},{20,12},{24,0},{28,4},{1,25},{... | collective-permute-start | bytes 319496 | tf_op jit(solution)/shard_map/ppermute | solution.py:28
  59.7 3.0 %collective-permute-start.19 = (bf16[32,1664]{1,0:T(8,128)(2,1)S(1)}, bf16[32,1664]{1,0:T(8,128)(2,1)S(1)}, u32[]{:S(2)}, u32[]{:S(2)}) collective-permute-start(bf16[32,1664]{1,0:T(8,128)(2,1)S(1)} %get-tuple-element.52.refs_0_), channel_id=1, source_target_pairs={{0,12},{4,8},{8,4},{12,0},{16,28},{20,24},{24,20},{28,16},{1,13},{... | collective-permute-start | bytes 319496 | tf_op jit(solution)/shard_map/ppermute | solution.py:28
  62.7 1.5 %collective-permute-start.17 = (bf16[32,1664]{1,0:T(8,128)(2,1)S(1)}, bf16[32,1664]{1,0:T(8,128)(2,1)S(1)}, u32[]{:S(2)}, u32[]{:S(2)}) collective-permute-start(bf16[32,1664]{1,0:T(8,128)(2,1)S(1)} %get-tuple-element.52.refs_0_), channel_id=1, source_target_pairs={{0,4},{4,0},{8,12},{12,8},{16,20},{20,16},{24,28},{28,24},{1,5},{5... | collective-permute-start | bytes 319496 | tf_op jit(solution)/shard_map/ppermute | solution.py:28
  64.2 1.8 %collective-permute-done.22.refs_6_ = bf16[32,1664]{1,0:T(8,128)(2,1)S(1)} collective-permute-done((bf16[32,1664]{1,0:T(8,128)(2,1)S(1)}, bf16[32,1664]{1,0:T(8,128)(2,1)S(1)}, u32[]{:S(2)}, u32[]{:S(2)}) %collective-permute-start.22) | collective-permute-done | bytes 106528 | tf_op jit(solution)/shard_map/ppermute | solution.py:28
  66.5 3.4 %collective-permute-done.20.refs_4_ = bf16[32,1664]{1,0:T(8,128)(2,1)S(1)} collective-permute-done((bf16[32,1664]{1,0:T(8,128)(2,1)S(1)}, bf16[32,1664]{1,0:T(8,128)(2,1)S(1)}, u32[]{:S(2)}, u32[]{:S(2)}) %collective-permute-start.20) | collective-permute-done | bytes 106528 | tf_op jit(solution)/shard_map/ppermute | solution.py:28
  70.5 1.7 %collective-permute-done.18.refs_2_ = bf16[32,1664]{1,0:T(8,128)(2,1)S(1)} collective-permute-done((bf16[32,1664]{1,0:T(8,128)(2,1)S(1)}, bf16[32,1664]{1,0:T(8,128)(2,1)S(1)}, u32[]{:S(2)}, u32[]{:S(2)}) %collective-permute-start.18) | collective-permute-done | bytes 106528 | tf_op jit(solution)/shard_map/ppermute | solution.py:28
  72.2 2.6 %collective-permute-done.21.refs_5_ = bf16[32,1664]{1,0:T(8,128)(2,1)S(1)} collective-permute-done((bf16[32,1664]{1,0:T(8,128)(2,1)S(1)}, bf16[32,1664]{1,0:T(8,128)(2,1)S(1)}, u32[]{:S(2)}, u32[]{:S(2)}) %collective-permute-start.21) | collective-permute-done | bytes 106528 | tf_op jit(solution)/shard_map/ppermute | solution.py:28
  74.8 2.8 %copy-done.2 = bf16[2,1536,1024]{2,1,0:T(8,128)(2,1)S(1)} copy-done((bf16[2,1536,1024]{2,1,0:T(8,128)(2,1)S(1)}, bf16[2,1536,1024]{2,1,0:T(8,128)(2,1)}, u32[]{:S(2)}) %copy-start.2) | copy-done | bytes 6291480
  77.5 3.4 %experts.1 = (bf16[32,1536]{1,0:T(8,128)(2,1)S(1)}, bf16[32,1536]{1,0:T(8,128)(2,1)S(1)}, bf16[32,1536]{1,0:T(8,128)(2,1)S(1)}, bf16[32,1536]{1,0:T(8,128)(2,1)S...) custom-call(s32[1]{0:T(128)} %bitcast.1.req_ref, ...), custom_call_target="tpu_custom_call" | custom-call | flops 4000000000 | bytes 12000000 | tf_op jit(solution)/shard_map/experts/pallas_call | solution.py:463
  81.6 1.8 %collective-permute-start.24 = (bf16[32,1536]{1,0:T(8,128)(2,1)S(1)}, bf16[32,1536]{1,0:T(8,128)(2,1)S(1)}, u32[]{:S(2)}, u32[]{:S(2)}) collective-permute-start(bf16[32,1536]{1,0:T(8,128)(2,1)S(1)} %get-tuple-element.54), channel_id=1, source_target_pairs={{0,8},{4,12},{8,0},{12,4},{16,24},{20,28},{24,16},{28,20},{1,9},{5... | collective-permute-start | bytes 294920 | tf_op jit(solution)/shard_map/ppermute | solution.py:28
  85.1 1.5 %collective-permute-start.29 = (bf16[32,1536]{1,0:T(8,128)(2,1)S(1)}, bf16[32,1536]{1,0:T(8,128)(2,1)S(1)}, u32[]{:S(2)}, u32[]{:S(2)}) collective-permute-start(bf16[32,1536]{1,0:T(8,128)(2,1)S(1)} %get-tuple-element.60), channel_id=1, source_target_pairs={{0,4},{4,0},{8,12},{12,8},{16,20},{20,16},{24,28},{28,24},{1,5},{5... | collective-permute-start | bytes 294920 | tf_op jit(solution)/shard_map/ppermute | solution.py:28
  87.8 4.2 %collective-permute-done.29 = bf16[32,1536]{1,0:T(8,128)(2,1)S(1)} collective-permute-done((bf16[32,1536]{1,0:T(8,128)(2,1)S(1)}, bf16[32,1536]{1,0:T(8,128)(2,1)S(1)}, u32[]{:S(2)}, u32[]{:S(2)}) %collective-permute-start.29) | collective-permute-done | bytes 98336 | tf_op jit(solution)/shard_map/ppermute | solution.py:28
  93.8 4.8 %collective-permute-done.30 = bf16[32,1536]{1,0:T(8,128)(2,1)S(1)} collective-permute-done((bf16[32,1536]{1,0:T(8,128)(2,1)S(1)}, bf16[32,1536]{1,0:T(8,128)(2,1)S(1)}, u32[]{:S(2)}, u32[]{:S(2)}) %collective-permute-start.30) | collective-permute-done | bytes 98336 | tf_op jit(solution)/shard_map/ppermute | solution.py:28
  (96 shorter events, 16.0 us)
Async XLA Ops:
  4.1 9.2 %collective-permute-start.5 = (bf16[128,384]{1,0:T(8,128)(2,1)S(1)}, bf16[128,384]{1,0:T(8,128)(2,1)S(1)}, u32[]{:S(2)}, u32[]{:S(2)}) collective-permute-start(bf16[128,384]{1,0:T(8,128)(2,1)S(1)} %get-tuple-element.35.refs_4_.refs_1_), channel_id=1, source_target_pairs={{0,24},{4,28},{8,16},{12,20},{16,8},{20,12},{24,0},{28,4},{1,25},{... | collective-permute-start | bytes 294920 | tf_op jit(solution)/shard_map/ppermute | solution.py:28
  9.2 8.4 %collective-permute-start.3 = (bf16[128,384]{1,0:T(8,128)(2,1)S(1)}, bf16[128,384]{1,0:T(8,128)(2,1)S(1)}, u32[]{:S(2)}, u32[]{:S(2)}) collective-permute-start(bf16[128,384]{1,0:T(8,128)(2,1)S(1)} %get-tuple-element.35.refs_4_.refs_1_), channel_id=1, source_target_pairs={{0,16},{4,20},{8,24},{12,28},{16,0},{20,4},{24,8},{28,12},{1,17},{... | collective-permute-start | bytes 294920 | tf_op jit(solution)/shard_map/ppermute | solution.py:28
  9.2 10.2 %collective-permute-start.2 = (bf16[128,384]{1,0:T(8,128)(2,1)S(1)}, bf16[128,384]{1,0:T(8,128)(2,1)S(1)}, u32[]{:S(2)}, u32[]{:S(2)}) collective-permute-start(bf16[128,384]{1,0:T(8,128)(2,1)S(1)} %get-tuple-element.35.refs_4_.refs_1_), channel_id=1, source_target_pairs={{0,12},{4,8},{8,4},{12,0},{16,28},{20,24},{24,20},{28,16},{1,13},{... | collective-permute-start | bytes 294920 | tf_op jit(solution)/shard_map/ppermute | solution.py:28
  10.9 8.5 %collective-permute-start.1 = (bf16[128,384]{1,0:T(8,128)(2,1)S(1)}, bf16[128,384]{1,0:T(8,128)(2,1)S(1)}, u32[]{:S(2)}, u32[]{:S(2)}) collective-permute-start(bf16[128,384]{1,0:T(8,128)(2,1)S(1)} %get-tuple-element.35.refs_4_.refs_1_), channel_id=1, source_target_pairs={{0,8},{4,12},{8,0},{12,4},{16,24},{20,28},{24,16},{28,20},{1,9},{5... | collective-permute-start | bytes 294920 | tf_op jit(solution)/shard_map/ppermute | solution.py:28
  12.1 7.3 %collective-permute-start = (bf16[128,384]{1,0:T(8,128)(2,1)S(1)}, bf16[128,384]{1,0:T(8,128)(2,1)S(1)}, u32[]{:S(2)}, u32[]{:S(2)}) collective-permute-start(bf16[128,384]{1,0:T(8,128)(2,1)S(1)} %get-tuple-element.35.refs_4_.refs_1_), channel_id=1, source_target_pairs={{0,4},{4,0},{8,12},{12,8},{16,20},{20,16},{24,28},{28,24},{1,5},{5... | collective-permute-start | bytes 294920 | tf_op jit(solution)/shard_map/ppermute | solution.py:28
  13.2 6.2 %collective-permute-start.6 = (bf16[128,384]{1,0:T(8,128)(2,1)S(1)}, bf16[128,384]{1,0:T(8,128)(2,1)S(1)}, u32[]{:S(2)}, u32[]{:S(2)}) collective-permute-start(bf16[128,384]{1,0:T(8,128)(2,1)S(1)} %collective-permute-done.5.refs_10_), channel_id=1, source_target_pairs={{0,4},{4,0},{8,12},{12,8},{16,20},{20,16},{24,28},{28,24},{1,5},{5... | collective-permute-start | bytes 294920 | tf_op jit(solution)/shard_map/ppermute | solution.py:28
  17.6 4.6 %collective-permute-start.4 = (bf16[128,384]{1,0:T(8,128)(2,1)S(1)}, bf16[128,384]{1,0:T(8,128)(2,1)S(1)}, u32[]{:S(2)}, u32[]{:S(2)}) collective-permute-start(bf16[128,384]{1,0:T(8,128)(2,1)S(1)} %collective-permute-done.3.refs_8_), channel_id=1, source_target_pairs={{0,4},{4,0},{8,12},{12,8},{16,20},{20,16},{24,28},{28,24},{1,5},{5... | collective-permute-start | bytes 294920 | tf_op jit(solution)/shard_map/ppermute | solution.py:28
  22.2 21.6 %copy-start.6 = (bf16[128,1536]{1,0:T(8,128)(2,1)S(1)}, bf16[128,1536]{1,0:T(8,128)(2,1)}, u32[]{:S(2)}) copy-start(bf16[128,1536]{1,0:T(8,128)(2,1)} %key_weight_ref.1) | copy-start | bytes 1179652
  32.6 7.4 %collective-permute-start.7 = (bf16[48,512]{1,0:T(8,128)(2,1)S(1)}, bf16[48,512]{1,0:T(8,128)(2,1)S(1)}, u32[]{:S(2)}, u32[]{:S(2)}) collective-permute-start(bf16[48,512]{1,0:T(8,128)(2,1)S(1)} %get-tuple-element.40), channel_id=1, source_target_pairs={{0,4},{4,0},{8,12},{12,8},{16,20},{20,16},{24,28},{28,24},{1,5},{5... | collective-permute-start | bytes 147464 | tf_op jit(solution)/shard_map/ppermute | solution.py:28
  34.2 8.3 %collective-permute-start.8 = (bf16[48,512]{1,0:T(8,128)(2,1)S(1)}, bf16[48,512]{1,0:T(8,128)(2,1)S(1)}, u32[]{:S(2)}, u32[]{:S(2)}) collective-permute-start(bf16[48,512]{1,0:T(8,128)(2,1)S(1)} %get-tuple-element.41), channel_id=1, source_target_pairs={{0,8},{4,12},{8,0},{12,4},{16,24},{20,28},{24,16},{28,20},{1,9},{5... | collective-permute-start | bytes 147464 | tf_op jit(solution)/shard_map/ppermute | solution.py:28
  34.6 9.7 %collective-permute-start.9 = (bf16[48,512]{1,0:T(8,128)(2,1)S(1)}, bf16[48,512]{1,0:T(8,128)(2,1)S(1)}, u32[]{:S(2)}, u32[]{:S(2)}) collective-permute-start(bf16[48,512]{1,0:T(8,128)(2,1)S(1)} %get-tuple-element.42), channel_id=1, source_target_pairs={{0,12},{4,8},{8,4},{12,0},{16,28},{20,24},{24,20},{28,16},{1,13},{... | collective-permute-start | bytes 147464 | tf_op jit(solution)/shard_map/ppermute | solution.py:28
  36.2 8.1 %collective-permute-start.10 = (bf16[48,512]{1,0:T(8,128)(2,1)S(1)}, bf16[48,512]{1,0:T(8,128)(2,1)S(1)}, u32[]{:S(2)}, u32[]{:S(2)}) collective-permute-start(bf16[48,512]{1,0:T(8,128)(2,1)S(1)} %get-tuple-element.43), channel_id=1, source_target_pairs={{0,16},{4,20},{8,24},{12,28},{16,0},{20,4},{24,8},{28,12},{1,17},{... | collective-permute-start | bytes 147464 | tf_op jit(solution)/shard_map/ppermute | solution.py:28
  38.2 6.2 %collective-permute-start.11 = (bf16[48,512]{1,0:T(8,128)(2,1)S(1)}, bf16[48,512]{1,0:T(8,128)(2,1)S(1)}, u32[]{:S(2)}, u32[]{:S(2)}) collective-permute-start(bf16[48,512]{1,0:T(8,128)(2,1)S(1)} %get-tuple-element.44), channel_id=1, source_target_pairs={{0,20},{4,16},{8,28},{12,24},{16,4},{20,0},{24,12},{28,8},{1,21},{... | collective-permute-start | bytes 147464 | tf_op jit(solution)/shard_map/ppermute | solution.py:28
  40.1 5.9 %collective-permute-start.12 = (bf16[48,512]{1,0:T(8,128)(2,1)S(1)}, bf16[48,512]{1,0:T(8,128)(2,1)S(1)}, u32[]{:S(2)}, u32[]{:S(2)}) collective-permute-start(bf16[48,512]{1,0:T(8,128)(2,1)S(1)} %get-tuple-element.45), channel_id=1, source_target_pairs={{0,24},{4,28},{8,16},{12,20},{16,8},{20,12},{24,0},{28,4},{1,25},{... | collective-permute-start | bytes 147464 | tf_op jit(solution)/shard_map/ppermute | solution.py:28
  42.5 6.8 %collective-permute-start.13 = (bf16[48,512]{1,0:T(8,128)(2,1)S(1)}, bf16[48,512]{1,0:T(8,128)(2,1)S(1)}, u32[]{:S(2)}, u32[]{:S(2)}) collective-permute-start(bf16[48,512]{1,0:T(8,128)(2,1)S(1)} %get-tuple-element.46), channel_id=1, source_target_pairs={{0,28},{4,24},{8,20},{12,16},{16,12},{20,8},{24,4},{28,0},{1,29},{... | collective-permute-start | bytes 147464 | tf_op jit(solution)/shard_map/ppermute | solution.py:28
  50.8 2.3 %collective-permute-start.14 = (bf16[32,1536]{1,0:T(8,128)(2,1)S(1)}, bf16[32,1536]{1,0:T(8,128)(2,1)S(1)}, u32[]{:S(2)}, u32[]{:S(2)}) collective-permute-start(bf16[32,1536]{1,0:T(8,128)(2,1)S(1)} %get-tuple-element.48), channel_id=1, source_target_pairs={{0,1},{1,0},{2,3},{3,2},{4,5},{5,4},{6,7},{7,6},{8,9},{9,8},{10,11... | collective-permute-start | bytes 294920 | tf_op jit(solution)/shard_map/ppermute | solution.py:28
  50.9 5.7 %collective-permute-start.15 = (bf16[32,1536]{1,0:T(8,128)(2,1)S(1)}, bf16[32,1536]{1,0:T(8,128)(2,1)S(1)}, u32[]{:S(2)}, u32[]{:S(2)}) collective-permute-start(bf16[32,1536]{1,0:T(8,128)(2,1)S(1)} %get-tuple-element.49), channel_id=1, source_target_pairs={{0,2},{1,3},{2,0},{3,1},{4,6},{5,7},{6,4},{7,5},{8,10},{9,11},{10,... | collective-permute-start | bytes 294920 | tf_op jit(solution)/shard_map/ppermute | solution.py:28
  52.4 5.3 %collective-permute-start.16 = (bf16[32,1536]{1,0:T(8,128)(2,1)S(1)}, bf16[32,1536]{1,0:T(8,128)(2,1)S(1)}, u32[]{:S(2)}, u32[]{:S(2)}) collective-permute-start(bf16[32,1536]{1,0:T(8,128)(2,1)S(1)} %get-tuple-element.50), channel_id=1, source_target_pairs={{0,3},{1,2},{2,1},{3,0},{4,7},{5,6},{6,5},{7,4},{8,11},{9,10},{10,... | collective-permute-start | bytes 294920 | tf_op jit(solution)/shard_map/ppermute | solution.py:28
  58.3 7.7 %collective-permute-start.22 = (bf16[32,1664]{1,0:T(8,128)(2,1)S(1)}, bf16[32,1664]{1,0:T(8,128)(2,1)S(1)}, u32[]{:S(2)}, u32[]{:S(2)}) collective-permute-start(bf16[32,1664]{1,0:T(8,128)(2,1)S(1)} %get-tuple-element.52.refs_0_), channel_id=1, source_target_pairs={{0,24},{4,28},{8,16},{12,20},{16,8},{20,12},{24,0},{28,4},{1,25},{... | collective-permute-start | bytes 319496 | tf_op jit(solution)/shard_map/ppermute | solution.py:28
  59.7 10.2 %collective-permute-start.20 = (bf16[32,1664]{1,0:T(8,128)(2,1)S(1)}, bf16[32,1664]{1,0:T(8,128)(2,1)S(1)}, u32[]{:S(2)}, u32[]{:S(2)}) collective-permute-start(bf16[32,1664]{1,0:T(8,128)(2,1)S(1)} %get-tuple-element.52.refs_0_), channel_id=1, source_target_pairs={{0,16},{4,20},{8,24},{12,28},{16,0},{20,4},{24,8},{28,12},{1,17},{... | collective-permute-start | bytes 319496 | tf_op jit(solution)/shard_map/ppermute | solution.py:28
  59.7 10.8 %collective-permute-start.19 = (bf16[32,1664]{1,0:T(8,128)(2,1)S(1)}, bf16[32,1664]{1,0:T(8,128)(2,1)S(1)}, u32[]{:S(2)}, u32[]{:S(2)}) collective-permute-start(bf16[32,1664]{1,0:T(8,128)(2,1)S(1)} %get-tuple-element.52.refs_0_), channel_id=1, source_target_pairs={{0,12},{4,8},{8,4},{12,0},{16,28},{20,24},{24,20},{28,16},{1,13},{... | collective-permute-start | bytes 319496 | tf_op jit(solution)/shard_map/ppermute | solution.py:28
  62.7 9.5 %collective-permute-start.18 = (bf16[32,1664]{1,0:T(8,128)(2,1)S(1)}, bf16[32,1664]{1,0:T(8,128)(2,1)S(1)}, u32[]{:S(2)}, u32[]{:S(2)}) collective-permute-start(bf16[32,1664]{1,0:T(8,128)(2,1)S(1)} %get-tuple-element.52.refs_0_), channel_id=1, source_target_pairs={{0,8},{4,12},{8,0},{12,4},{16,24},{20,28},{24,16},{28,20},{1,9},{5... | collective-permute-start | bytes 319496 | tf_op jit(solution)/shard_map/ppermute | solution.py:28
  62.7 9.5 %collective-permute-start.17 = (bf16[32,1664]{1,0:T(8,128)(2,1)S(1)}, bf16[32,1664]{1,0:T(8,128)(2,1)S(1)}, u32[]{:S(2)}, u32[]{:S(2)}) collective-permute-start(bf16[32,1664]{1,0:T(8,128)(2,1)S(1)} %get-tuple-element.52.refs_0_), channel_id=1, source_target_pairs={{0,4},{4,0},{8,12},{12,8},{16,20},{20,16},{24,28},{28,24},{1,5},{5... | collective-permute-start | bytes 319496 | tf_op jit(solution)/shard_map/ppermute | solution.py:28
  66.0 6.2 %collective-permute-start.23 = (bf16[32,1664]{1,0:T(8,128)(2,1)S(1)}, bf16[32,1664]{1,0:T(8,128)(2,1)S(1)}, u32[]{:S(2)}, u32[]{:S(2)}) collective-permute-start(bf16[32,1664]{1,0:T(8,128)(2,1)S(1)} %collective-permute-done.22.refs_6_), channel_id=1, source_target_pairs={{0,4},{4,0},{8,12},{12,8},{16,20},{20,16},{24,28},{28,24},{1,5},{5... | collective-permute-start | bytes 319496 | tf_op jit(solution)/shard_map/ppermute | solution.py:28
  69.9 4.8 %collective-permute-start.21 = (bf16[32,1664]{1,0:T(8,128)(2,1)S(1)}, bf16[32,1664]{1,0:T(8,128)(2,1)S(1)}, u32[]{:S(2)}, u32[]{:S(2)}) collective-permute-start(bf16[32,1664]{1,0:T(8,128)(2,1)S(1)} %collective-permute-done.20.refs_4_), channel_id=1, source_target_pairs={{0,4},{4,0},{8,12},{12,8},{16,20},{20,16},{24,28},{28,24},{1,5},{5... | collective-permute-start | bytes 319496 | tf_op jit(solution)/shard_map/ppermute | solution.py:28
  81.0 6.7 %collective-permute-start.27 = (bf16[32,1536]{1,0:T(8,128)(2,1)S(1)}, bf16[32,1536]{1,0:T(8,128)(2,1)S(1)}, u32[]{:S(2)}, u32[]{:S(2)}) collective-permute-start(bf16[32,1536]{1,0:T(8,128)(2,1)S(1)} %get-tuple-element.58), channel_id=1, source_target_pairs={{0,4},{4,0},{8,12},{12,8},{16,20},{20,16},{24,28},{28,24},{1,5},{5... | collective-permute-start | bytes 294920 | tf_op jit(solution)/shard_map/ppermute | solution.py:28
  81.6 11.2 %collective-permute-start.24 = (bf16[32,1536]{1,0:T(8,128)(2,1)S(1)}, bf16[32,1536]{1,0:T(8,128)(2,1)S(1)}, u32[]{:S(2)}, u32[]{:S(2)}) collective-permute-start(bf16[32,1536]{1,0:T(8,128)(2,1)S(1)} %get-tuple-element.54), channel_id=1, source_target_pairs={{0,8},{4,12},{8,0},{12,4},{16,24},{20,28},{24,16},{28,20},{1,9},{5... | collective-permute-start | bytes 294920 | tf_op jit(solution)/shard_map/ppermute | solution.py:28
  83.4 9.4 %collective-permute-start.25 = (bf16[32,1536]{1,0:T(8,128)(2,1)S(1)}, bf16[32,1536]{1,0:T(8,128)(2,1)S(1)}, u32[]{:S(2)}, u32[]{:S(2)}) collective-permute-start(bf16[32,1536]{1,0:T(8,128)(2,1)S(1)} %get-tuple-element.55), channel_id=1, source_target_pairs={{0,4},{4,0},{8,12},{12,8},{16,20},{20,16},{24,28},{28,24},{1,5},{5... | collective-permute-start | bytes 294920 | tf_op jit(solution)/shard_map/ppermute | solution.py:28
  83.9 8.9 %collective-permute-start.26 = (bf16[32,1536]{1,0:T(8,128)(2,1)S(1)}, bf16[32,1536]{1,0:T(8,128)(2,1)S(1)}, u32[]{:S(2)}, u32[]{:S(2)}) collective-permute-start(bf16[32,1536]{1,0:T(8,128)(2,1)S(1)} %get-tuple-element.56), channel_id=1, source_target_pairs={{0,12},{4,8},{8,4},{12,0},{16,28},{20,24},{24,20},{28,16},{1,13},{... | collective-permute-start | bytes 294920 | tf_op jit(solution)/shard_map/ppermute | solution.py:28
  85.1 6.9 %collective-permute-start.29 = (bf16[32,1536]{1,0:T(8,128)(2,1)S(1)}, bf16[32,1536]{1,0:T(8,128)(2,1)S(1)}, u32[]{:S(2)}, u32[]{:S(2)}) collective-permute-start(bf16[32,1536]{1,0:T(8,128)(2,1)S(1)} %get-tuple-element.60), channel_id=1, source_target_pairs={{0,4},{4,0},{8,12},{12,8},{16,20},{20,16},{24,28},{28,24},{1,5},{5... | collective-permute-start | bytes 294920 | tf_op jit(solution)/shard_map/ppermute | solution.py:28
  87.8 6.0 %collective-permute-start.28 = (bf16[32,1536]{1,0:T(8,128)(2,1)S(1)}, bf16[32,1536]{1,0:T(8,128)(2,1)S(1)}, u32[]{:S(2)}, u32[]{:S(2)}) collective-permute-start(bf16[32,1536]{1,0:T(8,128)(2,1)S(1)} %add_convert_fusion.2), channel_id=1, source_target_pairs={{0,16},{4,20},{8,24},{12,28},{16,0},{20,4},{24,8},{28,12},{1,17},{... | collective-permute-start | bytes 294920 | tf_op jit(solution)/shard_map/ppermute | solution.py:28
  92.0 6.5 %collective-permute-start.30 = (bf16[32,1536]{1,0:T(8,128)(2,1)S(1)}, bf16[32,1536]{1,0:T(8,128)(2,1)S(1)}, u32[]{:S(2)}, u32[]{:S(2)}) collective-permute-start(bf16[32,1536]{1,0:T(8,128)(2,1)S(1)} %add_convert_fusion.1), channel_id=1, source_target_pairs={{0,24},{4,28},{8,16},{12,20},{16,8},{20,12},{24,0},{28,4},{1,25},{... | collective-permute-start | bytes 294920 | tf_op jit(solution)/shard_map/ppermute | solution.py:28
  (19 other events, 197.8 us)

commit v3 on v2

--- a/solution.py
+++ b/solution.py
@@ -1,8 +1,8 @@
 import functools
+import math
 
 import jax
 import jax.numpy as jnp
-import numpy as np
 from jax import lax
 from jax.experimental import pallas as pl
 from jax.experimental.pallas import tpu as pltpu
@@ -13,7 +13,11 @@
 BLK = 128
 PAGES = 3
 CHUNK = 96
-COSTS = (12.0, 3.0, 12.0, 12.0, 12.0, 4.0, 12.0)
+QLIM = 60
+ALIM = 24
+SLIM = 1
+STAGE = True
+COSTS = (12.0, 1.0, 12.0, 12.0, 12.0, 4.0, 12.0)
 NEG = -1e30
 BF = jnp.bfloat16
 F32 = jnp.float32
@@ -47,17 +51,24 @@
         for distance in (start, start + 1):
             if distance:
                 held[distance] = swap(values[distance], axis, distance)
-    return [held[distance] for distance in range(size)]
+    return [held[distance] for distance in sorted(held, key=lambda distance: -distance)]
 
 
 def sum_rows(values, axis):
     size = lax.axis_size(axis)
     far = size // 2
-    beside = {distance: swap(values[distance], axis, 1) for distance in range(far + 1, size, 2)}
-    arrived = [swap(values[distance], axis, distance) for distance in list(range(2, far, 2)) + list(range(1, far, 2))]
-    for distance in range(far, size, 2):
-        joined = values[distance].astype(F32) + beside[distance + 1].astype(F32)
-        arrived.append(swap(joined.astype(BF), axis, distance))
+    split = far + far // 2
+    beside = {distance: swap(values[distance], axis, 1) for distance in range(split + 1, size, 2)}
+    arrived = [swap(values[distance], axis, distance) for distance in range(far, split)]
+    arrived += [swap(values[distance], axis, distance) for distance in range(2, far, 2)]
+    joined = {}
+    for distance in range(split, size, 2):
+        both = values[distance].astype(F32) + beside[distance + 1].astype(F32)
+        joined[distance] = both.astype(BF)
+    odd = {distance: values[distance] for distance in range(1, far, 2)}
+    joined, odd = lax.optimization_barrier((joined, odd))
+    arrived += [swap(value, axis, distance) for distance, value in joined.items()]
+    arrived += [swap(value, axis, distance) for distance, value in odd.items()]
     total = values[0].astype(F32)
     for value in arrived:
         total = total + value.astype(F32)
@@ -90,23 +101,60 @@
     return pieces[0] if len(pieces) == 1 else jnp.concatenate(pieces, 1)
 
 
-def table_kernel(req_ref, length_ref, frequency_ref, cosines_ref, sines_ref):
-    rows, width = cosines_ref.shape
+def query_kernel(req_ref, hidden_hbm, gain_hbm, weight_hbm, length_hbm, query_ref, normed_ref, cosines_ref,
+                 sines_ref, hidden_ref, gain_ref, weight_ref, length_ref, sem):
+    copies = [
+        pltpu.make_async_copy(source, target, sem.at[place])
+        for place, (source, target) in enumerate(
+            [(length_hbm, length_ref), (hidden_hbm, hidden_ref), (weight_hbm, weight_ref), (gain_hbm, gain_ref)]
+        )
+    ]
+    for copy in copies:
+        copy.start()
+    rows = cosines_ref.shape[0]
+    copies[0].wait()
     lengths = jnp.broadcast_to(length_ref[pl.ds(req_ref[0], 1), :].astype(F32), (rows, rows))
     lengths = jnp.where(iota((rows, rows), 0) == iota((rows, rows), 1), lengths, 0.0)
-    angles = jnp.sum(lengths, -1, keepdims=True) * frequency_ref[...]
-    cosines_ref[...] = jnp.cos(angles)
+    exponent = (iota((1, 2 * HD), 1) % (HD // 2)).astype(F32) * (-2.0 / HD)
+    angles = jnp.sum(lengths, -1, keepdims=True) * jnp.exp(exponent * math.log(10000.0))
+    cosines = jnp.cos(angles)
     sines = jnp.sin(angles)
-    sines_ref[...] = jnp.where(iota((rows, width), 1) % HD < HD // 2, -sines, sines)
-
-
-def query_kernel(hidden_ref, gain_ref, weight_ref, cosines_ref, sines_ref, query_ref, normed_ref):
+    sines = jnp.where(iota((1, 2 * HD), 1) % HD < HD // 2, -sines, sines)
+    cosines_ref[...] = cosines
+    sines_ref[...] = sines
+    copies[1].wait()
     hidden = hidden_ref[...].astype(F32)
     scale = lax.rsqrt(jnp.mean(hidden * hidden, -1, keepdims=True) + 1e-05)
-    normed = (hidden * scale * gain_ref[...]).astype(BF)
+    copies[3].wait()
+    normed = (hidden * scale * lanes_of(gain_ref)).astype(BF)
     normed_ref[...] = normed
+    copies[2].wait()
     query = project_rows(normed, weight_ref[...])
-    query_ref[...] = (rotate(query, cosines_ref[...], sines_ref[...]) * 0.125).astype(BF)
+    query_ref[...] = (rotate(query, cosines, sines) * 0.125).astype(BF)
+
+
+def place_kernel(rows, share, req_ref, block_ref, length_ref, query_ref, left_ref, slot_ref, local_ref):
+    blocks = block_ref.shape[1]
+    here = iota((blocks, blocks), 0)
+    there = iota((blocks, blocks), 1)
+    by_lane = block_ref[...]
+    by_row = jnp.sum(jnp.where(here == there, by_lane, 0), 1, keepdims=True)
+    owner = by_row // PAGES
+    home = owner // rows
+    local_ref[...] = owner % rows
+    query_ref[...] = jnp.bitwise_xor(home, req_ref[0]) * rows + owner % rows
+    lengths = lanes_of(length_ref)
+    owned = owner == iota((blocks, lengths.shape[1]), 1)
+    left = jnp.sum(jnp.where(owned, lengths, 0), 1, keepdims=True) - (by_row - owner * PAGES) * BLK
+    left_ref[...] = jnp.sum(jnp.where(here == there, left, 0), 0, keepdims=True)
+    lane_home = by_lane // PAGES // rows
+    earlier = jnp.logical_and(home == lane_home, here < there)
+    rank = jnp.sum(earlier.astype(jnp.int32), 0, keepdims=True)
+    slot_ref[...] = jnp.bitwise_xor(lane_home, req_ref[0]) * share + rank
+
+
+def lanes_of(ref):
+    return jnp.concatenate([ref[row : row + 1, :] for row in range(ref.shape[0])], 1)
 
 
 def fresh_kernel(normed_ref, key_weight_ref, value_weight_ref, cosines_ref, sines_ref, key_ref, value_ref):
@@ -154,7 +202,7 @@
                 first, second = (turned, tile) if odd else (tile, turned)
                 laid_ref[pl.ds(head, chunk, 16), :] = jnp.where(low, first, 0.0)
                 laid_ref[pl.ds(head + 8, chunk, 16), :] = jnp.where(low, 0.0, second)
-    query = laid_ref[...].astype(BF)
+    query = laid_ref[: chunk * 16, :].astype(BF)
     scores = lax.dot_general(
         query.reshape(chunk // 2, 32, 2 * HD), key_ref[...].reshape(chunk // 2, 2 * lanes, 2 * HD),
         (((2,), (2,)), ((0,), (0,))), preferred_element_type=F32)
@@ -162,11 +210,10 @@
     cell_row = iota((8, lanes), 0)
     cell_lane = iota((8, lanes), 1)
     position = jnp.where(cell_lane % groups == cell_row // per_group, 2 * (cell_lane // groups), 1 << 20)
-    position = position.astype(F32)[None]
-    spread = (iota((chunk * 8, chunk), 0) // 8 == iota((chunk * 8, chunk), 1)).astype(BF)
-    remaining = jnp.broadcast_to(left_ref[...].astype(F32), (chunk, lanes)).astype(BF)
-    remaining = dot(spread, remaining).reshape(chunk, 8, lanes)
-    usable = jnp.concatenate([position < remaining, position + 1.0 < remaining], 1)
+    position = position[None]
+    remaining = [jnp.full((1, 8, lanes), left_ref[0, base + place], jnp.int32) for place in range(chunk)]
+    remaining = jnp.concatenate(remaining, 0)
+    usable = jnp.concatenate([position < remaining, position + 1 < remaining], 1)
     scores = jnp.where(usable, scores, NEG)
     highest = jnp.max(jnp.maximum(scores[:, :8], scores[:, 8:]), -1, keepdims=True)
     weights = jnp.where(usable, jnp.exp(scores - jnp.concatenate([highest, highest], 1)), 0.0)
@@ -182,8 +229,8 @@
     highest = highest.reshape(chunk * 8, 1)
     some = total > 0.0
     safe = jnp.where(some, total, 1.0)
-    mean_ref[...] = numer / safe
-    level_ref[...] = jnp.broadcast_to(jnp.where(some, highest + jnp.log(safe), NEG), (chunk * 8, 2 * HD))
+    mean_ref[: chunk * 8, :] = numer / safe
+    level_ref[: chunk * 8, :] = jnp.broadcast_to(jnp.where(some, highest + jnp.log(safe), NEG), (chunk * 8, 2 * HD))
     lane = iota((chunk, 2 * HD), 1)
     means = [mean_ref[pl.ds(head, chunk, 8), :] for head in range(heads)]
     extras = jnp.zeros((chunk, 2 * HD), F32)
@@ -208,7 +255,7 @@
         for place, out_ref in enumerate(out_refs):
             out_ref[...] = sorted_rows[place * share : (place + 1) * share].astype(BF)
 
-def attend(heads, groups, chunk, width, qrow, left, slot, local, queries, keys, values, limit=24):
+def attend(heads, groups, chunk, width, qrow, left, slot, local, queries, keys, values, limit=ALIM):
     blocks, lanes = keys.shape[:2]
     whole = pl.BlockSpec(memory_space=pltpu.VMEM)
     block = lambda *shape: pl.BlockSpec(shape, lambda i: (i,) + (0,) * (len(shape) - 1))
@@ -216,14 +263,14 @@
         functools.partial(attend_kernel, heads, groups, chunk, len(queries)),
         grid=(blocks // chunk,),
         out_shape=[jax.ShapeDtypeStruct((blocks // len(queries), width), BF)] * len(queries),
-        in_specs=[whole, block(chunk, 1), whole, block(chunk, 1)] + [whole] * len(queries)
+        in_specs=[whole, pl.BlockSpec(memory_space=pltpu.SMEM), whole, block(chunk, 1)] + [whole] * len(queries)
         + [block(chunk, lanes, 2 * HD)] * 2,
         out_specs=[whole] * len(queries),
         scratch_shapes=[
             pltpu.VMEM((blocks, heads * HD), F32),
-            pltpu.VMEM((chunk * 16, 2 * HD), F32),
-            pltpu.VMEM((chunk * 8, 2 * HD), F32),
-            pltpu.VMEM((chunk * 8, 2 * HD), F32),
+            pltpu.VMEM((chunk * 16 + 16, 2 * HD), F32),
+            pltpu.VMEM((chunk * 8 + 8, 2 * HD), F32),
+            pltpu.VMEM((chunk * 8 + 8, 2 * HD), F32),
             pltpu.VMEM((blocks, width), BF),
         ],
         compiler_params=pltpu.CompilerParams(vmem_limit_bytes=limit << 20),
@@ -290,7 +337,7 @@
     after = hidden_ref[pl.ds(start, count), :].astype(F32) + total
     after_ref[...] = after
     scale = lax.rsqrt(jnp.mean(after * after, -1, keepdims=True) + 1e-05)
-    normed = (after * scale * gain_ref[...]).astype(BF)
+    normed = (after * scale * lanes_of(gain_ref)).astype(BF)
     out_ref[:, :model] = normed
     experts = router_ref.shape[1]
     logits = dot(normed, router_ref[...])
@@ -304,6 +351,12 @@
     high = gates.astype(BF).astype(F32)
     spare = jnp.zeros((count, 128 - 2 * experts), F32)
     out_ref[:, model:] = jnp.concatenate([high, gates - high, spare], 1).astype(BF)
+
+
+def stage_kernel(order_ref, source_ref, target_ref, sem):
+    copy = pltpu.make_async_copy(source_ref, target_ref, sem)
+    copy.start()
+    copy.wait()
 
 
 def expert_kernel(sources, experts, req_ref, *refs):
@@ -375,28 +428,28 @@
     vmem = pl.BlockSpec(memory_space=pltpu.VMEM)
     scalar = pl.BlockSpec(memory_space=pltpu.SMEM)
     req_scalar = jnp.reshape(req_index, (1,)).astype(jnp.int32)
-    frequency = 10000.0 ** (-(np.arange(2 * HD) % (HD // 2)) / (HD // 2))
-    cosines, sines = pl.pallas_call(
-        table_kernel,
-        out_shape=[jax.ShapeDtypeStruct((row_count, 2 * HD), F32)] * 2,
-        in_specs=[scalar, vmem, vmem],
-        out_specs=[vmem] * 2,
-        compiler_params=pltpu.CompilerParams(vmem_limit_bytes=4 << 20),
-        cost_estimate=cost(COSTS[6]),
-        name="tables",
-    )(req_scalar, cache_len.reshape(sources, row_count), jnp.asarray(frequency[None, :], F32))
-    query, normed = pl.pallas_call(
+    far = pl.BlockSpec(memory_space=pltpu.HBM)
+    query, normed, cosines, sines = pl.pallas_call(
         query_kernel,
         out_shape=[
             jax.ShapeDtypeStruct((row_count, heads * HD), BF),
             jax.ShapeDtypeStruct((row_count, model), BF),
-        ],
-        in_specs=[vmem] * 5,
-        out_specs=[vmem] * 2,
+            jax.ShapeDtypeStruct((row_count, 2 * HD), F32),
+            jax.ShapeDtypeStruct((row_count, 2 * HD), F32),
+        ],
+        in_specs=[scalar] + [far] * 4,
+        out_specs=[vmem] * 4,
+        scratch_shapes=[
+            pltpu.VMEM((row_count, model), BF),
+            pltpu.VMEM((model // 128, 128), F32),
+            pltpu.VMEM(w_query.shape, BF),
+            pltpu.VMEM((sources, row_count), jnp.int32),
+            pltpu.SemaphoreType.DMA((4,)),
+        ],
         cost_estimate=cost(COSTS[0]),
-        compiler_params=pltpu.CompilerParams(vmem_limit_bytes=8 << 20),
+        compiler_params=pltpu.CompilerParams(vmem_limit_bytes=QLIM << 20),
         name="query",
-    )(hidden_in, attn_gain[None, :], w_query, cosines, sines)
+    )(req_scalar, hidden_in, attn_gain.reshape(-1, 128), w_query, cache_len.reshape(sources, row_count))
     key_new, value_new = pl.pallas_call(
         fresh_kernel,
         out_shape=[jax.ShapeDtypeStruct((row_count, groups * HD), BF)] * 2,
@@ -408,26 +461,27 @@
     )(normed, w_key, w_value, cosines, sines)
     queries = gather_rows(query, "req")
 
-    owners = block_slot // PAGES
-    home = owners // row_count
-    local = owners % row_count
-    owned = owners[:, None] == jnp.arange(requests, dtype=jnp.int32)[None, :]
-    lengths = jnp.sum(jnp.where(owned, cache_len[None, :], 0), 1)
-    left = lengths - (block_slot % PAGES) * BLK
-    left = jnp.clip(left, 0, BLK)
-    number = jnp.arange(blocks, dtype=jnp.int32)
-    earlier = jnp.logical_and(home[:, None] == home[None, :], number[:, None] < number[None, :])
-    rank = jnp.sum(earlier.astype(jnp.int32), 0)
-    place = jnp.bitwise_xor(home, req_index)
-    slot = place * share + rank
-    query_row = place * row_count + local
+    query_row, left, slot, local = pl.pallas_call(
+        functools.partial(place_kernel, row_count, share),
+        out_shape=[
+            jax.ShapeDtypeStruct((blocks, 1), jnp.int32),
+            jax.ShapeDtypeStruct((1, blocks), jnp.int32),
+            jax.ShapeDtypeStruct((1, blocks), jnp.int32),
+            jax.ShapeDtypeStruct((blocks, 1), jnp.int32),
+        ],
+        in_specs=[scalar, vmem, vmem],
+        out_specs=[vmem] * 4,
+        cost_estimate=cost(COSTS[6]),
+        compiler_params=pltpu.CompilerParams(vmem_limit_bytes=8 << 20),
+        name="places",
+    )(req_scalar, block_slot[None, :], cache_len.reshape(sources, row_count))
 
     def pairs(cache):
         cache = cache.reshape(blocks, groups, HD, 2 * HD).transpose(0, 2, 1, 3)
         return cache.reshape(blocks, HD * groups, 2 * HD)
 
     partial = attend(
-        heads, groups, CHUNK, width, query_row[:, None], left[:, None], slot[None, :], local[:, None],
+        heads, groups, CHUNK, width, query_row, left, slot, local,
         queries, pairs(k_cache), pairs(v_cache),
     )
     parts = send_rows(partial, "req")
@@ -457,9 +511,20 @@
         compiler_params=pltpu.CompilerParams(vmem_limit_bytes=10 << 20),
         cost_estimate=cost(COSTS[4]),
         name="route",
-    )(kv_scalar, hidden_in, moe_gain[None, :], w_router, routes, *pieces)
+    )(kv_scalar, hidden_in, moe_gain.reshape(-1, 128), w_router, routes, *pieces)
     arrived = gather_rows(outgoing, "req")
     local_experts = w_gate_up.shape[0]
+    if STAGE:
+        w_gate_up = pl.pallas_call(
+            stage_kernel,
+            out_shape=jax.ShapeDtypeStruct(w_gate_up.shape, BF),
+            in_specs=[pl.BlockSpec(memory_space=pl.ANY), far],
+            out_specs=pl.BlockSpec(memory_space=pl.ANY),
+            scratch_shapes=[pltpu.SemaphoreType.DMA],
+            cost_estimate=cost(2.0),
+            compiler_params=pltpu.CompilerParams(vmem_limit_bytes=SLIM << 20),
+            name="stage",
+        )(outgoing, w_gate_up)
     mixed = pl.pallas_call(
         functools.partial(expert_kernel, sources, w_router.shape[1]),
         grid=(local_experts,),

time: 99.5 us -> 92.1 us (0.926)
  waiting for transfers between devices: 35.7 us -> 26.5 us
  local copies, waits for them, and re-layouts: 6.51 us -> 3.18 us
  starting transfers between devices: 38.2 us -> 41.5 us
  Pallas kernels: 17.2 us -> 19.6 us
    ppermute x31, waiting for transfers between devices: 35.7 us -> 26.5 us  [swap(): lax.ppermute(value, axis, [(source, source ^ distance) for source in rang...]
    ppermute x31, starting transfers between devices: 38.2 us -> 41.5 us  [swap(): lax.ppermute(value, axis, [(source, source ^ distance) for source in rang...]
    unnamed x42 -> x44, local copies, waits for them, and re-layouts: 5.48 us -> 3.18 us
    pallas_call x1, Pallas kernels: 0.66 us -> 2.73 us  [shards(): pl.pallas_call(query_kernel, out_shape=[jax.ShapeDtypeStruct((row_count,...]
    broadcast_in_dim x6 -> x1, local copies, waits for them, and re-layouts: 1.04 us -> 0.01 us  [shards(): block_slot[None, :]]
  transfers between devices with their start and end apart: 31 -> 31, of which waited for: 14 -> 14; matrix products, arithmetic and copies ran while one was open for 1% -> 0% of each run, Pallas kernels for 0% -> 2%
where the time goes in v3:
time: 92.1 us; the launch traced here: 91.9 us
  starting transfers between devices  41.5 us (45%)
  waiting for transfers between devices  26.5 us (29%)
  Pallas kernels  19.6 us (21%)
  local copies, waits for them, and re-layouts  3.18 us (3%)
    ppermute x31, starting transfers between devices, swap(): lax.ppermute(value, axis, [(source, source ^ distance) for source in rang...  41.5 us
    ppermute x31, waiting for transfers between devices, swap(): lax.ppermute(value, axis, [(source, source ^ distance) for source in rang...  26.5 us
    pallas_call x1, Pallas kernels, attend(): pl.pallas_call(functools.partial(attend_kernel, heads, groups, chunk, len...  9.71 us
    pallas_call x1, Pallas kernels, shards(): pl.pallas_call(functools.partial(expert_kernel, sources, w_router.shape[1...  3.45 us
    unnamed x44, local copies, waits for them, and re-layouts  3.18 us
    pallas_call x1, Pallas kernels, shards(): pl.pallas_call(query_kernel, out_shape=[jax.ShapeDtypeStruct((row_count,...  2.73 us
  transfers between devices with their start and end apart: 31, of which 14 were waited for; matrix products, arithmetic and copies ran while one was open for 0% of the time, Pallas kernels for 2%

profile of v3, /device:TPU:0, one launch (start us, length us, event | category | flops | bytes accessed | tf_op | source)
XLA Modules:
  0.0 91.9 jit_solution(17901742860133922136)
XLA Ops:
  0.0 2.7 %query.1 = (bf16[128,384]{1,0:T(8,128)(2,1)}, bf16[128,1536]{1,0:T(8,128)(2,1)}, f32[128,128]{1,0:T(8,128)}, f32[128,128]{1,0:T(8,128)}) custom-call(s32[1]{0:T(128)} %bitcast.2.req_ref, bf16[128,1536]{1,0:T(8,128)(2,1)} %hidden_ref.1, f32[12,128]{1,0:T(8,128)} %bitcast.24, bf16[384,1536]{1,0:T(8,128)(2,1)} %weight_hbm.1, s32[8,128]{1,0:T(8,128)} %bitcast.22), custom_call_target="tpu_custom_call" | custom-call | flops 12000000000 | bytes 36000000 | tf_op jit(solution)/shard_map/query/pallas_call | solution.py:432
  2.7 5.1 %collective-permute-start.5 = (bf16[128,384]{1,0:T(8,128)(2,1)}, bf16[128,384]{1,0:T(8,128)(2,1)S(1)}, u32[]{:S(2)}, u32[]{:S(2)}) collective-permute-start(bf16[128,384]{1,0:T(8,128)(2,1)} %get-tuple-element.40.refs_4_.refs_1_), channel_id=1, source_target_pairs={{0,24},{4,28},{8,16},{12,20},{16,8},{20,12},{24,0},{28,4},{1,25},{... | collective-permute-start | bytes 294920 | tf_op jit(solution)/shard_map/ppermute | solution.py:32
  7.9 1.7 %collective-permute-start.2 = (bf16[128,384]{1,0:T(8,128)(2,1)}, bf16[128,384]{1,0:T(8,128)(2,1)S(1)}, u32[]{:S(2)}, u32[]{:S(2)}) collective-permute-start(bf16[128,384]{1,0:T(8,128)(2,1)} %get-tuple-element.40.refs_4_.refs_1_), channel_id=1, source_target_pairs={{0,12},{4,8},{8,4},{12,0},{16,28},{20,24},{24,20},{28,16},{1,13},{... | collective-permute-start | bytes 294920 | tf_op jit(solution)/shard_map/ppermute | solution.py:32
  9.6 1.2 %collective-permute-start.1 = (bf16[128,384]{1,0:T(8,128)(2,1)}, bf16[128,384]{1,0:T(8,128)(2,1)S(1)}, u32[]{:S(2)}, u32[]{:S(2)}) collective-permute-start(bf16[128,384]{1,0:T(8,128)(2,1)} %get-tuple-element.40.refs_4_.refs_1_), channel_id=1, source_target_pairs={{0,8},{4,12},{8,0},{12,4},{16,24},{20,28},{24,16},{28,20},{1,9},{5... | collective-permute-start | bytes 294920 | tf_op jit(solution)/shard_map/ppermute | solution.py:32
  11.8 1.5 %collective-permute-start.6 = (bf16[128,384]{1,0:T(8,128)(2,1)S(1)}, bf16[128,384]{1,0:T(8,128)(2,1)S(1)}, u32[]{:S(2)}, u32[]{:S(2)}) collective-permute-start(bf16[128,384]{1,0:T(8,128)(2,1)S(1)} %collective-permute-done.5.refs_10_), channel_id=1, source_target_pairs={{0,4},{4,0},{8,12},{12,8},{16,20},{20,16},{24,28},{28,24},{1,5},{5... | collective-permute-start | bytes 294920 | tf_op jit(solution)/shard_map/ppermute | solution.py:32
  13.3 3.2 %collective-permute-done.3.refs_8_ = bf16[128,384]{1,0:T(8,128)(2,1)S(1)} collective-permute-done((bf16[128,384]{1,0:T(8,128)(2,1)}, bf16[128,384]{1,0:T(8,128)(2,1)S(1)}, u32[]{:S(2)}, u32[]{:S(2)}) %collective-permute-start.3) | collective-permute-done | bytes 98336 | tf_op jit(solution)/shard_map/ppermute | solution.py:32
  16.4 1.5 %collective-permute-start.4 = (bf16[128,384]{1,0:T(8,128)(2,1)S(1)}, bf16[128,384]{1,0:T(8,128)(2,1)S(1)}, u32[]{:S(2)}, u32[]{:S(2)}) collective-permute-start(bf16[128,384]{1,0:T(8,128)(2,1)S(1)} %collective-permute-done.3.refs_8_), channel_id=1, source_target_pairs={{0,4},{4,0},{8,12},{12,8},{16,20},{20,16},{24,28},{28,24},{1,5},{5... | collective-permute-start | bytes 294920 | tf_op jit(solution)/shard_map/ppermute | solution.py:32
  18.8 2.3 %collective-permute-done.4.refs_9_ = bf16[128,384]{1,0:T(8,128)(2,1)S(1)} collective-permute-done((bf16[128,384]{1,0:T(8,128)(2,1)S(1)}, bf16[128,384]{1,0:T(8,128)(2,1)S(1)}, u32[]{:S(2)}, u32[]{:S(2)}) %collective-permute-start.4) | collective-permute-done | bytes 98336 | tf_op jit(solution)/shard_map/ppermute | solution.py:32
  21.2 9.7 %attend.1 = (bf16[48,512]{1,0:T(8,128)(2,1)S(1)}, bf16[48,512]{1,0:T(8,128)(2,1)S(1)}, bf16[48,512]{1,0:T(8,128)(2,1)S(1)}, bf16[48,512]{1,0:T(8,128)(2,1)S(1)},...) custom-call(s32[384,1]{1,0:T(8,128)S(1)} %get-tuple-element.46.refs_, ...), custom_call_target="tpu_custom_call" | custom-call | flops 12000000000 | bytes 36000000 | tf_op jit(solution)/shard_map/attend/pallas_call | solution.py:262
  30.9 3.5 %collective-permute-start.7 = (bf16[48,512]{1,0:T(8,128)(2,1)S(1)}, bf16[48,512]{1,0:T(8,128)(2,1)S(1)}, u32[]{:S(2)}, u32[]{:S(2)}) collective-permute-start(bf16[48,512]{1,0:T(8,128)(2,1)S(1)} %get-tuple-element.50), channel_id=1, source_target_pairs={{0,28},{4,24},{8,20},{12,16},{16,12},{20,8},{24,4},{28,0},{1,29},{... | collective-permute-start | bytes 147464 | tf_op jit(solution)/shard_map/ppermute | solution.py:32
  34.4 1.4 %collective-permute-start.8 = (bf16[48,512]{1,0:T(8,128)(2,1)S(1)}, bf16[48,512]{1,0:T(8,128)(2,1)S(1)}, u32[]{:S(2)}, u32[]{:S(2)}) collective-permute-start(bf16[48,512]{1,0:T(8,128)(2,1)S(1)} %get-tuple-element.51), channel_id=1, source_target_pairs={{0,24},{4,28},{8,16},{12,20},{16,8},{20,12},{24,0},{28,4},{1,25},{... | collective-permute-start | bytes 147464 | tf_op jit(solution)/shard_map/ppermute | solution.py:32
  35.8 2.8 %collective-permute-start.10 = (bf16[48,512]{1,0:T(8,128)(2,1)S(1)}, bf16[48,512]{1,0:T(8,128)(2,1)S(1)}, u32[]{:S(2)}, u32[]{:S(2)}) collective-permute-start(bf16[48,512]{1,0:T(8,128)(2,1)S(1)} %get-tuple-element.53), channel_id=1, source_target_pairs={{0,16},{4,20},{8,24},{12,28},{16,0},{20,4},{24,8},{28,12},{1,17},{... | collective-permute-start | bytes 147464 | tf_op jit(solution)/shard_map/ppermute | solution.py:32
  39.7 1.9 %collective-permute-start.12 = (bf16[48,512]{1,0:T(8,128)(2,1)S(1)}, bf16[48,512]{1,0:T(8,128)(2,1)S(1)}, u32[]{:S(2)}, u32[]{:S(2)}) collective-permute-start(bf16[48,512]{1,0:T(8,128)(2,1)S(1)} %get-tuple-element.55), channel_id=1, source_target_pairs={{0,8},{4,12},{8,0},{12,4},{16,24},{20,28},{24,16},{28,20},{1,9},{5... | collective-permute-start | bytes 147464 | tf_op jit(solution)/shard_map/ppermute | solution.py:32
  44.2 1.5 %collective-permute-done.13.refs_11_ = bf16[48,512]{1,0:T(8,128)(2,1)S(1)} collective-permute-done((bf16[48,512]{1,0:T(8,128)(2,1)S(1)}, bf16[48,512]{1,0:T(8,128)(2,1)S(1)}, u32[]{:S(2)}, u32[]{:S(2)}) %collective-permute-start.13) | collective-permute-done | bytes 49184 | tf_op jit(solution)/shard_map/ppermute | solution.py:32
  45.7 1.5 %merge.1 = (bf16[32,1536]{1,0:T(8,128)(2,1)S(1)}, bf16[32,1536]{1,0:T(8,128)(2,1)S(1)}, bf16[32,1536]{1,0:T(8,128)(2,1)S(1)}, bf16[32,1536]{1,0:T(8,128)(2,1)S(1)}) custom-call(s32[1]{0:T(128)} %bitcast.refs_0_.kv_ref, bf16[128,384]{1,0:T(8,128)(2,1)S(1)} %copy-done.6, bf16[128,128]{1,0:T(8,128)(2,1)S(1)} %get-tuple-element.44.refs_2_, ...), custom_call_target="tpu_custom_call" | custom-call | flops 12000000000 | bytes 36000000 | tf_op jit(solution)/shard_map/merge/pallas_call | solution.py:490
  47.3 1.6 %collective-permute-start.15 = (bf16[32,1536]{1,0:T(8,128)(2,1)S(1)}, bf16[32,1536]{1,0:T(8,128)(2,1)S(1)}, u32[]{:S(2)}, u32[]{:S(2)}) collective-permute-start(bf16[32,1536]{1,0:T(8,128)(2,1)S(1)} %get-tuple-element.60), channel_id=1, source_target_pairs={{0,2},{1,3},{2,0},{3,1},{4,6},{5,7},{6,4},{7,5},{8,10},{9,11},{10,... | collective-permute-start | bytes 294920 | tf_op jit(solution)/shard_map/ppermute | solution.py:32
  49.4 3.5 %collective-permute-done.15.refs_2_ = bf16[32,1536]{1,0:T(8,128)(2,1)S(1)} collective-permute-done((bf16[32,1536]{1,0:T(8,128)(2,1)S(1)}, bf16[32,1536]{1,0:T(8,128)(2,1)S(1)}, u32[]{:S(2)}, u32[]{:S(2)}) %collective-permute-start.15) | collective-permute-done | bytes 98336 | tf_op jit(solution)/shard_map/ppermute | solution.py:32
  52.9 1.2 %collective-permute-done.16.refs_3_ = bf16[32,1536]{1,0:T(8,128)(2,1)S(1)} collective-permute-done((bf16[32,1536]{1,0:T(8,128)(2,1)S(1)}, bf16[32,1536]{1,0:T(8,128)(2,1)S(1)}, u32[]{:S(2)}, u32[]{:S(2)}) %collective-permute-start.16) | collective-permute-done | bytes 98336 | tf_op jit(solution)/shard_map/ppermute | solution.py:32
  54.7 2.5 %collective-permute-start.22 = (bf16[32,1664]{1,0:T(8,128)(2,1)S(1)}, bf16[32,1664]{1,0:T(8,128)(2,1)S(1)}, u32[]{:S(2)}, u32[]{:S(2)}) collective-permute-start(bf16[32,1664]{1,0:T(8,128)(2,1)S(1)} %get-tuple-element.63.order_ref.refs_0_), channel_id=1, source_target_pairs={{0,24},{4,28},{8,16},{12,20},{16,8},{20,12},{24,0},{28,4},{1,25},{... | collective-permute-start | bytes 319496 | tf_op jit(solution)/shard_map/ppermute | solution.py:32
  57.2 1.9 %collective-permute-start.19 = (bf16[32,1664]{1,0:T(8,128)(2,1)S(1)}, bf16[32,1664]{1,0:T(8,128)(2,1)S(1)}, u32[]{:S(2)}, u32[]{:S(2)}) collective-permute-start(bf16[32,1664]{1,0:T(8,128)(2,1)S(1)} %get-tuple-element.63.order_ref.refs_0_), channel_id=1, source_target_pairs={{0,12},{4,8},{8,4},{12,0},{16,28},{20,24},{24,20},{28,16},{1,13},{... | collective-permute-start | bytes 319496 | tf_op jit(solution)/shard_map/ppermute | solution.py:32
  59.2 1.5 %collective-permute-start.17 = (bf16[32,1664]{1,0:T(8,128)(2,1)S(1)}, bf16[32,1664]{1,0:T(8,128)(2,1)S(1)}, u32[]{:S(2)}, u32[]{:S(2)}) collective-permute-start(bf16[32,1664]{1,0:T(8,128)(2,1)S(1)} %get-tuple-element.63.order_ref.refs_0_), channel_id=1, source_target_pairs={{0,4},{4,0},{8,12},{12,8},{16,20},{20,16},{24,28},{28,24},{1,5},{5... | collective-permute-start | bytes 319496 | tf_op jit(solution)/shard_map/ppermute | solution.py:32
  60.7 1.7 %collective-permute-done.22.refs_6_ = bf16[32,1664]{1,0:T(8,128)(2,1)S(1)} collective-permute-done((bf16[32,1664]{1,0:T(8,128)(2,1)S(1)}, bf16[32,1664]{1,0:T(8,128)(2,1)S(1)}, u32[]{:S(2)}, u32[]{:S(2)}) %collective-permute-start.22) | collective-permute-done | bytes 106528 | tf_op jit(solution)/shard_map/ppermute | solution.py:32
  62.9 3.4 %collective-permute-done.20.refs_4_ = bf16[32,1664]{1,0:T(8,128)(2,1)S(1)} collective-permute-done((bf16[32,1664]{1,0:T(8,128)(2,1)S(1)}, bf16[32,1664]{1,0:T(8,128)(2,1)S(1)}, u32[]{:S(2)}, u32[]{:S(2)}) %collective-permute-start.20) | collective-permute-done | bytes 106528 | tf_op jit(solution)/shard_map/ppermute | solution.py:32
  66.9 2.8 %copy-done = bf16[2,1536,1024]{2,1,0:T(8,128)(2,1)S(1)} copy-done((bf16[2,1536,1024]{2,1,0:T(8,128)(2,1)S(1)}, bf16[2,1536,1024]{2,1,0:T(8,128)(2,1)}, u32[]{:S(2)}) %copy-start) | copy-done | bytes 6291480
  71.2 3.5 %experts.1 = (bf16[32,1536]{1,0:T(8,128)(2,1)S(1)}, bf16[32,1536]{1,0:T(8,128)(2,1)S(1)}, bf16[32,1536]{1,0:T(8,128)(2,1)S(1)}, bf16[32,1536]{1,0:T(8,128)(2,1)S...) custom-call(s32[1]{0:T(128)} %bitcast.2.req_ref, ...), custom_call_target="tpu_custom_call" | custom-call | flops 4000000000 | bytes 12000000 | tf_op jit(solution)/shard_map/experts/pallas_call | solution.py:528
  75.3 2.7 %collective-permute-start.24 = (bf16[32,1536]{1,0:T(8,128)(2,1)S(1)}, bf16[32,1536]{1,0:T(8,128)(2,1)S(1)}, u32[]{:S(2)}, u32[]{:S(2)}) collective-permute-start(bf16[32,1536]{1,0:T(8,128)(2,1)S(1)} %get-tuple-element.65), channel_id=1, source_target_pairs={{0,16},{4,20},{8,24},{12,28},{16,0},{20,4},{24,8},{28,12},{1,17},{... | collective-permute-start | bytes 294920 | tf_op jit(solution)/shard_map/ppermute | solution.py:32
  78.0 1.1 %collective-permute-start.25 = (bf16[32,1536]{1,0:T(8,128)(2,1)S(1)}, bf16[32,1536]{1,0:T(8,128)(2,1)S(1)}, u32[]{:S(2)}, u32[]{:S(2)}) collective-permute-start(bf16[32,1536]{1,0:T(8,128)(2,1)S(1)} %get-tuple-element.66), channel_id=1, source_target_pairs={{0,20},{4,16},{8,28},{12,24},{16,4},{20,0},{24,12},{28,8},{1,21},{... | collective-permute-start | bytes 294920 | tf_op jit(solution)/shard_map/ppermute | solution.py:32
  80.0 2.5 %collective-permute-start.28 = (bf16[32,1536]{1,0:T(8,128)(2,1)S(1)}, bf16[32,1536]{1,0:T(8,128)(2,1)S(1)}, u32[]{:S(2)}, u32[]{:S(2)}) collective-permute-start(bf16[32,1536]{1,0:T(8,128)(2,1)S(1)} %add_convert_fusion.1), channel_id=1, source_target_pairs={{0,24},{4,28},{8,16},{12,20},{16,8},{20,12},{24,0},{28,4},{1,25},{... | collective-permute-start | bytes 294920 | tf_op jit(solution)/shard_map/ppermute | solution.py:32
  82.5 1.5 %collective-permute-start.29 = (bf16[32,1536]{1,0:T(8,128)(2,1)S(1)}, bf16[32,1536]{1,0:T(8,128)(2,1)S(1)}, u32[]{:S(2)}, u32[]{:S(2)}) collective-permute-start(bf16[32,1536]{1,0:T(8,128)(2,1)S(1)} %get-tuple-element.73), channel_id=1, source_target_pairs={{0,4},{4,0},{8,12},{12,8},{16,20},{20,16},{24,28},{28,24},{1,5},{5... | collective-permute-start | bytes 294920 | tf_op jit(solution)/shard_map/ppermute | solution.py:32
  84.0 1.7 %collective-permute-done.24 = bf16[32,1536]{1,0:T(8,128)(2,1)S(1)} collective-permute-done((bf16[32,1536]{1,0:T(8,128)(2,1)S(1)}, bf16[32,1536]{1,0:T(8,128)(2,1)S(1)}, u32[]{:S(2)}, u32[]{:S(2)}) %collective-permute-start.24) | collective-permute-done | bytes 98336 | tf_op jit(solution)/shard_map/ppermute | solution.py:32
  86.1 3.7 %collective-permute-done.25 = bf16[32,1536]{1,0:T(8,128)(2,1)S(1)} collective-permute-done((bf16[32,1536]{1,0:T(8,128)(2,1)S(1)}, bf16[32,1536]{1,0:T(8,128)(2,1)S(1)}, u32[]{:S(2)}, u32[]{:S(2)}) %collective-permute-start.25) | collective-permute-done | bytes 98336 | tf_op jit(solution)/shard_map/ppermute | solution.py:32
  89.8 1.4 %collective-permute-done.30 = bf16[32,1536]{1,0:T(8,128)(2,1)S(1)} collective-permute-done((bf16[32,1536]{1,0:T(8,128)(2,1)S(1)}, bf16[32,1536]{1,0:T(8,128)(2,1)S(1)}, u32[]{:S(2)}, u32[]{:S(2)}) %collective-permute-start.30) | collective-permute-done | bytes 98336 | tf_op jit(solution)/shard_map/ppermute | solution.py:32
  (87 shorter events, 12.2 us)
Async XLA Ops:
  2.7 9.0 %collective-permute-start.5 = (bf16[128,384]{1,0:T(8,128)(2,1)}, bf16[128,384]{1,0:T(8,128)(2,1)S(1)}, u32[]{:S(2)}, u32[]{:S(2)}) collective-permute-start(bf16[128,384]{1,0:T(8,128)(2,1)} %get-tuple-element.40.refs_4_.refs_1_), channel_id=1, source_target_pairs={{0,24},{4,28},{8,16},{12,20},{16,8},{20,12},{24,0},{28,4},{1,25},{... | collective-permute-start | bytes 294920 | tf_op jit(solution)/shard_map/ppermute | solution.py:32
  7.9 8.6 %collective-permute-start.3 = (bf16[128,384]{1,0:T(8,128)(2,1)}, bf16[128,384]{1,0:T(8,128)(2,1)S(1)}, u32[]{:S(2)}, u32[]{:S(2)}) collective-permute-start(bf16[128,384]{1,0:T(8,128)(2,1)} %get-tuple-element.40.refs_4_.refs_1_), channel_id=1, source_target_pairs={{0,16},{4,20},{8,24},{12,28},{16,0},{20,4},{24,8},{28,12},{1,17},{... | collective-permute-start | bytes 294920 | tf_op jit(solution)/shard_map/ppermute | solution.py:32
  7.9 10.9 %collective-permute-start.2 = (bf16[128,384]{1,0:T(8,128)(2,1)}, bf16[128,384]{1,0:T(8,128)(2,1)S(1)}, u32[]{:S(2)}, u32[]{:S(2)}) collective-permute-start(bf16[128,384]{1,0:T(8,128)(2,1)} %get-tuple-element.40.refs_4_.refs_1_), channel_id=1, source_target_pairs={{0,12},{4,8},{8,4},{12,0},{16,28},{20,24},{24,20},{28,16},{1,13},{... | collective-permute-start | bytes 294920 | tf_op jit(solution)/shard_map/ppermute | solution.py:32
  9.6 9.2 %collective-permute-start.1 = (bf16[128,384]{1,0:T(8,128)(2,1)}, bf16[128,384]{1,0:T(8,128)(2,1)S(1)}, u32[]{:S(2)}, u32[]{:S(2)}) collective-permute-start(bf16[128,384]{1,0:T(8,128)(2,1)} %get-tuple-element.40.refs_4_.refs_1_), channel_id=1, source_target_pairs={{0,8},{4,12},{8,0},{12,4},{16,24},{20,28},{24,16},{28,20},{1,9},{5... | collective-permute-start | bytes 294920 | tf_op jit(solution)/shard_map/ppermute | solution.py:32
  10.8 7.9 %collective-permute-start = (bf16[128,384]{1,0:T(8,128)(2,1)}, bf16[128,384]{1,0:T(8,128)(2,1)S(1)}, u32[]{:S(2)}, u32[]{:S(2)}) collective-permute-start(bf16[128,384]{1,0:T(8,128)(2,1)} %get-tuple-element.40.refs_4_.refs_1_), channel_id=1, source_target_pairs={{0,4},{4,0},{8,12},{12,8},{16,20},{20,16},{24,28},{28,24},{1,5},{5... | collective-permute-start | bytes 294920 | tf_op jit(solution)/shard_map/ppermute | solution.py:32
  11.8 7.0 %collective-permute-start.6 = (bf16[128,384]{1,0:T(8,128)(2,1)S(1)}, bf16[128,384]{1,0:T(8,128)(2,1)S(1)}, u32[]{:S(2)}, u32[]{:S(2)}) collective-permute-start(bf16[128,384]{1,0:T(8,128)(2,1)S(1)} %collective-permute-done.5.refs_10_), channel_id=1, source_target_pairs={{0,4},{4,0},{8,12},{12,8},{16,20},{20,16},{24,28},{28,24},{1,5},{5... | collective-permute-start | bytes 294920 | tf_op jit(solution)/shard_map/ppermute | solution.py:32
  16.4 4.6 %collective-permute-start.4 = (bf16[128,384]{1,0:T(8,128)(2,1)S(1)}, bf16[128,384]{1,0:T(8,128)(2,1)S(1)}, u32[]{:S(2)}, u32[]{:S(2)}) collective-permute-start(bf16[128,384]{1,0:T(8,128)(2,1)S(1)} %collective-permute-done.3.refs_8_), channel_id=1, source_target_pairs={{0,4},{4,0},{8,12},{12,8},{16,20},{20,16},{24,28},{28,24},{1,5},{5... | collective-permute-start | bytes 294920 | tf_op jit(solution)/shard_map/ppermute | solution.py:32
  21.2 24.5 %copy-start.2 = (bf16[384,1536]{1,0:T(8,128)(2,1)S(1)}, bf16[384,1536]{1,0:T(8,128)(2,1)}, u32[]{:S(2)}) copy-start(bf16[384,1536]{1,0:T(8,128)(2,1)} %refs_4_.1) | copy-start | bytes 3538948
  30.9 8.8 %collective-permute-start.7 = (bf16[48,512]{1,0:T(8,128)(2,1)S(1)}, bf16[48,512]{1,0:T(8,128)(2,1)S(1)}, u32[]{:S(2)}, u32[]{:S(2)}) collective-permute-start(bf16[48,512]{1,0:T(8,128)(2,1)S(1)} %get-tuple-element.50), channel_id=1, source_target_pairs={{0,28},{4,24},{8,20},{12,16},{16,12},{20,8},{24,4},{28,0},{1,29},{... | collective-permute-start | bytes 147464 | tf_op jit(solution)/shard_map/ppermute | solution.py:32
  34.4 7.2 %collective-permute-start.8 = (bf16[48,512]{1,0:T(8,128)(2,1)S(1)}, bf16[48,512]{1,0:T(8,128)(2,1)S(1)}, u32[]{:S(2)}, u32[]{:S(2)}) collective-permute-start(bf16[48,512]{1,0:T(8,128)(2,1)S(1)} %get-tuple-element.51), channel_id=1, source_target_pairs={{0,24},{4,28},{8,16},{12,20},{16,8},{20,12},{24,0},{28,4},{1,25},{... | collective-permute-start | bytes 147464 | tf_op jit(solution)/shard_map/ppermute | solution.py:32
  35.7 6.9 %collective-permute-start.9 = (bf16[48,512]{1,0:T(8,128)(2,1)S(1)}, bf16[48,512]{1,0:T(8,128)(2,1)S(1)}, u32[]{:S(2)}, u32[]{:S(2)}) collective-permute-start(bf16[48,512]{1,0:T(8,128)(2,1)S(1)} %get-tuple-element.52), channel_id=1, source_target_pairs={{0,20},{4,16},{8,28},{12,24},{16,4},{20,0},{24,12},{28,8},{1,21},{... | collective-permute-start | bytes 147464 | tf_op jit(solution)/shard_map/ppermute | solution.py:32
  35.8 6.7 %collective-permute-start.10 = (bf16[48,512]{1,0:T(8,128)(2,1)S(1)}, bf16[48,512]{1,0:T(8,128)(2,1)S(1)}, u32[]{:S(2)}, u32[]{:S(2)}) collective-permute-start(bf16[48,512]{1,0:T(8,128)(2,1)S(1)} %get-tuple-element.53), channel_id=1, source_target_pairs={{0,16},{4,20},{8,24},{12,28},{16,0},{20,4},{24,8},{28,12},{1,17},{... | collective-permute-start | bytes 147464 | tf_op jit(solution)/shard_map/ppermute | solution.py:32
  38.6 5.0 %collective-permute-start.11 = (bf16[48,512]{1,0:T(8,128)(2,1)S(1)}, bf16[48,512]{1,0:T(8,128)(2,1)S(1)}, u32[]{:S(2)}, u32[]{:S(2)}) collective-permute-start(bf16[48,512]{1,0:T(8,128)(2,1)S(1)} %get-tuple-element.54), channel_id=1, source_target_pairs={{0,12},{4,8},{8,4},{12,0},{16,28},{20,24},{24,20},{28,16},{1,13},{... | collective-permute-start | bytes 147464 | tf_op jit(solution)/shard_map/ppermute | solution.py:32
  39.7 4.5 %collective-permute-start.12 = (bf16[48,512]{1,0:T(8,128)(2,1)S(1)}, bf16[48,512]{1,0:T(8,128)(2,1)S(1)}, u32[]{:S(2)}, u32[]{:S(2)}) collective-permute-start(bf16[48,512]{1,0:T(8,128)(2,1)S(1)} %get-tuple-element.55), channel_id=1, source_target_pairs={{0,8},{4,12},{8,0},{12,4},{16,24},{20,28},{24,16},{28,20},{1,9},{5... | collective-permute-start | bytes 147464 | tf_op jit(solution)/shard_map/ppermute | solution.py:32
  41.6 4.1 %collective-permute-start.13 = (bf16[48,512]{1,0:T(8,128)(2,1)S(1)}, bf16[48,512]{1,0:T(8,128)(2,1)S(1)}, u32[]{:S(2)}, u32[]{:S(2)}) collective-permute-start(bf16[48,512]{1,0:T(8,128)(2,1)S(1)} %get-tuple-element.56), channel_id=1, source_target_pairs={{0,4},{4,0},{8,12},{12,8},{16,20},{20,16},{24,28},{28,24},{1,5},{5... | collective-permute-start | bytes 147464 | tf_op jit(solution)/shard_map/ppermute | solution.py:32
  47.2 2.3 %collective-permute-start.14 = (bf16[32,1536]{1,0:T(8,128)(2,1)S(1)}, bf16[32,1536]{1,0:T(8,128)(2,1)S(1)}, u32[]{:S(2)}, u32[]{:S(2)}) collective-permute-start(bf16[32,1536]{1,0:T(8,128)(2,1)S(1)} %get-tuple-element.59), channel_id=1, source_target_pairs={{0,1},{1,0},{2,3},{3,2},{4,5},{5,4},{6,7},{7,6},{8,9},{9,8},{10,11... | collective-permute-start | bytes 294920 | tf_op jit(solution)/shard_map/ppermute | solution.py:32
  47.3 5.7 %collective-permute-start.15 = (bf16[32,1536]{1,0:T(8,128)(2,1)S(1)}, bf16[32,1536]{1,0:T(8,128)(2,1)S(1)}, u32[]{:S(2)}, u32[]{:S(2)}) collective-permute-start(bf16[32,1536]{1,0:T(8,128)(2,1)S(1)} %get-tuple-element.60), channel_id=1, source_target_pairs={{0,2},{1,3},{2,0},{3,1},{4,6},{5,7},{6,4},{7,5},{8,10},{9,11},{10,... | collective-permute-start | bytes 294920 | tf_op jit(solution)/shard_map/ppermute | solution.py:32
  48.8 5.3 %collective-permute-start.16 = (bf16[32,1536]{1,0:T(8,128)(2,1)S(1)}, bf16[32,1536]{1,0:T(8,128)(2,1)S(1)}, u32[]{:S(2)}, u32[]{:S(2)}) collective-permute-start(bf16[32,1536]{1,0:T(8,128)(2,1)S(1)} %get-tuple-element.61), channel_id=1, source_target_pairs={{0,3},{1,2},{2,1},{3,0},{4,7},{5,6},{6,5},{7,4},{8,11},{9,10},{10,... | collective-permute-start | bytes 294920 | tf_op jit(solution)/shard_map/ppermute | solution.py:32
  54.7 7.7 %collective-permute-start.22 = (bf16[32,1664]{1,0:T(8,128)(2,1)S(1)}, bf16[32,1664]{1,0:T(8,128)(2,1)S(1)}, u32[]{:S(2)}, u32[]{:S(2)}) collective-permute-start(bf16[32,1664]{1,0:T(8,128)(2,1)S(1)} %get-tuple-element.63.order_ref.refs_0_), channel_id=1, source_target_pairs={{0,24},{4,28},{8,16},{12,20},{16,8},{20,12},{24,0},{28,4},{1,25},{... | collective-permute-start | bytes 319496 | tf_op jit(solution)/shard_map/ppermute | solution.py:32
  57.2 9.2 %collective-permute-start.20 = (bf16[32,1664]{1,0:T(8,128)(2,1)S(1)}, bf16[32,1664]{1,0:T(8,128)(2,1)S(1)}, u32[]{:S(2)}, u32[]{:S(2)}) collective-permute-start(bf16[32,1664]{1,0:T(8,128)(2,1)S(1)} %get-tuple-element.63.order_ref.refs_0_), channel_id=1, source_target_pairs={{0,16},{4,20},{8,24},{12,28},{16,0},{20,4},{24,8},{28,12},{1,17},{... | collective-permute-start | bytes 319496 | tf_op jit(solution)/shard_map/ppermute | solution.py:32
  57.2 13.0 %collective-permute-start.19 = (bf16[32,1664]{1,0:T(8,128)(2,1)S(1)}, bf16[32,1664]{1,0:T(8,128)(2,1)S(1)}, u32[]{:S(2)}, u32[]{:S(2)}) collective-permute-start(bf16[32,1664]{1,0:T(8,128)(2,1)S(1)} %get-tuple-element.63.order_ref.refs_0_), channel_id=1, source_target_pairs={{0,12},{4,8},{8,4},{12,0},{16,28},{20,24},{24,20},{28,16},{1,13},{... | collective-permute-start | bytes 319496 | tf_op jit(solution)/shard_map/ppermute | solution.py:32
  59.1 11.1 %collective-permute-start.18 = (bf16[32,1664]{1,0:T(8,128)(2,1)S(1)}, bf16[32,1664]{1,0:T(8,128)(2,1)S(1)}, u32[]{:S(2)}, u32[]{:S(2)}) collective-permute-start(bf16[32,1664]{1,0:T(8,128)(2,1)S(1)} %get-tuple-element.63.order_ref.refs_0_), channel_id=1, source_target_pairs={{0,8},{4,12},{8,0},{12,4},{16,24},{20,28},{24,16},{28,20},{1,9},{5... | collective-permute-start | bytes 319496 | tf_op jit(solution)/shard_map/ppermute | solution.py:32
  59.2 11.0 %collective-permute-start.17 = (bf16[32,1664]{1,0:T(8,128)(2,1)S(1)}, bf16[32,1664]{1,0:T(8,128)(2,1)S(1)}, u32[]{:S(2)}, u32[]{:S(2)}) collective-permute-start(bf16[32,1664]{1,0:T(8,128)(2,1)S(1)} %get-tuple-element.63.order_ref.refs_0_), channel_id=1, source_target_pairs={{0,4},{4,0},{8,12},{12,8},{16,20},{20,16},{24,28},{28,24},{1,5},{5... | collective-permute-start | bytes 319496 | tf_op jit(solution)/shard_map/ppermute | solution.py:32
  62.4 7.8 %collective-permute-start.23 = (bf16[32,1664]{1,0:T(8,128)(2,1)S(1)}, bf16[32,1664]{1,0:T(8,128)(2,1)S(1)}, u32[]{:S(2)}, u32[]{:S(2)}) collective-permute-start(bf16[32,1664]{1,0:T(8,128)(2,1)S(1)} %collective-permute-done.22.refs_6_), channel_id=1, source_target_pairs={{0,4},{4,0},{8,12},{12,8},{16,20},{20,16},{24,28},{28,24},{1,5},{5... | collective-permute-start | bytes 319496 | tf_op jit(solution)/shard_map/ppermute | solution.py:32
  66.4 4.9 %collective-permute-start.21 = (bf16[32,1664]{1,0:T(8,128)(2,1)S(1)}, bf16[32,1664]{1,0:T(8,128)(2,1)S(1)}, u32[]{:S(2)}, u32[]{:S(2)}) collective-permute-start(bf16[32,1664]{1,0:T(8,128)(2,1)S(1)} %collective-permute-done.20.refs_4_), channel_id=1, source_target_pairs={{0,4},{4,0},{8,12},{12,8},{16,20},{20,16},{24,28},{28,24},{1,5},{5... | collective-permute-start | bytes 319496 | tf_op jit(solution)/shard_map/ppermute | solution.py:32
  74.7 5.3 %collective-permute-start.27 = (bf16[32,1536]{1,0:T(8,128)(2,1)S(1)}, bf16[32,1536]{1,0:T(8,128)(2,1)S(1)}, u32[]{:S(2)}, u32[]{:S(2)}) collective-permute-start(bf16[32,1536]{1,0:T(8,128)(2,1)S(1)} %get-tuple-element.69), channel_id=1, source_target_pairs={{0,4},{4,0},{8,12},{12,8},{16,20},{20,16},{24,28},{28,24},{1,5},{5... | collective-permute-start | bytes 294920 | tf_op jit(solution)/shard_map/ppermute | solution.py:32
  75.3 10.3 %collective-permute-start.24 = (bf16[32,1536]{1,0:T(8,128)(2,1)S(1)}, bf16[32,1536]{1,0:T(8,128)(2,1)S(1)}, u32[]{:S(2)}, u32[]{:S(2)}) collective-permute-start(bf16[32,1536]{1,0:T(8,128)(2,1)S(1)} %get-tuple-element.65), channel_id=1, source_target_pairs={{0,16},{4,20},{8,24},{12,28},{16,0},{20,4},{24,8},{28,12},{1,17},{... | collective-permute-start | bytes 294920 | tf_op jit(solution)/shard_map/ppermute | solution.py:32
  78.0 11.8 %collective-permute-start.25 = (bf16[32,1536]{1,0:T(8,128)(2,1)S(1)}, bf16[32,1536]{1,0:T(8,128)(2,1)S(1)}, u32[]{:S(2)}, u32[]{:S(2)}) collective-permute-start(bf16[32,1536]{1,0:T(8,128)(2,1)S(1)} %get-tuple-element.66), channel_id=1, source_target_pairs={{0,20},{4,16},{8,28},{12,24},{16,4},{20,0},{24,12},{28,8},{1,21},{... | collective-permute-start | bytes 294920 | tf_op jit(solution)/shard_map/ppermute | solution.py:32
  79.1 10.7 %collective-permute-start.26 = (bf16[32,1536]{1,0:T(8,128)(2,1)S(1)}, bf16[32,1536]{1,0:T(8,128)(2,1)S(1)}, u32[]{:S(2)}, u32[]{:S(2)}) collective-permute-start(bf16[32,1536]{1,0:T(8,128)(2,1)S(1)} %get-tuple-element.67), channel_id=1, source_target_pairs={{0,8},{4,12},{8,0},{12,4},{16,24},{20,28},{24,16},{28,20},{1,9},{5... | collective-permute-start | bytes 294920 | tf_op jit(solution)/shard_map/ppermute | solution.py:32
  80.0 9.8 %collective-permute-start.28 = (bf16[32,1536]{1,0:T(8,128)(2,1)S(1)}, bf16[32,1536]{1,0:T(8,128)(2,1)S(1)}, u32[]{:S(2)}, u32[]{:S(2)}) collective-permute-start(bf16[32,1536]{1,0:T(8,128)(2,1)S(1)} %add_convert_fusion.1), channel_id=1, source_target_pairs={{0,24},{4,28},{8,16},{12,20},{16,8},{20,12},{24,0},{28,4},{1,25},{... | collective-permute-start | bytes 294920 | tf_op jit(solution)/shard_map/ppermute | solution.py:32
  82.5 7.3 %collective-permute-start.29 = (bf16[32,1536]{1,0:T(8,128)(2,1)S(1)}, bf16[32,1536]{1,0:T(8,128)(2,1)S(1)}, u32[]{:S(2)}, u32[]{:S(2)}) collective-permute-start(bf16[32,1536]{1,0:T(8,128)(2,1)S(1)} %get-tuple-element.73), channel_id=1, source_target_pairs={{0,4},{4,0},{8,12},{12,8},{16,20},{20,16},{24,28},{28,24},{1,5},{5... | collective-permute-start | bytes 294920 | tf_op jit(solution)/shard_map/ppermute | solution.py:32
  85.7 5.5 %collective-permute-start.30 = (bf16[32,1536]{1,0:T(8,128)(2,1)S(1)}, bf16[32,1536]{1,0:T(8,128)(2,1)S(1)}, u32[]{:S(2)}, u32[]{:S(2)}) collective-permute-start(bf16[32,1536]{1,0:T(8,128)(2,1)S(1)} %get-tuple-element.74), channel_id=1, source_target_pairs={{0,12},{4,8},{8,4},{12,0},{16,28},{20,24},{24,20},{28,16},{1,13},{... | collective-permute-start | bytes 294920 | tf_op jit(solution)/shard_map/ppermute | solution.py:32
  (20 other events, 245.8 us)

commit v4 on v3

--- a/solution.py
+++ b/solution.py
@@ -54,22 +54,21 @@
     return [held[distance] for distance in sorted(held, key=lambda distance: -distance)]
 
 
-def sum_rows(values, axis):
+def sum_rows(values, near, axis):
     size = lax.axis_size(axis)
     far = size // 2
-    split = far + far // 2
+    split = far
+    count = values[0].shape[0]
     beside = {distance: swap(values[distance], axis, 1) for distance in range(split + 1, size, 2)}
     arrived = [swap(values[distance], axis, distance) for distance in range(far, split)]
-    arrived += [swap(values[distance], axis, distance) for distance in range(2, far, 2)]
-    joined = {}
+    near = swap(near, axis, 1)
     for distance in range(split, size, 2):
-        both = values[distance].astype(F32) + beside[distance + 1].astype(F32)
-        joined[distance] = both.astype(BF)
-    odd = {distance: values[distance] for distance in range(1, far, 2)}
-    joined, odd = lax.optimization_barrier((joined, odd))
-    arrived += [swap(value, axis, distance) for distance, value in joined.items()]
-    arrived += [swap(value, axis, distance) for distance, value in odd.items()]
-    total = values[0].astype(F32)
+        joined = values[distance].astype(F32) + beside[distance + 1].astype(F32)
+        arrived.append(swap(joined.astype(BF), axis, distance))
+    for distance in range(2, far, 2):
+        joined = values[distance].astype(F32) + near[distance // 2 * count : (distance // 2 + 1) * count].astype(F32)
+        arrived.append(swap(joined.astype(BF), axis, distance))
+    total = values[0].astype(F32) + near[:count].astype(F32)
     for value in arrived:
         total = total + value.astype(F32)
     return total
@@ -101,8 +100,17 @@
     return pieces[0] if len(pieces) == 1 else jnp.concatenate(pieces, 1)
 
 
-def query_kernel(req_ref, hidden_hbm, gain_hbm, weight_hbm, length_hbm, query_ref, normed_ref, cosines_ref,
-                 sines_ref, hidden_ref, gain_ref, weight_ref, length_ref, sem):
+def tables(req_ref, length_ref, rows):
+    lengths = jnp.broadcast_to(length_ref[pl.ds(req_ref[0], 1), :].astype(F32), (rows, rows))
+    lengths = jnp.where(iota((rows, rows), 0) == iota((rows, rows), 1), lengths, 0.0)
+    exponent = (iota((1, 2 * HD), 1) % (HD // 2)).astype(F32) * (-2.0 / HD)
+    angles = jnp.sum(lengths, -1, keepdims=True) * jnp.exp(exponent * math.log(10000.0))
+    sines = jnp.sin(angles)
+    return jnp.cos(angles), jnp.where(iota((1, 2 * HD), 1) % HD < HD // 2, -sines, sines)
+
+
+def query_kernel(req_ref, hidden_hbm, gain_hbm, weight_hbm, length_hbm, query_ref, hidden_ref, gain_ref, weight_ref,
+                 length_ref, sem):
     copies = [
         pltpu.make_async_copy(source, target, sem.at[place])
         for place, (source, target) in enumerate(
@@ -111,26 +119,20 @@
     ]
     for copy in copies:
         copy.start()
-    rows = cosines_ref.shape[0]
     copies[0].wait()
-    lengths = jnp.broadcast_to(length_ref[pl.ds(req_ref[0], 1), :].astype(F32), (rows, rows))
-    lengths = jnp.where(iota((rows, rows), 0) == iota((rows, rows), 1), lengths, 0.0)
-    exponent = (iota((1, 2 * HD), 1) % (HD // 2)).astype(F32) * (-2.0 / HD)
-    angles = jnp.sum(lengths, -1, keepdims=True) * jnp.exp(exponent * math.log(10000.0))
-    cosines = jnp.cos(angles)
-    sines = jnp.sin(angles)
-    sines = jnp.where(iota((1, 2 * HD), 1) % HD < HD // 2, -sines, sines)
-    cosines_ref[...] = cosines
-    sines_ref[...] = sines
+    cosines, sines = tables(req_ref, length_ref, query_ref.shape[0])
     copies[1].wait()
-    hidden = hidden_ref[...].astype(F32)
-    scale = lax.rsqrt(jnp.mean(hidden * hidden, -1, keepdims=True) + 1e-05)
     copies[3].wait()
-    normed = (hidden * scale * lanes_of(gain_ref)).astype(BF)
-    normed_ref[...] = normed
+    normed = rms_norm(hidden_ref[...], lanes_of(gain_ref))
     copies[2].wait()
     query = project_rows(normed, weight_ref[...])
     query_ref[...] = (rotate(query, cosines, sines) * 0.125).astype(BF)
+
+
+def rms_norm(hidden, gain):
+    hidden = hidden.astype(F32)
+    scale = lax.rsqrt(jnp.mean(hidden * hidden, -1, keepdims=True) + 1e-05)
+    return (hidden * scale * gain).astype(BF)
 
 
 def place_kernel(rows, share, req_ref, block_ref, length_ref, query_ref, left_ref, slot_ref, local_ref):
@@ -157,10 +159,18 @@
     return jnp.concatenate([ref[row : row + 1, :] for row in range(ref.shape[0])], 1)
 
 
-def fresh_kernel(normed_ref, key_weight_ref, value_weight_ref, cosines_ref, sines_ref, key_ref, value_ref):
-    key = project_rows(normed_ref[...], key_weight_ref[...])
-    key_ref[...] = rotate(key, cosines_ref[...], sines_ref[...]).astype(BF)
-    value_ref[...] = project_rows(normed_ref[...], value_weight_ref[...]).astype(BF)
+def fresh_kernel(req_ref, hidden_ref, gain_ref, key_weight_ref, value_weight_ref, length_ref, key_ref, value_ref):
+    cosines, sines = tables(req_ref, length_ref, key_ref.shape[0])
+    normed = rms_norm(hidden_ref[...], lanes_of(gain_ref))
+    key = project_rows(normed, key_weight_ref[...])
+    key_ref[...] = rotate(key, cosines, sines).astype(BF)
+    value_ref[...] = project_rows(normed, value_weight_ref[...]).astype(BF)
+
+
+def side_by_side(pairs):
+    none = jnp.zeros_like(pairs[:, 0])
+    first = jnp.concatenate([pairs[:, 0], none], 2)
+    return jnp.concatenate([first, jnp.concatenate([none, pairs[:, 1]], 2)], 1)
 
 
 def attend_kernel(heads, groups, chunk, nq, *refs):
@@ -178,13 +188,9 @@
 
     @pl.when(index == 0)
     def _():
-        total = None
-        for place, query_ref in enumerate(query_refs):
-            count = query_ref.shape[0]
-            picked = (iota((blocks, count), 1) + place * count == qrow_ref[...]).astype(BF)
-            part = dot(picked, query_ref[...])
-            total = part if total is None else total + part
-        asked_ref[...] = total
+        queries = jnp.concatenate([query_ref[...] for query_ref in query_refs], 0)
+        picked = (iota((blocks, queries.shape[0]), 1) == qrow_ref[...]).astype(BF)
+        asked_ref[...] = dot(picked, queries)
         laid_ref[...] = jnp.zeros(laid_ref.shape, F32)
 
     base = pl.multiple_of(index * chunk, chunk)
@@ -203,10 +209,12 @@
                 laid_ref[pl.ds(head, chunk, 16), :] = jnp.where(low, first, 0.0)
                 laid_ref[pl.ds(head + 8, chunk, 16), :] = jnp.where(low, 0.0, second)
     query = laid_ref[: chunk * 16, :].astype(BF)
-    scores = lax.dot_general(
-        query.reshape(chunk // 2, 32, 2 * HD), key_ref[...].reshape(chunk // 2, 2 * lanes, 2 * HD),
-        (((2,), (2,)), ((0,), (0,))), preferred_element_type=F32)
-    scores = jnp.concatenate([scores[:, None, :16, :lanes], scores[:, None, 16:, lanes:]], 1).reshape(chunk, 16, lanes)
+    query = side_by_side(query.reshape(chunk // 2, 2, 16, 2 * HD)).reshape(chunk // 4, 64, 4 * HD)
+    keys = key_ref[...].reshape(chunk // 4, 2, 2, lanes, 2 * HD)
+    keys = jnp.concatenate([keys[:, :, 0], keys[:, :, 1]], 3).reshape(chunk // 4, 2 * lanes, 4 * HD)
+    scores = lax.dot_general(query, keys, (((2,), (2,)), ((0,), (0,))), preferred_element_type=F32)
+    scores = jnp.concatenate([scores[:, None, :32, :lanes], scores[:, None, 32:, lanes:]], 1)
+    scores = scores.reshape(chunk, 16, lanes)
     cell_row = iota((8, lanes), 0)
     cell_lane = iota((8, lanes), 1)
     position = jnp.where(cell_lane % groups == cell_row // per_group, 2 * (cell_lane // groups), 1 << 20)
@@ -218,9 +226,7 @@
     highest = jnp.max(jnp.maximum(scores[:, :8], scores[:, 8:]), -1, keepdims=True)
     weights = jnp.where(usable, jnp.exp(scores - jnp.concatenate([highest, highest], 1)), 0.0)
     total = jnp.sum(weights[:, :8] + weights[:, 8:], -1, keepdims=True)
-    weights = weights.astype(BF).reshape(chunk // 2, 2, 16, lanes)
-    none = jnp.zeros((chunk // 2, 16, lanes), BF)
-    weights = jnp.concatenate([jnp.concatenate([weights[:, 0], none], 2), jnp.concatenate([none, weights[:, 1]], 2)], 1)
+    weights = side_by_side(weights.astype(BF).reshape(chunk // 2, 2, 16, lanes))
     numer = lax.dot_general(weights, value_ref[...].reshape(chunk // 2, 2 * lanes, 2 * HD), (((2,), (1,)), ((0,), (0,))), preferred_element_type=F32)
     numer = numer.reshape(chunk, 16, 2 * HD)
     numer = jnp.where(iota((1, 8, 2 * HD), 2) < HD, numer[:, :8], numer[:, 8:]).reshape(chunk * 8, 2 * HD)
@@ -281,9 +287,9 @@
 
 def merge_kernel(heads, groups, tokens, *refs):
     kv_ref, query_ref, key_ref, value_ref, weight_ref = refs[:5]
-    out_refs = refs[-1 - tokens : -1]
-    result_ref = refs[-1]
-    part_refs = refs[5 : -1 - tokens]
+    keep_refs = refs[-2 - tokens // 2 : -2]
+    give_ref, result_ref = refs[-2:]
+    part_refs = refs[5 : -2 - tokens // 2]
     parts = jnp.concatenate([part_ref[...] for part_ref in part_refs], 0)
     rows = query_ref.shape[0]
     blocks, width = parts.shape
@@ -321,18 +327,22 @@
     attended = joined[:, :feature].astype(BF)
     result_ref[...] = dot(attended, weight_ref[...])
     count = rows // tokens
-    for place, out_ref in enumerate(out_refs):
+    for place in range(tokens):
         start = pl.multiple_of(jnp.bitwise_xor(kv_ref[0], place) * count, count)
-        out_ref[...] = result_ref[pl.ds(start, count), :].astype(BF)
-
-
-def route_kernel(kv_ref, hidden_ref, gain_ref, router_ref, routes_ref, *refs):
+        piece = result_ref[pl.ds(start, count), :].astype(BF)
+        if place % 2:
+            give_ref[place // 2 * count : (place // 2 + 1) * count, :] = piece
+        else:
+            keep_refs[place // 2][...] = piece
+
+
+def route_kernel(kv_ref, hidden_ref, gain_ref, router_ref, routes_ref, given_ref, *refs):
     piece_refs = refs[:-2]
     after_ref, out_ref = refs[-2:]
     count, model = after_ref.shape
     start = pl.multiple_of(kv_ref[0] * count, count)
-    total = piece_refs[0][...].astype(F32)
-    for piece_ref in piece_refs[1:]:
+    total = given_ref[:count, :].astype(F32)
+    for piece_ref in piece_refs:
         total = total + piece_ref[...].astype(F32)
     after = hidden_ref[pl.ds(start, count), :].astype(F32) + total
     after_ref[...] = after
@@ -392,8 +402,14 @@
 
     @pl.when(index == pl.num_programs(0) - 1)
     def _():
-        for place, out_ref in enumerate(out_refs):
-            out_ref[...] = mixed_ref[place * count : (place + 1) * count, :].astype(BF)
+        far = sources // 2
+        out_ref = iter(out_refs[:-1])
+        for place in range(sources):
+            piece = mixed_ref[place * count : (place + 1) * count, :].astype(BF)
+            if place < far and place % 2:
+                out_refs[-1][place // 2 * count : (place // 2 + 1) * count, :] = piece
+            else:
+                next(out_ref)[...] = piece
 
 
 def shards(
@@ -429,16 +445,13 @@
     scalar = pl.BlockSpec(memory_space=pltpu.SMEM)
     req_scalar = jnp.reshape(req_index, (1,)).astype(jnp.int32)
     far = pl.BlockSpec(memory_space=pltpu.HBM)
-    query, normed, cosines, sines = pl.pallas_call(
+    gain = attn_gain.reshape(-1, 128)
+    lengths = cache_len.reshape(sources, row_count)
+    query = pl.pallas_call(
         query_kernel,
-        out_shape=[
-            jax.ShapeDtypeStruct((row_count, heads * HD), BF),
-            jax.ShapeDtypeStruct((row_count, model), BF),
-            jax.ShapeDtypeStruct((row_count, 2 * HD), F32),
-            jax.ShapeDtypeStruct((row_count, 2 * HD), F32),
-        ],
+        out_shape=jax.ShapeDtypeStruct((row_count, heads * HD), BF),
         in_specs=[scalar] + [far] * 4,
-        out_specs=[vmem] * 4,
+        out_specs=vmem,
         scratch_shapes=[
             pltpu.VMEM((row_count, model), BF),
             pltpu.VMEM((model // 128, 128), F32),
@@ -449,16 +462,16 @@
         cost_estimate=cost(COSTS[0]),
         compiler_params=pltpu.CompilerParams(vmem_limit_bytes=QLIM << 20),
         name="query",
-    )(req_scalar, hidden_in, attn_gain.reshape(-1, 128), w_query, cache_len.reshape(sources, row_count))
+    )(req_scalar, hidden_in, gain, w_query, lengths)
     key_new, value_new = pl.pallas_call(
         fresh_kernel,
         out_shape=[jax.ShapeDtypeStruct((row_count, groups * HD), BF)] * 2,
-        in_specs=[vmem] * 5,
+        in_specs=[scalar] + [vmem] * 5,
         out_specs=[vmem] * 2,
         cost_estimate=cost(COSTS[1]),
         compiler_params=pltpu.CompilerParams(vmem_limit_bytes=8 << 20),
         name="fresh",
-    )(normed, w_key, w_value, cosines, sines)
+    )(req_scalar, hidden_in, gain, w_key, w_value, lengths)
     queries = gather_rows(query, "req")
 
     query_row, left, slot, local = pl.pallas_call(
@@ -474,7 +487,7 @@
         cost_estimate=cost(COSTS[6]),
         compiler_params=pltpu.CompilerParams(vmem_limit_bytes=8 << 20),
         name="places",
-    )(req_scalar, block_slot[None, :], cache_len.reshape(sources, row_count))
+    )(req_scalar, block_slot[None, :], lengths)
 
     def pairs(cache):
         cache = cache.reshape(blocks, groups, HD, 2 * HD).transpose(0, 2, 1, 3)
@@ -489,29 +502,33 @@
     token_count = row_count // kv_size
     projected = pl.pallas_call(
         functools.partial(merge_kernel, heads, groups, kv_size),
-        out_shape=[jax.ShapeDtypeStruct((token_count, model), BF)] * kv_size,
+        out_shape=[jax.ShapeDtypeStruct((token_count, model), BF)] * (kv_size // 2)
+        + [jax.ShapeDtypeStruct((kv_size // 2 * token_count, model), BF)],
         in_specs=[scalar] + [vmem] * (4 + sources),
-        out_specs=[vmem] * kv_size,
+        out_specs=[vmem] * (kv_size // 2 + 1),
         scratch_shapes=[pltpu.VMEM((row_count, model), F32)],
         compiler_params=pltpu.CompilerParams(vmem_limit_bytes=10 << 20),
         cost_estimate=cost(COSTS[3]),
         name="merge",
     )(kv_scalar, query, key_new, value_new, w_out, *parts)
+    given = swap(projected[-1], "kv", 1)
     pieces = [projected[0]]
-    for distance in range(1, kv_size):
-        pieces.append(swap(projected[distance], "kv", distance))
+    for place in range(1, kv_size // 2):
+        joined = given[place * token_count : (place + 1) * token_count].astype(F32)
+        joined = (projected[place].astype(F32) + joined).astype(BF)
+        pieces.append(swap(joined, "kv", 2 * place))
     after_attn, outgoing = pl.pallas_call(
         route_kernel,
         out_shape=[
             jax.ShapeDtypeStruct((token_count, model), F32),
             jax.ShapeDtypeStruct((token_count, model + 128), BF),
         ],
-        in_specs=[scalar] + [vmem] * (4 + kv_size),
+        in_specs=[scalar] + [vmem] * (5 + kv_size // 2),
         out_specs=[vmem, vmem],
         compiler_params=pltpu.CompilerParams(vmem_limit_bytes=10 << 20),
         cost_estimate=cost(COSTS[4]),
         name="route",
-    )(kv_scalar, hidden_in, moe_gain.reshape(-1, 128), w_router, routes, *pieces)
+    )(kv_scalar, hidden_in, moe_gain.reshape(-1, 128), w_router, routes, given, *pieces)
     arrived = gather_rows(outgoing, "req")
     local_experts = w_gate_up.shape[0]
     if STAGE:
@@ -525,17 +542,19 @@
             compiler_params=pltpu.CompilerParams(vmem_limit_bytes=SLIM << 20),
             name="stage",
         )(outgoing, w_gate_up)
+    single = [distance for distance in range(sources) if distance % 2 == 0 or distance > sources // 2]
     mixed = pl.pallas_call(
         functools.partial(expert_kernel, sources, w_router.shape[1]),
         grid=(local_experts,),
-        out_shape=[jax.ShapeDtypeStruct((token_count, model), BF)] * sources,
+        out_shape=[jax.ShapeDtypeStruct((token_count, model), BF)] * len(single)
+        + [jax.ShapeDtypeStruct((sources // 4 * token_count, model), BF)],
         in_specs=[scalar]
         + [vmem] * sources
         + [
             pl.BlockSpec((1,) + w_gate_up.shape[1:], lambda i: (i, 0, 0)),
             pl.BlockSpec((1,) + w_down.shape[1:], lambda i: (i, 0, 0)),
         ],
-        out_specs=[vmem] * sources,
+        out_specs=[vmem] * (len(single) + 1),
         scratch_shapes=[
             pltpu.VMEM((sources * token_count, model + 128), BF),
             pltpu.VMEM((sources * token_count, model), F32),
@@ -544,7 +563,7 @@
         cost_estimate=cost(COSTS[5]),
         name="experts",
     )(req_scalar, *arrived, w_gate_up, w_down)
-    mixture = sum_rows(mixed, "req")
+    mixture = sum_rows(dict(zip(single, mixed)), mixed[-1], "req")
     return (after_attn + mixture).astype(BF)
 
 

time: 92.1 us -> 88.4 us (0.960)
  starting transfers between devices: 41.5 us -> 38.1 us
  Pallas kernels: 19.6 us -> 18.4 us
    ppermute x31 -> x29, starting transfers between devices: 41.5 us -> 38.1 us  [swap(): lax.ppermute(value, axis, [(source, source ^ distance) for source in rang...]
    pallas_call x1, Pallas kernels: 9.71 us -> 8.43 us  [attend(): pl.pallas_call(functools.partial(attend_kernel, heads, groups, chunk, len...]
    ppermute x31 -> x29, waiting for transfers between devices: 26.5 us -> 27.3 us  [swap(): lax.ppermute(value, axis, [(source, source ^ distance) for source in rang...]
    unnamed x44 -> x40, local copies, waits for them, and re-layouts: 3.18 us -> 3.17 us
  transfers between devices with their start and end apart: 31 -> 29, of which waited for: 14 -> 16; matrix products, arithmetic and copies ran while one was open for 0% -> 0% of each run, Pallas kernels for 2% -> 2%
where the time goes in v4:
time: 88.4 us; the launch traced here: 88.2 us
  starting transfers between devices  38.1 us (43%)
  waiting for transfers between devices  27.3 us (31%)
  Pallas kernels  18.4 us (21%)
  local copies, waits for them, and re-layouts  3.17 us (4%)
    ppermute x29, starting transfers between devices, swap(): lax.ppermute(value, axis, [(source, source ^ distance) for source in rang...  38.1 us
    ppermute x29, waiting for transfers between devices, swap(): lax.ppermute(value, axis, [(source, source ^ distance) for source in rang...  27.3 us
    pallas_call x1, Pallas kernels, attend(): pl.pallas_call(functools.partial(attend_kernel, heads, groups, chunk, len...  8.43 us
    pallas_call x1, Pallas kernels, shards(): pl.pallas_call(functools.partial(expert_kernel, sources, w_router.shape[1...  3.35 us
    unnamed x40, local copies, waits for them, and re-layouts  3.17 us
    pallas_call x1, Pallas kernels, shards(): pl.pallas_call(query_kernel, out_shape=jax.ShapeDtypeStruct((row_count, h...  2.72 us
  transfers between devices with their start and end apart: 29, of which 16 were waited for; matrix products, arithmetic and copies ran while one was open for 0% of the time, Pallas kernels for 2%

profile of v4, /device:TPU:0, one launch (start us, length us, event | category | flops | bytes accessed | tf_op | source)
XLA Modules:
  0.0 88.2 jit_solution(16294046497557095046)
XLA Ops:
  0.0 2.7 %query.1.refs_4_.refs_1_ = bf16[128,384]{1,0:T(8,128)(2,1)} custom-call(s32[1]{0:T(128)} %bitcast.2.req_ref, bf16[128,1536]{1,0:T(8,128)(2,1)} %hidden_ref.3, f32[12,128]{1,0:T(8,128)} %bitcast.21, bf16[384,1536]{1,0:T(8,128)(2,1)} %weight_hbm.1, s32[8,128]{1,0:T(8,128)} %bitcast.24), custom_call_target="tpu_custom_call" | custom-call | flops 12000000000 | bytes 36000000 | tf_op jit(solution)/shard_map/query/pallas_call | solution.py:450
  2.7 5.1 %collective-permute-start.5 = (bf16[128,384]{1,0:T(8,128)(2,1)}, bf16[128,384]{1,0:T(8,128)(2,1)S(1)}, u32[]{:S(2)}, u32[]{:S(2)}) collective-permute-start(bf16[128,384]{1,0:T(8,128)(2,1)} %query.1.refs_4_.refs_1_), channel_id=1, source_target_pairs={{0,24},{4,28},{8,16},{12,20},{16,8},{20,12},{24,0},{28,4},{1,25},{... | collective-permute-start | bytes 294920 | tf_op jit(solution)/shard_map/ppermute | solution.py:32
  7.9 1.7 %collective-permute-start.2 = (bf16[128,384]{1,0:T(8,128)(2,1)}, bf16[128,384]{1,0:T(8,128)(2,1)S(1)}, u32[]{:S(2)}, u32[]{:S(2)}) collective-permute-start(bf16[128,384]{1,0:T(8,128)(2,1)} %query.1.refs_4_.refs_1_), channel_id=1, source_target_pairs={{0,12},{4,8},{8,4},{12,0},{16,28},{20,24},{24,20},{28,16},{1,13},{... | collective-permute-start | bytes 294920 | tf_op jit(solution)/shard_map/ppermute | solution.py:32
  9.6 1.2 %collective-permute-start.1 = (bf16[128,384]{1,0:T(8,128)(2,1)}, bf16[128,384]{1,0:T(8,128)(2,1)S(1)}, u32[]{:S(2)}, u32[]{:S(2)}) collective-permute-start(bf16[128,384]{1,0:T(8,128)(2,1)} %query.1.refs_4_.refs_1_), channel_id=1, source_target_pairs={{0,8},{4,12},{8,0},{12,4},{16,24},{20,28},{24,16},{28,20},{1,9},{5... | collective-permute-start | bytes 294920 | tf_op jit(solution)/shard_map/ppermute | solution.py:32
  11.8 1.5 %collective-permute-start.6 = (bf16[128,384]{1,0:T(8,128)(2,1)S(1)}, bf16[128,384]{1,0:T(8,128)(2,1)S(1)}, u32[]{:S(2)}, u32[]{:S(2)}) collective-permute-start(bf16[128,384]{1,0:T(8,128)(2,1)S(1)} %collective-permute-done.5.refs_10_), channel_id=1, source_target_pairs={{0,4},{4,0},{8,12},{12,8},{16,20},{20,16},{24,28},{28,24},{1,5},{5... | collective-permute-start | bytes 294920 | tf_op jit(solution)/shard_map/ppermute | solution.py:32
  13.2 3.2 %collective-permute-done.3.refs_8_ = bf16[128,384]{1,0:T(8,128)(2,1)S(1)} collective-permute-done((bf16[128,384]{1,0:T(8,128)(2,1)}, bf16[128,384]{1,0:T(8,128)(2,1)S(1)}, u32[]{:S(2)}, u32[]{:S(2)}) %collective-permute-start.3) | collective-permute-done | bytes 98336 | tf_op jit(solution)/shard_map/ppermute | solution.py:32
  16.4 1.5 %collective-permute-start.4 = (bf16[128,384]{1,0:T(8,128)(2,1)S(1)}, bf16[128,384]{1,0:T(8,128)(2,1)S(1)}, u32[]{:S(2)}, u32[]{:S(2)}) collective-permute-start(bf16[128,384]{1,0:T(8,128)(2,1)S(1)} %collective-permute-done.3.refs_8_), channel_id=1, source_target_pairs={{0,4},{4,0},{8,12},{12,8},{16,20},{20,16},{24,28},{28,24},{1,5},{5... | collective-permute-start | bytes 294920 | tf_op jit(solution)/shard_map/ppermute | solution.py:32
  18.8 2.3 %collective-permute-done.4.refs_9_ = bf16[128,384]{1,0:T(8,128)(2,1)S(1)} collective-permute-done((bf16[128,384]{1,0:T(8,128)(2,1)S(1)}, bf16[128,384]{1,0:T(8,128)(2,1)S(1)}, u32[]{:S(2)}, u32[]{:S(2)}) %collective-permute-start.4) | collective-permute-done | bytes 98336 | tf_op jit(solution)/shard_map/ppermute | solution.py:32
  21.2 8.4 %attend.1 = (bf16[48,512]{1,0:T(8,128)(2,1)S(1)}, bf16[48,512]{1,0:T(8,128)(2,1)S(1)}, bf16[48,512]{1,0:T(8,128)(2,1)S(1)}, bf16[48,512]{1,0:T(8,128)(2,1)S(1)},...) custom-call(s32[384,1]{1,0:T(8,128)S(1)} %get-tuple-element.33.refs_, ...), custom_call_target="tpu_custom_call" | custom-call | flops 12000000000 | bytes 36000000 | tf_op jit(solution)/shard_map/attend/pallas_call | solution.py:268
  29.6 3.5 %collective-permute-start.7 = (bf16[48,512]{1,0:T(8,128)(2,1)S(1)}, bf16[48,512]{1,0:T(8,128)(2,1)S(1)}, u32[]{:S(2)}, u32[]{:S(2)}) collective-permute-start(bf16[48,512]{1,0:T(8,128)(2,1)S(1)} %get-tuple-element.37), channel_id=1, source_target_pairs={{0,28},{4,24},{8,20},{12,16},{16,12},{20,8},{24,4},{28,0},{1,29},{... | collective-permute-start | bytes 147464 | tf_op jit(solution)/shard_map/ppermute | solution.py:32
  33.1 1.4 %collective-permute-start.8 = (bf16[48,512]{1,0:T(8,128)(2,1)S(1)}, bf16[48,512]{1,0:T(8,128)(2,1)S(1)}, u32[]{:S(2)}, u32[]{:S(2)}) collective-permute-start(bf16[48,512]{1,0:T(8,128)(2,1)S(1)} %get-tuple-element.38), channel_id=1, source_target_pairs={{0,24},{4,28},{8,16},{12,20},{16,8},{20,12},{24,0},{28,4},{1,25},{... | collective-permute-start | bytes 147464 | tf_op jit(solution)/shard_map/ppermute | solution.py:32
  34.6 2.8 %collective-permute-start.10 = (bf16[48,512]{1,0:T(8,128)(2,1)S(1)}, bf16[48,512]{1,0:T(8,128)(2,1)S(1)}, u32[]{:S(2)}, u32[]{:S(2)}) collective-permute-start(bf16[48,512]{1,0:T(8,128)(2,1)S(1)} %get-tuple-element.40), channel_id=1, source_target_pairs={{0,16},{4,20},{8,24},{12,28},{16,0},{20,4},{24,8},{28,12},{1,17},{... | collective-permute-start | bytes 147464 | tf_op jit(solution)/shard_map/ppermute | solution.py:32
  37.3 1.0 %collective-permute-start.11 = (bf16[48,512]{1,0:T(8,128)(2,1)S(1)}, bf16[48,512]{1,0:T(8,128)(2,1)S(1)}, u32[]{:S(2)}, u32[]{:S(2)}) collective-permute-start(bf16[48,512]{1,0:T(8,128)(2,1)S(1)} %get-tuple-element.41), channel_id=1, source_target_pairs={{0,12},{4,8},{8,4},{12,0},{16,28},{20,24},{24,20},{28,16},{1,13},{... | collective-permute-start | bytes 147464 | tf_op jit(solution)/shard_map/ppermute | solution.py:32
  38.4 1.9 %collective-permute-start.12 = (bf16[48,512]{1,0:T(8,128)(2,1)S(1)}, bf16[48,512]{1,0:T(8,128)(2,1)S(1)}, u32[]{:S(2)}, u32[]{:S(2)}) collective-permute-start(bf16[48,512]{1,0:T(8,128)(2,1)S(1)} %get-tuple-element.42), channel_id=1, source_target_pairs={{0,8},{4,12},{8,0},{12,4},{16,24},{20,28},{24,16},{28,20},{1,9},{5... | collective-permute-start | bytes 147464 | tf_op jit(solution)/shard_map/ppermute | solution.py:32
  42.9 1.5 %collective-permute-done.13.refs_11_ = bf16[48,512]{1,0:T(8,128)(2,1)S(1)} collective-permute-done((bf16[48,512]{1,0:T(8,128)(2,1)S(1)}, bf16[48,512]{1,0:T(8,128)(2,1)S(1)}, u32[]{:S(2)}, u32[]{:S(2)}) %collective-permute-start.13) | collective-permute-done | bytes 49184 | tf_op jit(solution)/shard_map/ppermute | solution.py:32
  44.4 1.5 %merge.1 = (bf16[32,1536]{1,0:T(8,128)(2,1)S(1)}, bf16[32,1536]{1,0:T(8,128)(2,1)S(1)}, bf16[64,1536]{1,0:T(8,128)(2,1)S(1)}) custom-call(s32[1]{0:T(128)} %bitcast.refs_0_.kv_ref, bf16[128,384]{1,0:T(8,128)(2,1)S(1)} %copy-done.6, bf16[128,128]{1,0:T(8,128)(2,1)S(1)} %get-tuple-element.31.refs_2_, bf16[128,128]{1,0:T(8,128)(2,1)S(1)} %get-tuple-element.32.refs_3_, ...), custom_call_target="tpu_custom_call" | custom-call | flops 12000000000 | bytes 36000000 | tf_op jit(solution)/shard_map/merge/pallas_call | solution.py:503
  46.0 1.4 %collective-permute-done.14.given_ref = bf16[64,1536]{1,0:T(8,128)(2,1)S(1)} collective-permute-done((bf16[64,1536]{1,0:T(8,128)(2,1)S(1)}, bf16[64,1536]{1,0:T(8,128)(2,1)S(1)}, u32[]{:S(2)}, u32[]{:S(2)}) %collective-permute-start.14) | collective-permute-done | bytes 196640 | tf_op jit(solution)/shard_map/ppermute | solution.py:32
  47.4 1.6 %collective-permute-start.15 = (bf16[32,1536]{1,0:T(8,128)(2,1)S(1)}, bf16[32,1536]{1,0:T(8,128)(2,1)S(1)}, u32[]{:S(2)}, u32[]{:S(2)}) collective-permute-start(bf16[32,1536]{1,0:T(8,128)(2,1)S(1)} %add_convert_fusion.4), channel_id=1, source_target_pairs={{0,2},{1,3},{2,0},{3,1},{4,6},{5,7},{6,4},{7,5},{8,10},{9,11},{10,... | collective-permute-start | bytes 294920 | tf_op jit(solution)/shard_map/ppermute | solution.py:32
  49.3 3.0 %collective-permute-done.15.refs_1_ = bf16[32,1536]{1,0:T(8,128)(2,1)S(1)} collective-permute-done((bf16[32,1536]{1,0:T(8,128)(2,1)S(1)}, bf16[32,1536]{1,0:T(8,128)(2,1)S(1)}, u32[]{:S(2)}, u32[]{:S(2)}) %collective-permute-start.15) | collective-permute-done | bytes 98336 | tf_op jit(solution)/shard_map/ppermute | solution.py:32
  52.9 2.5 %collective-permute-start.21 = (bf16[32,1664]{1,0:T(8,128)(2,1)S(1)}, bf16[32,1664]{1,0:T(8,128)(2,1)S(1)}, u32[]{:S(2)}, u32[]{:S(2)}) collective-permute-start(bf16[32,1664]{1,0:T(8,128)(2,1)S(1)} %get-tuple-element.49.order_ref.refs_0_), channel_id=1, source_target_pairs={{0,24},{4,28},{8,16},{12,20},{16,8},{20,12},{24,0},{28,4},{1,25},{... | collective-permute-start | bytes 319496 | tf_op jit(solution)/shard_map/ppermute | solution.py:32
  55.4 1.9 %collective-permute-start.18 = (bf16[32,1664]{1,0:T(8,128)(2,1)S(1)}, bf16[32,1664]{1,0:T(8,128)(2,1)S(1)}, u32[]{:S(2)}, u32[]{:S(2)}) collective-permute-start(bf16[32,1664]{1,0:T(8,128)(2,1)S(1)} %get-tuple-element.49.order_ref.refs_0_), channel_id=1, source_target_pairs={{0,12},{4,8},{8,4},{12,0},{16,28},{20,24},{24,20},{28,16},{1,13},{... | collective-permute-start | bytes 319496 | tf_op jit(solution)/shard_map/ppermute | solution.py:32
  57.4 1.5 %collective-permute-start.16 = (bf16[32,1664]{1,0:T(8,128)(2,1)S(1)}, bf16[32,1664]{1,0:T(8,128)(2,1)S(1)}, u32[]{:S(2)}, u32[]{:S(2)}) collective-permute-start(bf16[32,1664]{1,0:T(8,128)(2,1)S(1)} %get-tuple-element.49.order_ref.refs_0_), channel_id=1, source_target_pairs={{0,4},{4,0},{8,12},{12,8},{16,20},{20,16},{24,28},{28,24},{1,5},{5... | collective-permute-start | bytes 319496 | tf_op jit(solution)/shard_map/ppermute | solution.py:32
  58.9 1.7 %collective-permute-done.21.refs_6_ = bf16[32,1664]{1,0:T(8,128)(2,1)S(1)} collective-permute-done((bf16[32,1664]{1,0:T(8,128)(2,1)S(1)}, bf16[32,1664]{1,0:T(8,128)(2,1)S(1)}, u32[]{:S(2)}, u32[]{:S(2)}) %collective-permute-start.21) | collective-permute-done | bytes 106528 | tf_op jit(solution)/shard_map/ppermute | solution.py:32
  60.8 3.2 %collective-permute-done.19.refs_4_ = bf16[32,1664]{1,0:T(8,128)(2,1)S(1)} collective-permute-done((bf16[32,1664]{1,0:T(8,128)(2,1)S(1)}, bf16[32,1664]{1,0:T(8,128)(2,1)S(1)}, u32[]{:S(2)}, u32[]{:S(2)}) %collective-permute-start.19) | collective-permute-done | bytes 106528 | tf_op jit(solution)/shard_map/ppermute | solution.py:32
  64.6 2.8 %copy-done = bf16[2,1536,1024]{2,1,0:T(8,128)(2,1)S(1)} copy-done((bf16[2,1536,1024]{2,1,0:T(8,128)(2,1)S(1)}, bf16[2,1536,1024]{2,1,0:T(8,128)(2,1)}, u32[]{:S(2)}) %copy-start) | copy-done | bytes 6291480
  68.7 3.3 %experts.1 = (bf16[32,1536]{1,0:T(8,128)(2,1)S(1)}, bf16[32,1536]{1,0:T(8,128)(2,1)S(1)}, bf16[32,1536]{1,0:T(8,128)(2,1)S(1)}, bf16[32,1536]{1,0:T(8,128)(2,1)S...) custom-call(s32[1]{0:T(128)} %bitcast.2.req_ref, ...), custom_call_target="tpu_custom_call" | custom-call | flops 4000000000 | bytes 12000000 | tf_op jit(solution)/shard_map/experts/pallas_call | solution.py:546
  72.8 1.4 %collective-permute-start.26 = (bf16[32,1536]{1,0:T(8,128)(2,1)S(1)}, bf16[32,1536]{1,0:T(8,128)(2,1)S(1)}, u32[]{:S(2)}, u32[]{:S(2)}) collective-permute-start(bf16[32,1536]{1,0:T(8,128)(2,1)S(1)} %get-tuple-element.55), channel_id=1, source_target_pairs={{0,4},{4,0},{8,12},{12,8},{16,20},{20,16},{24,28},{28,24},{1,5},{5... | collective-permute-start | bytes 294920 | tf_op jit(solution)/shard_map/ppermute | solution.py:32
  74.8 3.0 %collective-permute-done.24 = bf16[32,1536]{1,0:T(8,128)(2,1)S(1)} collective-permute-done((bf16[32,1536]{1,0:T(8,128)(2,1)S(1)}, bf16[32,1536]{1,0:T(8,128)(2,1)S(1)}, u32[]{:S(2)}, u32[]{:S(2)}) %collective-permute-start.24) | collective-permute-done | bytes 98336 | tf_op jit(solution)/shard_map/ppermute | solution.py:32
  77.8 1.4 %collective-permute-start.25 = (bf16[32,1536]{1,0:T(8,128)(2,1)S(1)}, bf16[32,1536]{1,0:T(8,128)(2,1)S(1)}, u32[]{:S(2)}, u32[]{:S(2)}) collective-permute-start(bf16[32,1536]{1,0:T(8,128)(2,1)S(1)} %add_convert_fusion.3), channel_id=1, source_target_pairs={{0,16},{4,20},{8,24},{12,28},{16,0},{20,4},{24,8},{28,12},{1,17},{... | collective-permute-start | bytes 294920 | tf_op jit(solution)/shard_map/ppermute | solution.py:32
  79.8 2.4 %collective-permute-start.27 = (bf16[32,1536]{1,0:T(8,128)(2,1)S(1)}, bf16[32,1536]{1,0:T(8,128)(2,1)S(1)}, u32[]{:S(2)}, u32[]{:S(2)}) collective-permute-start(bf16[32,1536]{1,0:T(8,128)(2,1)S(1)} %add_convert_fusion.2), channel_id=1, source_target_pairs={{0,24},{4,28},{8,16},{12,20},{16,8},{20,12},{24,0},{28,4},{1,25},{... | collective-permute-start | bytes 294920 | tf_op jit(solution)/shard_map/ppermute | solution.py:32
  82.7 1.8 %collective-permute-done.25 = bf16[32,1536]{1,0:T(8,128)(2,1)S(1)} collective-permute-done((bf16[32,1536]{1,0:T(8,128)(2,1)S(1)}, bf16[32,1536]{1,0:T(8,128)(2,1)S(1)}, u32[]{:S(2)}, u32[]{:S(2)}) %collective-permute-start.25) | collective-permute-done | bytes 98336 | tf_op jit(solution)/shard_map/ppermute | solution.py:32
  84.5 1.9 %collective-permute-done.27 = bf16[32,1536]{1,0:T(8,128)(2,1)S(1)} collective-permute-done((bf16[32,1536]{1,0:T(8,128)(2,1)S(1)}, bf16[32,1536]{1,0:T(8,128)(2,1)S(1)}, u32[]{:S(2)}, u32[]{:S(2)}) %collective-permute-start.27) | collective-permute-done | bytes 98336 | tf_op jit(solution)/shard_map/ppermute | solution.py:32
  (82 shorter events, 11.7 us)
Async XLA Ops:
  2.7 9.0 %collective-permute-start.5 = (bf16[128,384]{1,0:T(8,128)(2,1)}, bf16[128,384]{1,0:T(8,128)(2,1)S(1)}, u32[]{:S(2)}, u32[]{:S(2)}) collective-permute-start(bf16[128,384]{1,0:T(8,128)(2,1)} %query.1.refs_4_.refs_1_), channel_id=1, source_target_pairs={{0,24},{4,28},{8,16},{12,20},{16,8},{20,12},{24,0},{28,4},{1,25},{... | collective-permute-start | bytes 294920 | tf_op jit(solution)/shard_map/ppermute | solution.py:32
  7.8 8.6 %collective-permute-start.3 = (bf16[128,384]{1,0:T(8,128)(2,1)}, bf16[128,384]{1,0:T(8,128)(2,1)S(1)}, u32[]{:S(2)}, u32[]{:S(2)}) collective-permute-start(bf16[128,384]{1,0:T(8,128)(2,1)} %query.1.refs_4_.refs_1_), channel_id=1, source_target_pairs={{0,16},{4,20},{8,24},{12,28},{16,0},{20,4},{24,8},{28,12},{1,17},{... | collective-permute-start | bytes 294920 | tf_op jit(solution)/shard_map/ppermute | solution.py:32
  7.9 10.9 %collective-permute-start.2 = (bf16[128,384]{1,0:T(8,128)(2,1)}, bf16[128,384]{1,0:T(8,128)(2,1)S(1)}, u32[]{:S(2)}, u32[]{:S(2)}) collective-permute-start(bf16[128,384]{1,0:T(8,128)(2,1)} %query.1.refs_4_.refs_1_), channel_id=1, source_target_pairs={{0,12},{4,8},{8,4},{12,0},{16,28},{20,24},{24,20},{28,16},{1,13},{... | collective-permute-start | bytes 294920 | tf_op jit(solution)/shard_map/ppermute | solution.py:32
  9.6 9.2 %collective-permute-start.1 = (bf16[128,384]{1,0:T(8,128)(2,1)}, bf16[128,384]{1,0:T(8,128)(2,1)S(1)}, u32[]{:S(2)}, u32[]{:S(2)}) collective-permute-start(bf16[128,384]{1,0:T(8,128)(2,1)} %query.1.refs_4_.refs_1_), channel_id=1, source_target_pairs={{0,8},{4,12},{8,0},{12,4},{16,24},{20,28},{24,16},{28,20},{1,9},{5... | collective-permute-start | bytes 294920 | tf_op jit(solution)/shard_map/ppermute | solution.py:32
  10.8 7.9 %collective-permute-start = (bf16[128,384]{1,0:T(8,128)(2,1)}, bf16[128,384]{1,0:T(8,128)(2,1)S(1)}, u32[]{:S(2)}, u32[]{:S(2)}) collective-permute-start(bf16[128,384]{1,0:T(8,128)(2,1)} %query.1.refs_4_.refs_1_), channel_id=1, source_target_pairs={{0,4},{4,0},{8,12},{12,8},{16,20},{20,16},{24,28},{28,24},{1,5},{5... | collective-permute-start | bytes 294920 | tf_op jit(solution)/shard_map/ppermute | solution.py:32
  11.8 7.0 %collective-permute-start.6 = (bf16[128,384]{1,0:T(8,128)(2,1)S(1)}, bf16[128,384]{1,0:T(8,128)(2,1)S(1)}, u32[]{:S(2)}, u32[]{:S(2)}) collective-permute-start(bf16[128,384]{1,0:T(8,128)(2,1)S(1)} %collective-permute-done.5.refs_10_), channel_id=1, source_target_pairs={{0,4},{4,0},{8,12},{12,8},{16,20},{20,16},{24,28},{28,24},{1,5},{5... | collective-permute-start | bytes 294920 | tf_op jit(solution)/shard_map/ppermute | solution.py:32
  16.4 4.6 %collective-permute-start.4 = (bf16[128,384]{1,0:T(8,128)(2,1)S(1)}, bf16[128,384]{1,0:T(8,128)(2,1)S(1)}, u32[]{:S(2)}, u32[]{:S(2)}) collective-permute-start(bf16[128,384]{1,0:T(8,128)(2,1)S(1)} %collective-permute-done.3.refs_8_), channel_id=1, source_target_pairs={{0,4},{4,0},{8,12},{12,8},{16,20},{20,16},{24,28},{28,24},{1,5},{5... | collective-permute-start | bytes 294920 | tf_op jit(solution)/shard_map/ppermute | solution.py:32
  21.1 19.7 %copy-start.3 = (bf16[128,1536]{1,0:T(8,128)(2,1)S(1)}, bf16[128,1536]{1,0:T(8,128)(2,1)}, u32[]{:S(2)}) copy-start(bf16[128,1536]{1,0:T(8,128)(2,1)} %key_weight_ref.1) | copy-start | bytes 1179652
  21.1 19.7 %copy-start.4 = (bf16[128,1536]{1,0:T(8,128)(2,1)S(1)}, bf16[128,1536]{1,0:T(8,128)(2,1)}, u32[]{:S(2)}) copy-start(bf16[128,1536]{1,0:T(8,128)(2,1)} %value_weight_ref.1) | copy-start | bytes 1179652
  21.2 23.2 %copy-start.2 = (bf16[384,1536]{1,0:T(8,128)(2,1)S(1)}, bf16[384,1536]{1,0:T(8,128)(2,1)}, u32[]{:S(2)}) copy-start(bf16[384,1536]{1,0:T(8,128)(2,1)} %refs_4_.1) | copy-start | bytes 3538948
  29.6 8.8 %collective-permute-start.7 = (bf16[48,512]{1,0:T(8,128)(2,1)S(1)}, bf16[48,512]{1,0:T(8,128)(2,1)S(1)}, u32[]{:S(2)}, u32[]{:S(2)}) collective-permute-start(bf16[48,512]{1,0:T(8,128)(2,1)S(1)} %get-tuple-element.37), channel_id=1, source_target_pairs={{0,28},{4,24},{8,20},{12,16},{16,12},{20,8},{24,4},{28,0},{1,29},{... | collective-permute-start | bytes 147464 | tf_op jit(solution)/shard_map/ppermute | solution.py:32
  33.1 7.2 %collective-permute-start.8 = (bf16[48,512]{1,0:T(8,128)(2,1)S(1)}, bf16[48,512]{1,0:T(8,128)(2,1)S(1)}, u32[]{:S(2)}, u32[]{:S(2)}) collective-permute-start(bf16[48,512]{1,0:T(8,128)(2,1)S(1)} %get-tuple-element.38), channel_id=1, source_target_pairs={{0,24},{4,28},{8,16},{12,20},{16,8},{20,12},{24,0},{28,4},{1,25},{... | collective-permute-start | bytes 147464 | tf_op jit(solution)/shard_map/ppermute | solution.py:32
  34.4 7.0 %collective-permute-start.9 = (bf16[48,512]{1,0:T(8,128)(2,1)S(1)}, bf16[48,512]{1,0:T(8,128)(2,1)S(1)}, u32[]{:S(2)}, u32[]{:S(2)}) collective-permute-start(bf16[48,512]{1,0:T(8,128)(2,1)S(1)} %get-tuple-element.39), channel_id=1, source_target_pairs={{0,20},{4,16},{8,28},{12,24},{16,4},{20,0},{24,12},{28,8},{1,21},{... | collective-permute-start | bytes 147464 | tf_op jit(solution)/shard_map/ppermute | solution.py:32
  34.6 6.9 %collective-permute-start.10 = (bf16[48,512]{1,0:T(8,128)(2,1)S(1)}, bf16[48,512]{1,0:T(8,128)(2,1)S(1)}, u32[]{:S(2)}, u32[]{:S(2)}) collective-permute-start(bf16[48,512]{1,0:T(8,128)(2,1)S(1)} %get-tuple-element.40), channel_id=1, source_target_pairs={{0,16},{4,20},{8,24},{12,28},{16,0},{20,4},{24,8},{28,12},{1,17},{... | collective-permute-start | bytes 147464 | tf_op jit(solution)/shard_map/ppermute | solution.py:32
  37.3 5.0 %collective-permute-start.11 = (bf16[48,512]{1,0:T(8,128)(2,1)S(1)}, bf16[48,512]{1,0:T(8,128)(2,1)S(1)}, u32[]{:S(2)}, u32[]{:S(2)}) collective-permute-start(bf16[48,512]{1,0:T(8,128)(2,1)S(1)} %get-tuple-element.41), channel_id=1, source_target_pairs={{0,12},{4,8},{8,4},{12,0},{16,28},{20,24},{24,20},{28,16},{1,13},{... | collective-permute-start | bytes 147464 | tf_op jit(solution)/shard_map/ppermute | solution.py:32
  38.4 4.5 %collective-permute-start.12 = (bf16[48,512]{1,0:T(8,128)(2,1)S(1)}, bf16[48,512]{1,0:T(8,128)(2,1)S(1)}, u32[]{:S(2)}, u32[]{:S(2)}) collective-permute-start(bf16[48,512]{1,0:T(8,128)(2,1)S(1)} %get-tuple-element.42), channel_id=1, source_target_pairs={{0,8},{4,12},{8,0},{12,4},{16,24},{20,28},{24,16},{28,20},{1,9},{5... | collective-permute-start | bytes 147464 | tf_op jit(solution)/shard_map/ppermute | solution.py:32
  40.3 4.1 %collective-permute-start.13 = (bf16[48,512]{1,0:T(8,128)(2,1)S(1)}, bf16[48,512]{1,0:T(8,128)(2,1)S(1)}, u32[]{:S(2)}, u32[]{:S(2)}) collective-permute-start(bf16[48,512]{1,0:T(8,128)(2,1)S(1)} %get-tuple-element.43), channel_id=1, source_target_pairs={{0,4},{4,0},{8,12},{12,8},{16,20},{20,16},{24,28},{28,24},{1,5},{5... | collective-permute-start | bytes 147464 | tf_op jit(solution)/shard_map/ppermute | solution.py:32
  45.9 1.5 %collective-permute-start.14 = (bf16[64,1536]{1,0:T(8,128)(2,1)S(1)}, bf16[64,1536]{1,0:T(8,128)(2,1)S(1)}, u32[]{:S(2)}, u32[]{:S(2)}) collective-permute-start(bf16[64,1536]{1,0:T(8,128)(2,1)S(1)} %get-tuple-element.45), channel_id=1, source_target_pairs={{0,1},{1,0},{2,3},{3,2},{4,5},{5,4},{6,7},{7,6},{8,9},{9,8},{10,11... | collective-permute-start | bytes 589832 | tf_op jit(solution)/shard_map/ppermute | solution.py:32
  47.4 4.9 %collective-permute-start.15 = (bf16[32,1536]{1,0:T(8,128)(2,1)S(1)}, bf16[32,1536]{1,0:T(8,128)(2,1)S(1)}, u32[]{:S(2)}, u32[]{:S(2)}) collective-permute-start(bf16[32,1536]{1,0:T(8,128)(2,1)S(1)} %add_convert_fusion.4), channel_id=1, source_target_pairs={{0,2},{1,3},{2,0},{3,1},{4,6},{5,7},{6,4},{7,5},{8,10},{9,11},{10,... | collective-permute-start | bytes 294920 | tf_op jit(solution)/shard_map/ppermute | solution.py:32
  52.9 7.7 %collective-permute-start.21 = (bf16[32,1664]{1,0:T(8,128)(2,1)S(1)}, bf16[32,1664]{1,0:T(8,128)(2,1)S(1)}, u32[]{:S(2)}, u32[]{:S(2)}) collective-permute-start(bf16[32,1664]{1,0:T(8,128)(2,1)S(1)} %get-tuple-element.49.order_ref.refs_0_), channel_id=1, source_target_pairs={{0,24},{4,28},{8,16},{12,20},{16,8},{20,12},{24,0},{28,4},{1,25},{... | collective-permute-start | bytes 319496 | tf_op jit(solution)/shard_map/ppermute | solution.py:32
  55.4 8.6 %collective-permute-start.19 = (bf16[32,1664]{1,0:T(8,128)(2,1)S(1)}, bf16[32,1664]{1,0:T(8,128)(2,1)S(1)}, u32[]{:S(2)}, u32[]{:S(2)}) collective-permute-start(bf16[32,1664]{1,0:T(8,128)(2,1)S(1)} %get-tuple-element.49.order_ref.refs_0_), channel_id=1, source_target_pairs={{0,16},{4,20},{8,24},{12,28},{16,0},{20,4},{24,8},{28,12},{1,17},{... | collective-permute-start | bytes 319496 | tf_op jit(solution)/shard_map/ppermute | solution.py:32
  55.4 12.4 %collective-permute-start.18 = (bf16[32,1664]{1,0:T(8,128)(2,1)S(1)}, bf16[32,1664]{1,0:T(8,128)(2,1)S(1)}, u32[]{:S(2)}, u32[]{:S(2)}) collective-permute-start(bf16[32,1664]{1,0:T(8,128)(2,1)S(1)} %get-tuple-element.49.order_ref.refs_0_), channel_id=1, source_target_pairs={{0,12},{4,8},{8,4},{12,0},{16,28},{20,24},{24,20},{28,16},{1,13},{... | collective-permute-start | bytes 319496 | tf_op jit(solution)/shard_map/ppermute | solution.py:32
  57.3 10.5 %collective-permute-start.17 = (bf16[32,1664]{1,0:T(8,128)(2,1)S(1)}, bf16[32,1664]{1,0:T(8,128)(2,1)S(1)}, u32[]{:S(2)}, u32[]{:S(2)}) collective-permute-start(bf16[32,1664]{1,0:T(8,128)(2,1)S(1)} %get-tuple-element.49.order_ref.refs_0_), channel_id=1, source_target_pairs={{0,8},{4,12},{8,0},{12,4},{16,24},{20,28},{24,16},{28,20},{1,9},{5... | collective-permute-start | bytes 319496 | tf_op jit(solution)/shard_map/ppermute | solution.py:32
  57.4 10.4 %collective-permute-start.16 = (bf16[32,1664]{1,0:T(8,128)(2,1)S(1)}, bf16[32,1664]{1,0:T(8,128)(2,1)S(1)}, u32[]{:S(2)}, u32[]{:S(2)}) collective-permute-start(bf16[32,1664]{1,0:T(8,128)(2,1)S(1)} %get-tuple-element.49.order_ref.refs_0_), channel_id=1, source_target_pairs={{0,4},{4,0},{8,12},{12,8},{16,20},{20,16},{24,28},{28,24},{1,5},{5... | collective-permute-start | bytes 319496 | tf_op jit(solution)/shard_map/ppermute | solution.py:32
  60.6 7.2 %collective-permute-start.22 = (bf16[32,1664]{1,0:T(8,128)(2,1)S(1)}, bf16[32,1664]{1,0:T(8,128)(2,1)S(1)}, u32[]{:S(2)}, u32[]{:S(2)}) collective-permute-start(bf16[32,1664]{1,0:T(8,128)(2,1)S(1)} %collective-permute-done.21.refs_6_), channel_id=1, source_target_pairs={{0,4},{4,0},{8,12},{12,8},{16,20},{20,16},{24,28},{28,24},{1,5},{5... | collective-permute-start | bytes 319496 | tf_op jit(solution)/shard_map/ppermute | solution.py:32
  64.0 4.7 %collective-permute-start.20 = (bf16[32,1664]{1,0:T(8,128)(2,1)S(1)}, bf16[32,1664]{1,0:T(8,128)(2,1)S(1)}, u32[]{:S(2)}, u32[]{:S(2)}) collective-permute-start(bf16[32,1664]{1,0:T(8,128)(2,1)S(1)} %collective-permute-done.19.refs_4_), channel_id=1, source_target_pairs={{0,4},{4,0},{8,12},{12,8},{16,20},{20,16},{24,28},{28,24},{1,5},{5... | collective-permute-start | bytes 319496 | tf_op jit(solution)/shard_map/ppermute | solution.py:32
  72.1 5.8 %collective-permute-start.24 = (bf16[32,1536]{1,0:T(8,128)(2,1)S(1)}, bf16[32,1536]{1,0:T(8,128)(2,1)S(1)}, u32[]{:S(2)}, u32[]{:S(2)}) collective-permute-start(bf16[32,1536]{1,0:T(8,128)(2,1)S(1)} %get-tuple-element.53), channel_id=1, source_target_pairs={{0,4},{4,0},{8,12},{12,8},{16,20},{20,16},{24,28},{28,24},{1,5},{5... | collective-permute-start | bytes 294920 | tf_op jit(solution)/shard_map/ppermute | solution.py:32
  72.8 7.0 %collective-permute-start.26 = (bf16[32,1536]{1,0:T(8,128)(2,1)S(1)}, bf16[32,1536]{1,0:T(8,128)(2,1)S(1)}, u32[]{:S(2)}, u32[]{:S(2)}) collective-permute-start(bf16[32,1536]{1,0:T(8,128)(2,1)S(1)} %get-tuple-element.55), channel_id=1, source_target_pairs={{0,4},{4,0},{8,12},{12,8},{16,20},{20,16},{24,28},{28,24},{1,5},{5... | collective-permute-start | bytes 294920 | tf_op jit(solution)/shard_map/ppermute | solution.py:32
  74.2 8.1 %collective-permute-start.23 = (bf16[64,1536]{1,0:T(8,128)(2,1)S(1)}, bf16[64,1536]{1,0:T(8,128)(2,1)S(1)}, u32[]{:S(2)}, u32[]{:S(2)}) collective-permute-start(bf16[64,1536]{1,0:T(8,128)(2,1)S(1)} %get-tuple-element.51), channel_id=1, source_target_pairs={{0,4},{4,0},{8,12},{12,8},{16,20},{20,16},{24,28},{28,24},{1,5},{5... | collective-permute-start | bytes 589832 | tf_op jit(solution)/shard_map/ppermute | solution.py:32
  77.8 6.7 %collective-permute-start.25 = (bf16[32,1536]{1,0:T(8,128)(2,1)S(1)}, bf16[32,1536]{1,0:T(8,128)(2,1)S(1)}, u32[]{:S(2)}, u32[]{:S(2)}) collective-permute-start(bf16[32,1536]{1,0:T(8,128)(2,1)S(1)} %add_convert_fusion.3), channel_id=1, source_target_pairs={{0,16},{4,20},{8,24},{12,28},{16,0},{20,4},{24,8},{28,12},{1,17},{... | collective-permute-start | bytes 294920 | tf_op jit(solution)/shard_map/ppermute | solution.py:32
  79.8 6.6 %collective-permute-start.27 = (bf16[32,1536]{1,0:T(8,128)(2,1)S(1)}, bf16[32,1536]{1,0:T(8,128)(2,1)S(1)}, u32[]{:S(2)}, u32[]{:S(2)}) collective-permute-start(bf16[32,1536]{1,0:T(8,128)(2,1)S(1)} %add_convert_fusion.2), channel_id=1, source_target_pairs={{0,24},{4,28},{8,16},{12,20},{16,8},{20,12},{24,0},{28,4},{1,25},{... | collective-permute-start | bytes 294920 | tf_op jit(solution)/shard_map/ppermute | solution.py:32
  82.3 5.2 %collective-permute-start.28 = (bf16[32,1536]{1,0:T(8,128)(2,1)S(1)}, bf16[32,1536]{1,0:T(8,128)(2,1)S(1)}, u32[]{:S(2)}, u32[]{:S(2)}) collective-permute-start(bf16[32,1536]{1,0:T(8,128)(2,1)S(1)} %add_convert_fusion.1), channel_id=1, source_target_pairs={{0,8},{4,12},{8,0},{12,4},{16,24},{20,28},{24,16},{28,20},{1,9},{5... | collective-permute-start | bytes 294920 | tf_op jit(solution)/shard_map/ppermute | solution.py:32
  (16 other events, 172.9 us)

commit v5 on v4

--- a/solution.py
+++ b/solution.py
@@ -34,12 +34,12 @@
 
 def gather_rows(value, axis):
     size = lax.axis_size(axis)
-    held = {0: value}
     far = size // 2
-    for distance in list(range(far, size, 2)) + list(range(2, far, 2)) + list(range(1, far, 2)):
+    held = {0: value, far: swap(value, axis, far)}
+    for distance in range(far - 1, 0, -1):
         held[distance] = swap(value, axis, distance)
-    for distance in range(far + 1, size, 2):
-        held[distance] = swap(held[distance - 1], axis, 1)
+    for distance in range(far - 1, 0, -1):
+        held[far + distance] = swap(held[far], axis, distance)
     return [held[distance] for distance in range(size)]
 
 
@@ -54,21 +54,17 @@
     return [held[distance] for distance in sorted(held, key=lambda distance: -distance)]
 
 
-def sum_rows(values, near, axis):
+def sum_rows(values, axis):
     size = lax.axis_size(axis)
     far = size // 2
-    split = far
-    count = values[0].shape[0]
-    beside = {distance: swap(values[distance], axis, 1) for distance in range(split + 1, size, 2)}
-    arrived = [swap(values[distance], axis, distance) for distance in range(far, split)]
-    near = swap(near, axis, 1)
-    for distance in range(split, size, 2):
-        joined = values[distance].astype(F32) + beside[distance + 1].astype(F32)
-        arrived.append(swap(joined.astype(BF), axis, distance))
-    for distance in range(2, far, 2):
-        joined = values[distance].astype(F32) + near[distance // 2 * count : (distance // 2 + 1) * count].astype(F32)
-        arrived.append(swap(joined.astype(BF), axis, distance))
-    total = values[0].astype(F32) + near[:count].astype(F32)
+    beside = [swap(values[far + distance], axis, distance) for distance in range(far - 1, 0, -1)]
+    joined = values[far].astype(F32)
+    for value in beside:
+        joined = joined + value.astype(F32)
+    joined, near = joined.astype(BF), values[1:far]
+    arrived = [swap(joined, axis, far)]
+    arrived += [swap(near[distance - 1], axis, distance) for distance in range(far - 1, 0, -1)]
+    total = values[0].astype(F32)
     for value in arrived:
         total = total + value.astype(F32)
     return total
@@ -313,7 +309,7 @@
     value = dot(value_ref[...], widen)
     products = query_ref[...].astype(F32) * key[:, :feature]
     lane_head = iota((rows, width), 1) // HD
-    joined = jnp.zeros((rows, width), F32)
+    shares, owns, totals = [], [], []
     for head in range(heads):
         own = jnp.sum(jnp.where(lane_head[:, :feature] == head, products, 0.0), -1, keepdims=True)
         level = levels[head : head + 1]
@@ -321,9 +317,14 @@
         highest = jnp.maximum(highest, own)
         weights = jnp.where(member, jnp.exp(level - highest), 0.0).astype(BF)
         own_weight = jnp.exp(own - highest)
-        total = jnp.sum(weights.astype(F32), -1, keepdims=True) + own_weight
-        numer = dot(weights, parts) + own_weight * value
-        joined = jnp.where(lane_head == head, numer / total, joined)
+        shares.append(weights)
+        owns.append(own_weight)
+        totals.append(jnp.sum(weights.astype(F32), -1, keepdims=True) + own_weight)
+    numers = dot(jnp.concatenate(shares, 0), parts)
+    joined = jnp.zeros((rows, width), F32)
+    for head in range(heads):
+        numer = numers[head * rows : (head + 1) * rows] + owns[head] * value
+        joined = jnp.where(lane_head == head, numer / totals[head], joined)
     attended = joined[:, :feature].astype(BF)
     result_ref[...] = dot(attended, weight_ref[...])
     count = rows // tokens
@@ -402,14 +403,8 @@
 
     @pl.when(index == pl.num_programs(0) - 1)
     def _():
-        far = sources // 2
-        out_ref = iter(out_refs[:-1])
-        for place in range(sources):
-            piece = mixed_ref[place * count : (place + 1) * count, :].astype(BF)
-            if place < far and place % 2:
-                out_refs[-1][place // 2 * count : (place // 2 + 1) * count, :] = piece
-            else:
-                next(out_ref)[...] = piece
+        for place, out_ref in enumerate(out_refs):
+            out_ref[...] = mixed_ref[place * count : (place + 1) * count, :].astype(BF)
 
 
 def shards(
@@ -542,19 +537,17 @@
             compiler_params=pltpu.CompilerParams(vmem_limit_bytes=SLIM << 20),
             name="stage",
         )(outgoing, w_gate_up)
-    single = [distance for distance in range(sources) if distance % 2 == 0 or distance > sources // 2]
     mixed = pl.pallas_call(
         functools.partial(expert_kernel, sources, w_router.shape[1]),
         grid=(local_experts,),
-        out_shape=[jax.ShapeDtypeStruct((token_count, model), BF)] * len(single)
-        + [jax.ShapeDtypeStruct((sources // 4 * token_count, model), BF)],
+        out_shape=[jax.ShapeDtypeStruct((token_count, model), BF)] * sources,
         in_specs=[scalar]
         + [vmem] * sources
         + [
             pl.BlockSpec((1,) + w_gate_up.shape[1:], lambda i: (i, 0, 0)),
             pl.BlockSpec((1,) + w_down.shape[1:], lambda i: (i, 0, 0)),
         ],
-        out_specs=[vmem] * (len(single) + 1),
+        out_specs=[vmem] * sources,
         scratch_shapes=[
             pltpu.VMEM((sources * token_count, model + 128), BF),
             pltpu.VMEM((sources * token_count, model), F32),
@@ -563,7 +556,7 @@
         cost_estimate=cost(COSTS[5]),
         name="experts",
     )(req_scalar, *arrived, w_gate_up, w_down)
-    mixture = sum_rows(dict(zip(single, mixed)), mixed[-1], "req")
+    mixture = sum_rows(mixed, "req")
     return (after_attn + mixture).astype(BF)
 
 

time: 88.4 us -> 85 us (0.962)
  waiting for transfers between devices: 27.3 us -> 19.8 us
  starting transfers between devices: 38.1 us -> 42.4 us
    ppermute x29 -> x30, waiting for transfers between devices: 27.3 us -> 19.8 us  [swap(): lax.ppermute(value, axis, [(source, source ^ distance) for source in rang...]
    ppermute x29 -> x30, starting transfers between devices: 38.1 us -> 42.4 us  [swap(): lax.ppermute(value, axis, [(source, source ^ distance) for source in rang...]
  transfers between devices with their start and end apart: 29 -> 30, of which waited for: 16 -> 20; matrix products, arithmetic and copies ran while one was open for 0% -> 0% of each run, Pallas kernels for 2% -> 2%
where the time goes in v5:
time: 85 us; the launch traced here: 84.8 us
  starting transfers between devices  42.4 us (50%)
  waiting for transfers between devices  19.8 us (23%)
  Pallas kernels  18.3 us (22%)
  local copies, waits for them, and re-layouts  3.17 us (4%)
    ppermute x30, starting transfers between devices, swap(): lax.ppermute(value, axis, [(source, source ^ distance) for source in rang...  42.4 us
    ppermute x30, waiting for transfers between devices, swap(): lax.ppermute(value, axis, [(source, source ^ distance) for source in rang...  19.8 us
    pallas_call x1, Pallas kernels, attend(): pl.pallas_call(functools.partial(attend_kernel, heads, groups, chunk, len...  8.43 us
    pallas_call x1, Pallas kernels, shards(): pl.pallas_call(functools.partial(expert_kernel, sources, w_router.shape[1...  3.35 us
    unnamed x40, local copies, waits for them, and re-layouts  3.17 us
    pallas_call x1, Pallas kernels, shards(): pl.pallas_call(query_kernel, out_shape=jax.ShapeDtypeStruct((row_count, h...  2.72 us
  transfers between devices with their start and end apart: 30, of which 20 were waited for; matrix products, arithmetic and copies ran while one was open for 0% of the time, Pallas kernels for 2%

profile of v5, /device:TPU:0, one launch (start us, length us, event | category | flops | bytes accessed | tf_op | source)
XLA Modules:
  0.0 84.8 jit_solution(7195605860360672602)
XLA Ops:
  0.0 2.7 %query.1.refs_4_.refs_1_ = bf16[128,384]{1,0:T(8,128)(2,1)} custom-call(s32[1]{0:T(128)} %bitcast.2.req_ref, bf16[128,1536]{1,0:T(8,128)(2,1)} %hidden_ref.3, f32[12,128]{1,0:T(8,128)} %bitcast.21, bf16[384,1536]{1,0:T(8,128)(2,1)} %weight_hbm.1, s32[8,128]{1,0:T(8,128)} %bitcast.24), custom_call_target="tpu_custom_call" | custom-call | flops 12000000000 | bytes 36000000 | tf_op jit(solution)/shard_map/query/pallas_call | solution.py:445
  2.7 4.1 %collective-permute-start.3 = (bf16[128,384]{1,0:T(8,128)(2,1)}, bf16[128,384]{1,0:T(8,128)(2,1)S(1)}, u32[]{:S(2)}, u32[]{:S(2)}) collective-permute-start(bf16[128,384]{1,0:T(8,128)(2,1)} %query.1.refs_4_.refs_1_), channel_id=1, source_target_pairs={{0,16},{4,20},{8,24},{12,28},{16,0},{20,4},{24,8},{28,12},{1,17},{... | collective-permute-start | bytes 294920 | tf_op jit(solution)/shard_map/ppermute | solution.py:32
  6.8 2.5 %collective-permute-start.2 = (bf16[128,384]{1,0:T(8,128)(2,1)}, bf16[128,384]{1,0:T(8,128)(2,1)S(1)}, u32[]{:S(2)}, u32[]{:S(2)}) collective-permute-start(bf16[128,384]{1,0:T(8,128)(2,1)} %query.1.refs_4_.refs_1_), channel_id=1, source_target_pairs={{0,12},{4,8},{8,4},{12,0},{16,28},{20,24},{24,20},{28,16},{1,13},{... | collective-permute-start | bytes 294920 | tf_op jit(solution)/shard_map/ppermute | solution.py:32
  10.4 1.5 %collective-permute-done.3.refs_8_ = bf16[128,384]{1,0:T(8,128)(2,1)S(1)} collective-permute-done((bf16[128,384]{1,0:T(8,128)(2,1)}, bf16[128,384]{1,0:T(8,128)(2,1)S(1)}, u32[]{:S(2)}, u32[]{:S(2)}) %collective-permute-start.3) | collective-permute-done | bytes 98336 | tf_op jit(solution)/shard_map/ppermute | solution.py:32
  11.9 1.9 %collective-permute-start.6 = (bf16[128,384]{1,0:T(8,128)(2,1)S(1)}, bf16[128,384]{1,0:T(8,128)(2,1)S(1)}, u32[]{:S(2)}, u32[]{:S(2)}) collective-permute-start(bf16[128,384]{1,0:T(8,128)(2,1)S(1)} %collective-permute-done.3.refs_8_), channel_id=1, source_target_pairs={{0,12},{4,8},{8,4},{12,0},{16,28},{20,24},{24,20},{28,16},{1,13},{... | collective-permute-start | bytes 294920 | tf_op jit(solution)/shard_map/ppermute | solution.py:32
  13.7 1.1 %collective-permute-start.5 = (bf16[128,384]{1,0:T(8,128)(2,1)S(1)}, bf16[128,384]{1,0:T(8,128)(2,1)S(1)}, u32[]{:S(2)}, u32[]{:S(2)}) collective-permute-start(bf16[128,384]{1,0:T(8,128)(2,1)S(1)} %collective-permute-done.3.refs_8_), channel_id=1, source_target_pairs={{0,8},{4,12},{8,0},{12,4},{16,24},{20,28},{24,16},{28,20},{1,9},{5... | collective-permute-start | bytes 294920 | tf_op jit(solution)/shard_map/ppermute | solution.py:32
  16.2 2.3 %collective-permute-done.6.refs_11_ = bf16[128,384]{1,0:T(8,128)(2,1)S(1)} collective-permute-done((bf16[128,384]{1,0:T(8,128)(2,1)S(1)}, bf16[128,384]{1,0:T(8,128)(2,1)S(1)}, u32[]{:S(2)}, u32[]{:S(2)}) %collective-permute-start.6) | collective-permute-done | bytes 98336 | tf_op jit(solution)/shard_map/ppermute | solution.py:32
  18.5 0.9 %collective-permute-done.5.refs_10_ = bf16[128,384]{1,0:T(8,128)(2,1)S(1)} collective-permute-done((bf16[128,384]{1,0:T(8,128)(2,1)S(1)}, bf16[128,384]{1,0:T(8,128)(2,1)S(1)}, u32[]{:S(2)}, u32[]{:S(2)}) %collective-permute-start.5) | collective-permute-done | bytes 98336 | tf_op jit(solution)/shard_map/ppermute | solution.py:32
  19.7 8.4 %attend.1 = (bf16[48,512]{1,0:T(8,128)(2,1)S(1)}, bf16[48,512]{1,0:T(8,128)(2,1)S(1)}, bf16[48,512]{1,0:T(8,128)(2,1)S(1)}, bf16[48,512]{1,0:T(8,128)(2,1)S(1)},...) custom-call(s32[384,1]{1,0:T(8,128)S(1)} %get-tuple-element.34.refs_, ...), custom_call_target="tpu_custom_call" | custom-call | flops 12000000000 | bytes 36000000 | tf_op jit(solution)/shard_map/attend/pallas_call | solution.py:264
  28.1 4.7 %collective-permute-start.7 = (bf16[48,512]{1,0:T(8,128)(2,1)S(1)}, bf16[48,512]{1,0:T(8,128)(2,1)S(1)}, u32[]{:S(2)}, u32[]{:S(2)}) collective-permute-start(bf16[48,512]{1,0:T(8,128)(2,1)S(1)} %get-tuple-element.38), channel_id=1, source_target_pairs={{0,28},{4,24},{8,20},{12,16},{16,12},{20,8},{24,4},{28,0},{1,29},{... | collective-permute-start | bytes 147464 | tf_op jit(solution)/shard_map/ppermute | solution.py:32
  33.7 2.2 %collective-permute-start.10 = (bf16[48,512]{1,0:T(8,128)(2,1)S(1)}, bf16[48,512]{1,0:T(8,128)(2,1)S(1)}, u32[]{:S(2)}, u32[]{:S(2)}) collective-permute-start(bf16[48,512]{1,0:T(8,128)(2,1)S(1)} %get-tuple-element.41), channel_id=1, source_target_pairs={{0,16},{4,20},{8,24},{12,28},{16,0},{20,4},{24,8},{28,12},{1,17},{... | collective-permute-start | bytes 147464 | tf_op jit(solution)/shard_map/ppermute | solution.py:32
  35.9 2.2 %collective-permute-start.11 = (bf16[48,512]{1,0:T(8,128)(2,1)S(1)}, bf16[48,512]{1,0:T(8,128)(2,1)S(1)}, u32[]{:S(2)}, u32[]{:S(2)}) collective-permute-start(bf16[48,512]{1,0:T(8,128)(2,1)S(1)} %get-tuple-element.42), channel_id=1, source_target_pairs={{0,12},{4,8},{8,4},{12,0},{16,28},{20,24},{24,20},{28,16},{1,13},{... | collective-permute-start | bytes 147464 | tf_op jit(solution)/shard_map/ppermute | solution.py:32
  40.6 1.0 %collective-permute-done.11.refs_9_ = bf16[48,512]{1,0:T(8,128)(2,1)S(1)} collective-permute-done((bf16[48,512]{1,0:T(8,128)(2,1)S(1)}, bf16[48,512]{1,0:T(8,128)(2,1)S(1)}, u32[]{:S(2)}, u32[]{:S(2)}) %collective-permute-start.11) | collective-permute-done | bytes 49184 | tf_op jit(solution)/shard_map/ppermute | solution.py:32
  43.0 1.4 %merge.1 = (bf16[32,1536]{1,0:T(8,128)(2,1)S(1)}, bf16[32,1536]{1,0:T(8,128)(2,1)S(1)}, bf16[64,1536]{1,0:T(8,128)(2,1)S(1)}) custom-call(s32[1]{0:T(128)} %bitcast.refs_0_.kv_ref, bf16[128,384]{1,0:T(8,128)(2,1)S(1)} %copy-done.6, bf16[128,128]{1,0:T(8,128)(2,1)S(1)} %get-tuple-element.32.refs_2_, bf16[128,128]{1,0:T(8,128)(2,1)S(1)} %get-tuple-element.33.refs_3_, ...), custom_call_target="tpu_custom_call" | custom-call | flops 12000000000 | bytes 36000000 | tf_op jit(solution)/shard_map/merge/pallas_call | solution.py:498
  44.5 1.4 %collective-permute-done.14.given_ref = bf16[64,1536]{1,0:T(8,128)(2,1)S(1)} collective-permute-done((bf16[64,1536]{1,0:T(8,128)(2,1)S(1)}, bf16[64,1536]{1,0:T(8,128)(2,1)S(1)}, u32[]{:S(2)}, u32[]{:S(2)}) %collective-permute-start.14) | collective-permute-done | bytes 196640 | tf_op jit(solution)/shard_map/ppermute | solution.py:32
  46.0 1.6 %collective-permute-start.15 = (bf16[32,1536]{1,0:T(8,128)(2,1)S(1)}, bf16[32,1536]{1,0:T(8,128)(2,1)S(1)}, u32[]{:S(2)}, u32[]{:S(2)}) collective-permute-start(bf16[32,1536]{1,0:T(8,128)(2,1)S(1)} %add_convert_fusion.2), channel_id=1, source_target_pairs={{0,2},{1,3},{2,0},{3,1},{4,6},{5,7},{6,4},{7,5},{8,10},{9,11},{10,... | collective-permute-start | bytes 294920 | tf_op jit(solution)/shard_map/ppermute | solution.py:32
  47.9 3.0 %collective-permute-done.15.refs_1_ = bf16[32,1536]{1,0:T(8,128)(2,1)S(1)} collective-permute-done((bf16[32,1536]{1,0:T(8,128)(2,1)S(1)}, bf16[32,1536]{1,0:T(8,128)(2,1)S(1)}, u32[]{:S(2)}, u32[]{:S(2)}) %collective-permute-start.15) | collective-permute-done | bytes 98336 | tf_op jit(solution)/shard_map/ppermute | solution.py:32
  51.4 2.2 %collective-permute-start.19 = (bf16[32,1664]{1,0:T(8,128)(2,1)S(1)}, bf16[32,1664]{1,0:T(8,128)(2,1)S(1)}, u32[]{:S(2)}, u32[]{:S(2)}) collective-permute-start(bf16[32,1664]{1,0:T(8,128)(2,1)S(1)} %get-tuple-element.50.order_ref.refs_0_), channel_id=1, source_target_pairs={{0,16},{4,20},{8,24},{12,28},{16,0},{20,4},{24,8},{28,12},{1,17},{... | collective-permute-start | bytes 319496 | tf_op jit(solution)/shard_map/ppermute | solution.py:32
  53.6 2.1 %collective-permute-start.18 = (bf16[32,1664]{1,0:T(8,128)(2,1)S(1)}, bf16[32,1664]{1,0:T(8,128)(2,1)S(1)}, u32[]{:S(2)}, u32[]{:S(2)}) collective-permute-start(bf16[32,1664]{1,0:T(8,128)(2,1)S(1)} %get-tuple-element.50.order_ref.refs_0_), channel_id=1, source_target_pairs={{0,12},{4,8},{8,4},{12,0},{16,28},{20,24},{24,20},{28,16},{1,13},{... | collective-permute-start | bytes 319496 | tf_op jit(solution)/shard_map/ppermute | solution.py:32
  55.8 1.3 %collective-permute-start.16 = (bf16[32,1664]{1,0:T(8,128)(2,1)S(1)}, bf16[32,1664]{1,0:T(8,128)(2,1)S(1)}, u32[]{:S(2)}, u32[]{:S(2)}) collective-permute-start(bf16[32,1664]{1,0:T(8,128)(2,1)S(1)} %get-tuple-element.50.order_ref.refs_0_), channel_id=1, source_target_pairs={{0,4},{4,0},{8,12},{12,8},{16,20},{20,16},{24,28},{28,24},{1,5},{5... | collective-permute-start | bytes 319496 | tf_op jit(solution)/shard_map/ppermute | solution.py:32
  57.1 1.6 %collective-permute-done.19.refs_4_ = bf16[32,1664]{1,0:T(8,128)(2,1)S(1)} collective-permute-done((bf16[32,1664]{1,0:T(8,128)(2,1)S(1)}, bf16[32,1664]{1,0:T(8,128)(2,1)S(1)}, u32[]{:S(2)}, u32[]{:S(2)}) %collective-permute-start.19) | collective-permute-done | bytes 106528 | tf_op jit(solution)/shard_map/ppermute | solution.py:32
  58.7 1.0 %collective-permute-start.22 = (bf16[32,1664]{1,0:T(8,128)(2,1)S(1)}, bf16[32,1664]{1,0:T(8,128)(2,1)S(1)}, u32[]{:S(2)}, u32[]{:S(2)}) collective-permute-start(bf16[32,1664]{1,0:T(8,128)(2,1)S(1)} %collective-permute-done.19.refs_4_), channel_id=1, source_target_pairs={{0,12},{4,8},{8,4},{12,0},{16,28},{20,24},{24,20},{28,16},{1,13},{... | collective-permute-start | bytes 319496 | tf_op jit(solution)/shard_map/ppermute | solution.py:32
  59.6 1.3 %collective-permute-start.21 = (bf16[32,1664]{1,0:T(8,128)(2,1)S(1)}, bf16[32,1664]{1,0:T(8,128)(2,1)S(1)}, u32[]{:S(2)}, u32[]{:S(2)}) collective-permute-start(bf16[32,1664]{1,0:T(8,128)(2,1)S(1)} %collective-permute-done.19.refs_4_), channel_id=1, source_target_pairs={{0,8},{4,12},{8,0},{12,4},{16,24},{20,28},{24,16},{28,20},{1,9},{5... | collective-permute-start | bytes 319496 | tf_op jit(solution)/shard_map/ppermute | solution.py:32
  60.9 1.2 %collective-permute-start.20 = (bf16[32,1664]{1,0:T(8,128)(2,1)S(1)}, bf16[32,1664]{1,0:T(8,128)(2,1)S(1)}, u32[]{:S(2)}, u32[]{:S(2)}) collective-permute-start(bf16[32,1664]{1,0:T(8,128)(2,1)S(1)} %collective-permute-done.19.refs_4_), channel_id=1, source_target_pairs={{0,4},{4,0},{8,12},{12,8},{16,20},{20,16},{24,28},{28,24},{1,5},{5... | collective-permute-start | bytes 319496 | tf_op jit(solution)/shard_map/ppermute | solution.py:32
  62.2 2.8 %copy-done = bf16[2,1536,1024]{2,1,0:T(8,128)(2,1)S(1)} copy-done((bf16[2,1536,1024]{2,1,0:T(8,128)(2,1)S(1)}, bf16[2,1536,1024]{2,1,0:T(8,128)(2,1)}, u32[]{:S(2)}) %copy-start) | copy-done | bytes 6291480
  66.1 3.3 %experts.1 = (bf16[32,1536]{1,0:T(8,128)(2,1)S(1)}, bf16[32,1536]{1,0:T(8,128)(2,1)S(1)}, bf16[32,1536]{1,0:T(8,128)(2,1)S(1)}, bf16[32,1536]{1,0:T(8,128)(2,1)S...) custom-call(s32[1]{0:T(128)} %bitcast.2.req_ref, ...), custom_call_target="tpu_custom_call" | custom-call | flops 4000000000 | bytes 12000000 | tf_op jit(solution)/shard_map/experts/pallas_call | solution.py:540
  69.5 2.0 %collective-permute-start.23 = (bf16[32,1536]{1,0:T(8,128)(2,1)S(1)}, bf16[32,1536]{1,0:T(8,128)(2,1)S(1)}, u32[]{:S(2)}, u32[]{:S(2)}) collective-permute-start(bf16[32,1536]{1,0:T(8,128)(2,1)S(1)} %get-tuple-element.53), channel_id=1, source_target_pairs={{0,12},{4,8},{8,4},{12,0},{16,28},{20,24},{24,20},{28,16},{1,13},{... | collective-permute-start | bytes 294920 | tf_op jit(solution)/shard_map/ppermute | solution.py:32
  72.1 1.0 %collective-permute-start.25 = (bf16[32,1536]{1,0:T(8,128)(2,1)S(1)}, bf16[32,1536]{1,0:T(8,128)(2,1)S(1)}, u32[]{:S(2)}, u32[]{:S(2)}) collective-permute-start(bf16[32,1536]{1,0:T(8,128)(2,1)S(1)} %get-tuple-element.55), channel_id=1, source_target_pairs={{0,4},{4,0},{8,12},{12,8},{16,20},{20,16},{24,28},{28,24},{1,5},{5... | collective-permute-start | bytes 294920 | tf_op jit(solution)/shard_map/ppermute | solution.py:32
  73.1 1.9 %collective-permute-start.27 = (bf16[32,1536]{1,0:T(8,128)(2,1)S(1)}, bf16[32,1536]{1,0:T(8,128)(2,1)S(1)}, u32[]{:S(2)}, u32[]{:S(2)}) collective-permute-start(bf16[32,1536]{1,0:T(8,128)(2,1)S(1)} %get-tuple-element.56), channel_id=1, source_target_pairs={{0,12},{4,8},{8,4},{12,0},{16,28},{20,24},{24,20},{28,16},{1,13},{... | collective-permute-start | bytes 294920 | tf_op jit(solution)/shard_map/ppermute | solution.py:32
  76.2 1.0 %collective-permute-start.29 = (bf16[32,1536]{1,0:T(8,128)(2,1)S(1)}, bf16[32,1536]{1,0:T(8,128)(2,1)S(1)}, u32[]{:S(2)}, u32[]{:S(2)}) collective-permute-start(bf16[32,1536]{1,0:T(8,128)(2,1)S(1)} %get-tuple-element.58), channel_id=1, source_target_pairs={{0,4},{4,0},{8,12},{12,8},{16,20},{20,16},{24,28},{28,24},{1,5},{5... | collective-permute-start | bytes 294920 | tf_op jit(solution)/shard_map/ppermute | solution.py:32
  78.5 2.1 %collective-permute-start.26 = (bf16[32,1536]{1,0:T(8,128)(2,1)S(1)}, bf16[32,1536]{1,0:T(8,128)(2,1)S(1)}, u32[]{:S(2)}, u32[]{:S(2)}) collective-permute-start(bf16[32,1536]{1,0:T(8,128)(2,1)S(1)} %add_convert_fusion.1), channel_id=1, source_target_pairs={{0,16},{4,20},{8,24},{12,28},{16,0},{20,4},{24,8},{28,12},{1,17},{... | collective-permute-start | bytes 294920 | tf_op jit(solution)/shard_map/ppermute | solution.py:32
  81.6 2.5 %collective-permute-done.26 = bf16[32,1536]{1,0:T(8,128)(2,1)S(1)} collective-permute-done((bf16[32,1536]{1,0:T(8,128)(2,1)S(1)}, bf16[32,1536]{1,0:T(8,128)(2,1)S(1)}, u32[]{:S(2)}, u32[]{:S(2)}) %collective-permute-start.26) | collective-permute-done | bytes 98336 | tf_op jit(solution)/shard_map/ppermute | solution.py:32
  (82 shorter events, 14.1 us)
Async XLA Ops:
  2.7 9.1 %collective-permute-start.3 = (bf16[128,384]{1,0:T(8,128)(2,1)}, bf16[128,384]{1,0:T(8,128)(2,1)S(1)}, u32[]{:S(2)}, u32[]{:S(2)}) collective-permute-start(bf16[128,384]{1,0:T(8,128)(2,1)} %query.1.refs_4_.refs_1_), channel_id=1, source_target_pairs={{0,16},{4,20},{8,24},{12,28},{16,0},{20,4},{24,8},{28,12},{1,17},{... | collective-permute-start | bytes 294920 | tf_op jit(solution)/shard_map/ppermute | solution.py:32
  6.8 8.1 %collective-permute-start.2 = (bf16[128,384]{1,0:T(8,128)(2,1)}, bf16[128,384]{1,0:T(8,128)(2,1)S(1)}, u32[]{:S(2)}, u32[]{:S(2)}) collective-permute-start(bf16[128,384]{1,0:T(8,128)(2,1)} %query.1.refs_4_.refs_1_), channel_id=1, source_target_pairs={{0,12},{4,8},{8,4},{12,0},{16,28},{20,24},{24,20},{28,16},{1,13},{... | collective-permute-start | bytes 294920 | tf_op jit(solution)/shard_map/ppermute | solution.py:32
  9.3 6.8 %collective-permute-start.1 = (bf16[128,384]{1,0:T(8,128)(2,1)}, bf16[128,384]{1,0:T(8,128)(2,1)S(1)}, u32[]{:S(2)}, u32[]{:S(2)}) collective-permute-start(bf16[128,384]{1,0:T(8,128)(2,1)} %query.1.refs_4_.refs_1_), channel_id=1, source_target_pairs={{0,8},{4,12},{8,0},{12,4},{16,24},{20,28},{24,16},{28,20},{1,9},{5... | collective-permute-start | bytes 294920 | tf_op jit(solution)/shard_map/ppermute | solution.py:32
  9.8 6.4 %collective-permute-start = (bf16[128,384]{1,0:T(8,128)(2,1)}, bf16[128,384]{1,0:T(8,128)(2,1)S(1)}, u32[]{:S(2)}, u32[]{:S(2)}) collective-permute-start(bf16[128,384]{1,0:T(8,128)(2,1)} %query.1.refs_4_.refs_1_), channel_id=1, source_target_pairs={{0,4},{4,0},{8,12},{12,8},{16,20},{20,16},{24,28},{28,24},{1,5},{5... | collective-permute-start | bytes 294920 | tf_op jit(solution)/shard_map/ppermute | solution.py:32
  11.9 6.6 %collective-permute-start.6 = (bf16[128,384]{1,0:T(8,128)(2,1)S(1)}, bf16[128,384]{1,0:T(8,128)(2,1)S(1)}, u32[]{:S(2)}, u32[]{:S(2)}) collective-permute-start(bf16[128,384]{1,0:T(8,128)(2,1)S(1)} %collective-permute-done.3.refs_8_), channel_id=1, source_target_pairs={{0,12},{4,8},{8,4},{12,0},{16,28},{20,24},{24,20},{28,16},{1,13},{... | collective-permute-start | bytes 294920 | tf_op jit(solution)/shard_map/ppermute | solution.py:32
  13.7 5.7 %collective-permute-start.5 = (bf16[128,384]{1,0:T(8,128)(2,1)S(1)}, bf16[128,384]{1,0:T(8,128)(2,1)S(1)}, u32[]{:S(2)}, u32[]{:S(2)}) collective-permute-start(bf16[128,384]{1,0:T(8,128)(2,1)S(1)} %collective-permute-done.3.refs_8_), channel_id=1, source_target_pairs={{0,8},{4,12},{8,0},{12,4},{16,24},{20,28},{24,16},{28,20},{1,9},{5... | collective-permute-start | bytes 294920 | tf_op jit(solution)/shard_map/ppermute | solution.py:32
  14.9 4.7 %collective-permute-start.4 = (bf16[128,384]{1,0:T(8,128)(2,1)S(1)}, bf16[128,384]{1,0:T(8,128)(2,1)S(1)}, u32[]{:S(2)}, u32[]{:S(2)}) collective-permute-start(bf16[128,384]{1,0:T(8,128)(2,1)S(1)} %collective-permute-done.3.refs_8_), channel_id=1, source_target_pairs={{0,4},{4,0},{8,12},{12,8},{16,20},{20,16},{24,28},{28,24},{1,5},{5... | collective-permute-start | bytes 294920 | tf_op jit(solution)/shard_map/ppermute | solution.py:32
  19.6 20.0 %copy-start.3 = (bf16[128,1536]{1,0:T(8,128)(2,1)S(1)}, bf16[128,1536]{1,0:T(8,128)(2,1)}, u32[]{:S(2)}) copy-start(bf16[128,1536]{1,0:T(8,128)(2,1)} %key_weight_ref.1) | copy-start | bytes 1179652
  19.7 23.3 %copy-start.2 = (bf16[384,1536]{1,0:T(8,128)(2,1)S(1)}, bf16[384,1536]{1,0:T(8,128)(2,1)}, u32[]{:S(2)}) copy-start(bf16[384,1536]{1,0:T(8,128)(2,1)} %refs_4_.1) | copy-start | bytes 3538948
  28.1 10.0 %collective-permute-start.7 = (bf16[48,512]{1,0:T(8,128)(2,1)S(1)}, bf16[48,512]{1,0:T(8,128)(2,1)S(1)}, u32[]{:S(2)}, u32[]{:S(2)}) collective-permute-start(bf16[48,512]{1,0:T(8,128)(2,1)S(1)} %get-tuple-element.38), channel_id=1, source_target_pairs={{0,28},{4,24},{8,20},{12,16},{16,12},{20,8},{24,4},{28,0},{1,29},{... | collective-permute-start | bytes 147464 | tf_op jit(solution)/shard_map/ppermute | solution.py:32
  32.8 6.1 %collective-permute-start.8 = (bf16[48,512]{1,0:T(8,128)(2,1)S(1)}, bf16[48,512]{1,0:T(8,128)(2,1)S(1)}, u32[]{:S(2)}, u32[]{:S(2)}) collective-permute-start(bf16[48,512]{1,0:T(8,128)(2,1)S(1)} %get-tuple-element.39), channel_id=1, source_target_pairs={{0,24},{4,28},{8,16},{12,20},{16,8},{20,12},{24,0},{28,4},{1,25},{... | collective-permute-start | bytes 147464 | tf_op jit(solution)/shard_map/ppermute | solution.py:32
  32.8 7.8 %collective-permute-start.9 = (bf16[48,512]{1,0:T(8,128)(2,1)S(1)}, bf16[48,512]{1,0:T(8,128)(2,1)S(1)}, u32[]{:S(2)}, u32[]{:S(2)}) collective-permute-start(bf16[48,512]{1,0:T(8,128)(2,1)S(1)} %get-tuple-element.40), channel_id=1, source_target_pairs={{0,20},{4,16},{8,28},{12,24},{16,4},{20,0},{24,12},{28,8},{1,21},{... | collective-permute-start | bytes 147464 | tf_op jit(solution)/shard_map/ppermute | solution.py:32
  33.7 6.9 %collective-permute-start.10 = (bf16[48,512]{1,0:T(8,128)(2,1)S(1)}, bf16[48,512]{1,0:T(8,128)(2,1)S(1)}, u32[]{:S(2)}, u32[]{:S(2)}) collective-permute-start(bf16[48,512]{1,0:T(8,128)(2,1)S(1)} %get-tuple-element.41), channel_id=1, source_target_pairs={{0,16},{4,20},{8,24},{12,28},{16,0},{20,4},{24,8},{28,12},{1,17},{... | collective-permute-start | bytes 147464 | tf_op jit(solution)/shard_map/ppermute | solution.py:32
  35.9 5.7 %collective-permute-start.11 = (bf16[48,512]{1,0:T(8,128)(2,1)S(1)}, bf16[48,512]{1,0:T(8,128)(2,1)S(1)}, u32[]{:S(2)}, u32[]{:S(2)}) collective-permute-start(bf16[48,512]{1,0:T(8,128)(2,1)S(1)} %get-tuple-element.42), channel_id=1, source_target_pairs={{0,12},{4,8},{8,4},{12,0},{16,28},{20,24},{24,20},{28,16},{1,13},{... | collective-permute-start | bytes 147464 | tf_op jit(solution)/shard_map/ppermute | solution.py:32
  38.1 4.1 %collective-permute-start.12 = (bf16[48,512]{1,0:T(8,128)(2,1)S(1)}, bf16[48,512]{1,0:T(8,128)(2,1)S(1)}, u32[]{:S(2)}, u32[]{:S(2)}) collective-permute-start(bf16[48,512]{1,0:T(8,128)(2,1)S(1)} %get-tuple-element.43), channel_id=1, source_target_pairs={{0,8},{4,12},{8,0},{12,4},{16,24},{20,28},{24,16},{28,20},{1,9},{5... | collective-permute-start | bytes 147464 | tf_op jit(solution)/shard_map/ppermute | solution.py:32
  38.9 4.1 %collective-permute-start.13 = (bf16[48,512]{1,0:T(8,128)(2,1)S(1)}, bf16[48,512]{1,0:T(8,128)(2,1)S(1)}, u32[]{:S(2)}, u32[]{:S(2)}) collective-permute-start(bf16[48,512]{1,0:T(8,128)(2,1)S(1)} %get-tuple-element.44), channel_id=1, source_target_pairs={{0,4},{4,0},{8,12},{12,8},{16,20},{20,16},{24,28},{28,24},{1,5},{5... | collective-permute-start | bytes 147464 | tf_op jit(solution)/shard_map/ppermute | solution.py:32
  44.4 1.5 %collective-permute-start.14 = (bf16[64,1536]{1,0:T(8,128)(2,1)S(1)}, bf16[64,1536]{1,0:T(8,128)(2,1)S(1)}, u32[]{:S(2)}, u32[]{:S(2)}) collective-permute-start(bf16[64,1536]{1,0:T(8,128)(2,1)S(1)} %get-tuple-element.46), channel_id=1, source_target_pairs={{0,1},{1,0},{2,3},{3,2},{4,5},{5,4},{6,7},{7,6},{8,9},{9,8},{10,11... | collective-permute-start | bytes 589832 | tf_op jit(solution)/shard_map/ppermute | solution.py:32
  46.0 4.9 %collective-permute-start.15 = (bf16[32,1536]{1,0:T(8,128)(2,1)S(1)}, bf16[32,1536]{1,0:T(8,128)(2,1)S(1)}, u32[]{:S(2)}, u32[]{:S(2)}) collective-permute-start(bf16[32,1536]{1,0:T(8,128)(2,1)S(1)} %add_convert_fusion.2), channel_id=1, source_target_pairs={{0,2},{1,3},{2,0},{3,1},{4,6},{5,7},{6,4},{7,5},{8,10},{9,11},{10,... | collective-permute-start | bytes 294920 | tf_op jit(solution)/shard_map/ppermute | solution.py:32
  51.4 7.3 %collective-permute-start.19 = (bf16[32,1664]{1,0:T(8,128)(2,1)S(1)}, bf16[32,1664]{1,0:T(8,128)(2,1)S(1)}, u32[]{:S(2)}, u32[]{:S(2)}) collective-permute-start(bf16[32,1664]{1,0:T(8,128)(2,1)S(1)} %get-tuple-element.50.order_ref.refs_0_), channel_id=1, source_target_pairs={{0,16},{4,20},{8,24},{12,28},{16,0},{20,4},{24,8},{28,12},{1,17},{... | collective-permute-start | bytes 319496 | tf_op jit(solution)/shard_map/ppermute | solution.py:32
  53.6 7.3 %collective-permute-start.18 = (bf16[32,1664]{1,0:T(8,128)(2,1)S(1)}, bf16[32,1664]{1,0:T(8,128)(2,1)S(1)}, u32[]{:S(2)}, u32[]{:S(2)}) collective-permute-start(bf16[32,1664]{1,0:T(8,128)(2,1)S(1)} %get-tuple-element.50.order_ref.refs_0_), channel_id=1, source_target_pairs={{0,12},{4,8},{8,4},{12,0},{16,28},{20,24},{24,20},{28,16},{1,13},{... | collective-permute-start | bytes 319496 | tf_op jit(solution)/shard_map/ppermute | solution.py:32
  55.8 9.6 %collective-permute-start.17 = (bf16[32,1664]{1,0:T(8,128)(2,1)S(1)}, bf16[32,1664]{1,0:T(8,128)(2,1)S(1)}, u32[]{:S(2)}, u32[]{:S(2)}) collective-permute-start(bf16[32,1664]{1,0:T(8,128)(2,1)S(1)} %get-tuple-element.50.order_ref.refs_0_), channel_id=1, source_target_pairs={{0,8},{4,12},{8,0},{12,4},{16,24},{20,28},{24,16},{28,20},{1,9},{5... | collective-permute-start | bytes 319496 | tf_op jit(solution)/shard_map/ppermute | solution.py:32
  55.8 9.6 %collective-permute-start.16 = (bf16[32,1664]{1,0:T(8,128)(2,1)S(1)}, bf16[32,1664]{1,0:T(8,128)(2,1)S(1)}, u32[]{:S(2)}, u32[]{:S(2)}) collective-permute-start(bf16[32,1664]{1,0:T(8,128)(2,1)S(1)} %get-tuple-element.50.order_ref.refs_0_), channel_id=1, source_target_pairs={{0,4},{4,0},{8,12},{12,8},{16,20},{20,16},{24,28},{28,24},{1,5},{5... | collective-permute-start | bytes 319496 | tf_op jit(solution)/shard_map/ppermute | solution.py:32
  58.7 6.7 %collective-permute-start.22 = (bf16[32,1664]{1,0:T(8,128)(2,1)S(1)}, bf16[32,1664]{1,0:T(8,128)(2,1)S(1)}, u32[]{:S(2)}, u32[]{:S(2)}) collective-permute-start(bf16[32,1664]{1,0:T(8,128)(2,1)S(1)} %collective-permute-done.19.refs_4_), channel_id=1, source_target_pairs={{0,12},{4,8},{8,4},{12,0},{16,28},{20,24},{24,20},{28,16},{1,13},{... | collective-permute-start | bytes 319496 | tf_op jit(solution)/shard_map/ppermute | solution.py:32
  59.6 6.2 %collective-permute-start.21 = (bf16[32,1664]{1,0:T(8,128)(2,1)S(1)}, bf16[32,1664]{1,0:T(8,128)(2,1)S(1)}, u32[]{:S(2)}, u32[]{:S(2)}) collective-permute-start(bf16[32,1664]{1,0:T(8,128)(2,1)S(1)} %collective-permute-done.19.refs_4_), channel_id=1, source_target_pairs={{0,8},{4,12},{8,0},{12,4},{16,24},{20,28},{24,16},{28,20},{1,9},{5... | collective-permute-start | bytes 319496 | tf_op jit(solution)/shard_map/ppermute | solution.py:32
  60.9 5.2 %collective-permute-start.20 = (bf16[32,1664]{1,0:T(8,128)(2,1)S(1)}, bf16[32,1664]{1,0:T(8,128)(2,1)S(1)}, u32[]{:S(2)}, u32[]{:S(2)}) collective-permute-start(bf16[32,1664]{1,0:T(8,128)(2,1)S(1)} %collective-permute-done.19.refs_4_), channel_id=1, source_target_pairs={{0,4},{4,0},{8,12},{12,8},{16,20},{20,16},{24,28},{28,24},{1,5},{5... | collective-permute-start | bytes 319496 | tf_op jit(solution)/shard_map/ppermute | solution.py:32
  69.5 6.7 %collective-permute-start.23 = (bf16[32,1536]{1,0:T(8,128)(2,1)S(1)}, bf16[32,1536]{1,0:T(8,128)(2,1)S(1)}, u32[]{:S(2)}, u32[]{:S(2)}) collective-permute-start(bf16[32,1536]{1,0:T(8,128)(2,1)S(1)} %get-tuple-element.53), channel_id=1, source_target_pairs={{0,12},{4,8},{8,4},{12,0},{16,28},{20,24},{24,20},{28,16},{1,13},{... | collective-permute-start | bytes 294920 | tf_op jit(solution)/shard_map/ppermute | solution.py:32
  71.5 6.3 %collective-permute-start.24 = (bf16[32,1536]{1,0:T(8,128)(2,1)S(1)}, bf16[32,1536]{1,0:T(8,128)(2,1)S(1)}, u32[]{:S(2)}, u32[]{:S(2)}) collective-permute-start(bf16[32,1536]{1,0:T(8,128)(2,1)S(1)} %get-tuple-element.54), channel_id=1, source_target_pairs={{0,8},{4,12},{8,0},{12,4},{16,24},{20,28},{24,16},{28,20},{1,9},{5... | collective-permute-start | bytes 294920 | tf_op jit(solution)/shard_map/ppermute | solution.py:32
  72.1 6.4 %collective-permute-start.25 = (bf16[32,1536]{1,0:T(8,128)(2,1)S(1)}, bf16[32,1536]{1,0:T(8,128)(2,1)S(1)}, u32[]{:S(2)}, u32[]{:S(2)}) collective-permute-start(bf16[32,1536]{1,0:T(8,128)(2,1)S(1)} %get-tuple-element.55), channel_id=1, source_target_pairs={{0,4},{4,0},{8,12},{12,8},{16,20},{20,16},{24,28},{28,24},{1,5},{5... | collective-permute-start | bytes 294920 | tf_op jit(solution)/shard_map/ppermute | solution.py:32
  73.1 7.6 %collective-permute-start.27 = (bf16[32,1536]{1,0:T(8,128)(2,1)S(1)}, bf16[32,1536]{1,0:T(8,128)(2,1)S(1)}, u32[]{:S(2)}, u32[]{:S(2)}) collective-permute-start(bf16[32,1536]{1,0:T(8,128)(2,1)S(1)} %get-tuple-element.56), channel_id=1, source_target_pairs={{0,12},{4,8},{8,4},{12,0},{16,28},{20,24},{24,20},{28,16},{1,13},{... | collective-permute-start | bytes 294920 | tf_op jit(solution)/shard_map/ppermute | solution.py:32
  75.0 6.4 %collective-permute-start.28 = (bf16[32,1536]{1,0:T(8,128)(2,1)S(1)}, bf16[32,1536]{1,0:T(8,128)(2,1)S(1)}, u32[]{:S(2)}, u32[]{:S(2)}) collective-permute-start(bf16[32,1536]{1,0:T(8,128)(2,1)S(1)} %get-tuple-element.57), channel_id=1, source_target_pairs={{0,8},{4,12},{8,0},{12,4},{16,24},{20,28},{24,16},{28,20},{1,9},{5... | collective-permute-start | bytes 294920 | tf_op jit(solution)/shard_map/ppermute | solution.py:32
  76.2 5.4 %collective-permute-start.29 = (bf16[32,1536]{1,0:T(8,128)(2,1)S(1)}, bf16[32,1536]{1,0:T(8,128)(2,1)S(1)}, u32[]{:S(2)}, u32[]{:S(2)}) collective-permute-start(bf16[32,1536]{1,0:T(8,128)(2,1)S(1)} %get-tuple-element.58), channel_id=1, source_target_pairs={{0,4},{4,0},{8,12},{12,8},{16,20},{20,16},{24,28},{28,24},{1,5},{5... | collective-permute-start | bytes 294920 | tf_op jit(solution)/shard_map/ppermute | solution.py:32
  78.5 5.6 %collective-permute-start.26 = (bf16[32,1536]{1,0:T(8,128)(2,1)S(1)}, bf16[32,1536]{1,0:T(8,128)(2,1)S(1)}, u32[]{:S(2)}, u32[]{:S(2)}) collective-permute-start(bf16[32,1536]{1,0:T(8,128)(2,1)S(1)} %add_convert_fusion.1), channel_id=1, source_target_pairs={{0,16},{4,20},{8,24},{12,28},{16,0},{20,4},{24,8},{28,12},{1,17},{... | collective-permute-start | bytes 294920 | tf_op jit(solution)/shard_map/ppermute | solution.py:32
  (17 other events, 185.3 us)

commit v6 on v5

--- a/solution.py
+++ b/solution.py
@@ -115,12 +115,10 @@
     ]
     for copy in copies:
         copy.start()
-    copies[0].wait()
+    for copy in copies:
+        copy.wait()
+    normed = rms_norm(hidden_ref[...], lanes_of(gain_ref))
     cosines, sines = tables(req_ref, length_ref, query_ref.shape[0])
-    copies[1].wait()
-    copies[3].wait()
-    normed = rms_norm(hidden_ref[...], lanes_of(gain_ref))
-    copies[2].wait()
     query = project_rows(normed, weight_ref[...])
     query_ref[...] = (rotate(query, cosines, sines) * 0.125).astype(BF)
 

time: 85 us -> 85.1 us (level)
  no operation moved by 1% of the time
where the time goes in v6:
time: 85.1 us; the launch traced here: 84.9 us
  starting transfers between devices  42.4 us (50%)
  waiting for transfers between devices  19.8 us (23%)
  Pallas kernels  18.4 us (22%)
  local copies, waits for them, and re-layouts  3.17 us (4%)
    ppermute x30, starting transfers between devices, swap(): lax.ppermute(value, axis, [(source, source ^ distance) for source in rang...  42.4 us
    ppermute x30, waiting for transfers between devices, swap(): lax.ppermute(value, axis, [(source, source ^ distance) for source in rang...  19.8 us
    pallas_call x1, Pallas kernels, attend(): pl.pallas_call(functools.partial(attend_kernel, heads, groups, chunk, len...  8.43 us
    pallas_call x1, Pallas kernels, shards(): pl.pallas_call(functools.partial(expert_kernel, sources, w_router.shape[1...  3.35 us
    unnamed x40, local copies, waits for them, and re-layouts  3.17 us
    pallas_call x1, Pallas kernels, shards(): pl.pallas_call(query_kernel, out_shape=jax.ShapeDtypeStruct((row_count, h...  2.82 us
  transfers between devices with their start and end apart: 30, of which 20 were waited for; matrix products, arithmetic and copies ran while one was open for 0% of the time, Pallas kernels for 2%

profile of v6, /device:TPU:0, one launch (start us, length us, event | category | flops | bytes accessed | tf_op | source)
XLA Modules:
  0.0 84.9 jit_solution(4606724026229991378)
XLA Ops:
  0.0 2.8 %query.1.refs_4_.refs_1_ = bf16[128,384]{1,0:T(8,128)(2,1)} custom-call(s32[1]{0:T(128)} %bitcast.2.req_ref, bf16[128,1536]{1,0:T(8,128)(2,1)} %hidden_ref.3, f32[12,128]{1,0:T(8,128)} %bitcast.21, bf16[384,1536]{1,0:T(8,128)(2,1)} %weight_hbm.1, s32[8,128]{1,0:T(8,128)} %bitcast.24), custom_call_target="tpu_custom_call" | custom-call | flops 12000000000 | bytes 36000000 | tf_op jit(solution)/shard_map/query/pallas_call | solution.py:443
  2.8 4.1 %collective-permute-start.3 = (bf16[128,384]{1,0:T(8,128)(2,1)}, bf16[128,384]{1,0:T(8,128)(2,1)S(1)}, u32[]{:S(2)}, u32[]{:S(2)}) collective-permute-start(bf16[128,384]{1,0:T(8,128)(2,1)} %query.1.refs_4_.refs_1_), channel_id=1, source_target_pairs={{0,16},{4,20},{8,24},{12,28},{16,0},{20,4},{24,8},{28,12},{1,17},{... | collective-permute-start | bytes 294920 | tf_op jit(solution)/shard_map/ppermute | solution.py:32
  6.9 2.5 %collective-permute-start.2 = (bf16[128,384]{1,0:T(8,128)(2,1)}, bf16[128,384]{1,0:T(8,128)(2,1)S(1)}, u32[]{:S(2)}, u32[]{:S(2)}) collective-permute-start(bf16[128,384]{1,0:T(8,128)(2,1)} %query.1.refs_4_.refs_1_), channel_id=1, source_target_pairs={{0,12},{4,8},{8,4},{12,0},{16,28},{20,24},{24,20},{28,16},{1,13},{... | collective-permute-start | bytes 294920 | tf_op jit(solution)/shard_map/ppermute | solution.py:32
  10.5 1.5 %collective-permute-done.3.refs_8_ = bf16[128,384]{1,0:T(8,128)(2,1)S(1)} collective-permute-done((bf16[128,384]{1,0:T(8,128)(2,1)}, bf16[128,384]{1,0:T(8,128)(2,1)S(1)}, u32[]{:S(2)}, u32[]{:S(2)}) %collective-permute-start.3) | collective-permute-done | bytes 98336 | tf_op jit(solution)/shard_map/ppermute | solution.py:32
  12.0 1.9 %collective-permute-start.6 = (bf16[128,384]{1,0:T(8,128)(2,1)S(1)}, bf16[128,384]{1,0:T(8,128)(2,1)S(1)}, u32[]{:S(2)}, u32[]{:S(2)}) collective-permute-start(bf16[128,384]{1,0:T(8,128)(2,1)S(1)} %collective-permute-done.3.refs_8_), channel_id=1, source_target_pairs={{0,12},{4,8},{8,4},{12,0},{16,28},{20,24},{24,20},{28,16},{1,13},{... | collective-permute-start | bytes 294920 | tf_op jit(solution)/shard_map/ppermute | solution.py:32
  13.9 1.1 %collective-permute-start.5 = (bf16[128,384]{1,0:T(8,128)(2,1)S(1)}, bf16[128,384]{1,0:T(8,128)(2,1)S(1)}, u32[]{:S(2)}, u32[]{:S(2)}) collective-permute-start(bf16[128,384]{1,0:T(8,128)(2,1)S(1)} %collective-permute-done.3.refs_8_), channel_id=1, source_target_pairs={{0,8},{4,12},{8,0},{12,4},{16,24},{20,28},{24,16},{28,20},{1,9},{5... | collective-permute-start | bytes 294920 | tf_op jit(solution)/shard_map/ppermute | solution.py:32
  16.3 2.3 %collective-permute-done.6.refs_11_ = bf16[128,384]{1,0:T(8,128)(2,1)S(1)} collective-permute-done((bf16[128,384]{1,0:T(8,128)(2,1)S(1)}, bf16[128,384]{1,0:T(8,128)(2,1)S(1)}, u32[]{:S(2)}, u32[]{:S(2)}) %collective-permute-start.6) | collective-permute-done | bytes 98336 | tf_op jit(solution)/shard_map/ppermute | solution.py:32
  18.6 0.9 %collective-permute-done.5.refs_10_ = bf16[128,384]{1,0:T(8,128)(2,1)S(1)} collective-permute-done((bf16[128,384]{1,0:T(8,128)(2,1)S(1)}, bf16[128,384]{1,0:T(8,128)(2,1)S(1)}, u32[]{:S(2)}, u32[]{:S(2)}) %collective-permute-start.5) | collective-permute-done | bytes 98336 | tf_op jit(solution)/shard_map/ppermute | solution.py:32
  19.8 8.4 %attend.1 = (bf16[48,512]{1,0:T(8,128)(2,1)S(1)}, bf16[48,512]{1,0:T(8,128)(2,1)S(1)}, bf16[48,512]{1,0:T(8,128)(2,1)S(1)}, bf16[48,512]{1,0:T(8,128)(2,1)S(1)},...) custom-call(s32[384,1]{1,0:T(8,128)S(1)} %get-tuple-element.34.refs_, ...), custom_call_target="tpu_custom_call" | custom-call | flops 12000000000 | bytes 36000000 | tf_op jit(solution)/shard_map/attend/pallas_call | solution.py:262
  28.2 4.7 %collective-permute-start.7 = (bf16[48,512]{1,0:T(8,128)(2,1)S(1)}, bf16[48,512]{1,0:T(8,128)(2,1)S(1)}, u32[]{:S(2)}, u32[]{:S(2)}) collective-permute-start(bf16[48,512]{1,0:T(8,128)(2,1)S(1)} %get-tuple-element.38), channel_id=1, source_target_pairs={{0,28},{4,24},{8,20},{12,16},{16,12},{20,8},{24,4},{28,0},{1,29},{... | collective-permute-start | bytes 147464 | tf_op jit(solution)/shard_map/ppermute | solution.py:32
  33.8 2.2 %collective-permute-start.10 = (bf16[48,512]{1,0:T(8,128)(2,1)S(1)}, bf16[48,512]{1,0:T(8,128)(2,1)S(1)}, u32[]{:S(2)}, u32[]{:S(2)}) collective-permute-start(bf16[48,512]{1,0:T(8,128)(2,1)S(1)} %get-tuple-element.41), channel_id=1, source_target_pairs={{0,16},{4,20},{8,24},{12,28},{16,0},{20,4},{24,8},{28,12},{1,17},{... | collective-permute-start | bytes 147464 | tf_op jit(solution)/shard_map/ppermute | solution.py:32
  36.0 2.2 %collective-permute-start.11 = (bf16[48,512]{1,0:T(8,128)(2,1)S(1)}, bf16[48,512]{1,0:T(8,128)(2,1)S(1)}, u32[]{:S(2)}, u32[]{:S(2)}) collective-permute-start(bf16[48,512]{1,0:T(8,128)(2,1)S(1)} %get-tuple-element.42), channel_id=1, source_target_pairs={{0,12},{4,8},{8,4},{12,0},{16,28},{20,24},{24,20},{28,16},{1,13},{... | collective-permute-start | bytes 147464 | tf_op jit(solution)/shard_map/ppermute | solution.py:32
  40.7 1.0 %collective-permute-done.11.refs_9_ = bf16[48,512]{1,0:T(8,128)(2,1)S(1)} collective-permute-done((bf16[48,512]{1,0:T(8,128)(2,1)S(1)}, bf16[48,512]{1,0:T(8,128)(2,1)S(1)}, u32[]{:S(2)}, u32[]{:S(2)}) %collective-permute-start.11) | collective-permute-done | bytes 49184 | tf_op jit(solution)/shard_map/ppermute | solution.py:32
  43.1 1.4 %merge.1 = (bf16[32,1536]{1,0:T(8,128)(2,1)S(1)}, bf16[32,1536]{1,0:T(8,128)(2,1)S(1)}, bf16[64,1536]{1,0:T(8,128)(2,1)S(1)}) custom-call(s32[1]{0:T(128)} %bitcast.refs_0_.kv_ref, bf16[128,384]{1,0:T(8,128)(2,1)S(1)} %copy-done.6, bf16[128,128]{1,0:T(8,128)(2,1)S(1)} %get-tuple-element.32.refs_2_, bf16[128,128]{1,0:T(8,128)(2,1)S(1)} %get-tuple-element.33.refs_3_, ...), custom_call_target="tpu_custom_call" | custom-call | flops 12000000000 | bytes 36000000 | tf_op jit(solution)/shard_map/merge/pallas_call | solution.py:496
  44.6 1.4 %collective-permute-done.14.given_ref = bf16[64,1536]{1,0:T(8,128)(2,1)S(1)} collective-permute-done((bf16[64,1536]{1,0:T(8,128)(2,1)S(1)}, bf16[64,1536]{1,0:T(8,128)(2,1)S(1)}, u32[]{:S(2)}, u32[]{:S(2)}) %collective-permute-start.14) | collective-permute-done | bytes 196640 | tf_op jit(solution)/shard_map/ppermute | solution.py:32
  46.1 1.6 %collective-permute-start.15 = (bf16[32,1536]{1,0:T(8,128)(2,1)S(1)}, bf16[32,1536]{1,0:T(8,128)(2,1)S(1)}, u32[]{:S(2)}, u32[]{:S(2)}) collective-permute-start(bf16[32,1536]{1,0:T(8,128)(2,1)S(1)} %add_convert_fusion.2), channel_id=1, source_target_pairs={{0,2},{1,3},{2,0},{3,1},{4,6},{5,7},{6,4},{7,5},{8,10},{9,11},{10,... | collective-permute-start | bytes 294920 | tf_op jit(solution)/shard_map/ppermute | solution.py:32
  47.9 3.0 %collective-permute-done.15.refs_1_ = bf16[32,1536]{1,0:T(8,128)(2,1)S(1)} collective-permute-done((bf16[32,1536]{1,0:T(8,128)(2,1)S(1)}, bf16[32,1536]{1,0:T(8,128)(2,1)S(1)}, u32[]{:S(2)}, u32[]{:S(2)}) %collective-permute-start.15) | collective-permute-done | bytes 98336 | tf_op jit(solution)/shard_map/ppermute | solution.py:32
  51.5 2.2 %collective-permute-start.19 = (bf16[32,1664]{1,0:T(8,128)(2,1)S(1)}, bf16[32,1664]{1,0:T(8,128)(2,1)S(1)}, u32[]{:S(2)}, u32[]{:S(2)}) collective-permute-start(bf16[32,1664]{1,0:T(8,128)(2,1)S(1)} %get-tuple-element.50.order_ref.refs_0_), channel_id=1, source_target_pairs={{0,16},{4,20},{8,24},{12,28},{16,0},{20,4},{24,8},{28,12},{1,17},{... | collective-permute-start | bytes 319496 | tf_op jit(solution)/shard_map/ppermute | solution.py:32
  53.8 2.1 %collective-permute-start.18 = (bf16[32,1664]{1,0:T(8,128)(2,1)S(1)}, bf16[32,1664]{1,0:T(8,128)(2,1)S(1)}, u32[]{:S(2)}, u32[]{:S(2)}) collective-permute-start(bf16[32,1664]{1,0:T(8,128)(2,1)S(1)} %get-tuple-element.50.order_ref.refs_0_), channel_id=1, source_target_pairs={{0,12},{4,8},{8,4},{12,0},{16,28},{20,24},{24,20},{28,16},{1,13},{... | collective-permute-start | bytes 319496 | tf_op jit(solution)/shard_map/ppermute | solution.py:32
  55.9 1.3 %collective-permute-start.16 = (bf16[32,1664]{1,0:T(8,128)(2,1)S(1)}, bf16[32,1664]{1,0:T(8,128)(2,1)S(1)}, u32[]{:S(2)}, u32[]{:S(2)}) collective-permute-start(bf16[32,1664]{1,0:T(8,128)(2,1)S(1)} %get-tuple-element.50.order_ref.refs_0_), channel_id=1, source_target_pairs={{0,4},{4,0},{8,12},{12,8},{16,20},{20,16},{24,28},{28,24},{1,5},{5... | collective-permute-start | bytes 319496 | tf_op jit(solution)/shard_map/ppermute | solution.py:32
  57.2 1.5 %collective-permute-done.19.refs_4_ = bf16[32,1664]{1,0:T(8,128)(2,1)S(1)} collective-permute-done((bf16[32,1664]{1,0:T(8,128)(2,1)S(1)}, bf16[32,1664]{1,0:T(8,128)(2,1)S(1)}, u32[]{:S(2)}, u32[]{:S(2)}) %collective-permute-start.19) | collective-permute-done | bytes 106528 | tf_op jit(solution)/shard_map/ppermute | solution.py:32
  58.8 1.0 %collective-permute-start.22 = (bf16[32,1664]{1,0:T(8,128)(2,1)S(1)}, bf16[32,1664]{1,0:T(8,128)(2,1)S(1)}, u32[]{:S(2)}, u32[]{:S(2)}) collective-permute-start(bf16[32,1664]{1,0:T(8,128)(2,1)S(1)} %collective-permute-done.19.refs_4_), channel_id=1, source_target_pairs={{0,12},{4,8},{8,4},{12,0},{16,28},{20,24},{24,20},{28,16},{1,13},{... | collective-permute-start | bytes 319496 | tf_op jit(solution)/shard_map/ppermute | solution.py:32
  59.7 1.3 %collective-permute-start.21 = (bf16[32,1664]{1,0:T(8,128)(2,1)S(1)}, bf16[32,1664]{1,0:T(8,128)(2,1)S(1)}, u32[]{:S(2)}, u32[]{:S(2)}) collective-permute-start(bf16[32,1664]{1,0:T(8,128)(2,1)S(1)} %collective-permute-done.19.refs_4_), channel_id=1, source_target_pairs={{0,8},{4,12},{8,0},{12,4},{16,24},{20,28},{24,16},{28,20},{1,9},{5... | collective-permute-start | bytes 319496 | tf_op jit(solution)/shard_map/ppermute | solution.py:32
  61.0 1.2 %collective-permute-start.20 = (bf16[32,1664]{1,0:T(8,128)(2,1)S(1)}, bf16[32,1664]{1,0:T(8,128)(2,1)S(1)}, u32[]{:S(2)}, u32[]{:S(2)}) collective-permute-start(bf16[32,1664]{1,0:T(8,128)(2,1)S(1)} %collective-permute-done.19.refs_4_), channel_id=1, source_target_pairs={{0,4},{4,0},{8,12},{12,8},{16,20},{20,16},{24,28},{28,24},{1,5},{5... | collective-permute-start | bytes 319496 | tf_op jit(solution)/shard_map/ppermute | solution.py:32
  62.3 2.8 %copy-done = bf16[2,1536,1024]{2,1,0:T(8,128)(2,1)S(1)} copy-done((bf16[2,1536,1024]{2,1,0:T(8,128)(2,1)S(1)}, bf16[2,1536,1024]{2,1,0:T(8,128)(2,1)}, u32[]{:S(2)}) %copy-start) | copy-done | bytes 6291480
  66.2 3.3 %experts.1 = (bf16[32,1536]{1,0:T(8,128)(2,1)S(1)}, bf16[32,1536]{1,0:T(8,128)(2,1)S(1)}, bf16[32,1536]{1,0:T(8,128)(2,1)S(1)}, bf16[32,1536]{1,0:T(8,128)(2,1)S...) custom-call(s32[1]{0:T(128)} %bitcast.2.req_ref, ...), custom_call_target="tpu_custom_call" | custom-call | flops 4000000000 | bytes 12000000 | tf_op jit(solution)/shard_map/experts/pallas_call | solution.py:538
  69.6 2.0 %collective-permute-start.23 = (bf16[32,1536]{1,0:T(8,128)(2,1)S(1)}, bf16[32,1536]{1,0:T(8,128)(2,1)S(1)}, u32[]{:S(2)}, u32[]{:S(2)}) collective-permute-start(bf16[32,1536]{1,0:T(8,128)(2,1)S(1)} %get-tuple-element.53), channel_id=1, source_target_pairs={{0,12},{4,8},{8,4},{12,0},{16,28},{20,24},{24,20},{28,16},{1,13},{... | collective-permute-start | bytes 294920 | tf_op jit(solution)/shard_map/ppermute | solution.py:32
  72.2 1.0 %collective-permute-start.25 = (bf16[32,1536]{1,0:T(8,128)(2,1)S(1)}, bf16[32,1536]{1,0:T(8,128)(2,1)S(1)}, u32[]{:S(2)}, u32[]{:S(2)}) collective-permute-start(bf16[32,1536]{1,0:T(8,128)(2,1)S(1)} %get-tuple-element.55), channel_id=1, source_target_pairs={{0,4},{4,0},{8,12},{12,8},{16,20},{20,16},{24,28},{28,24},{1,5},{5... | collective-permute-start | bytes 294920 | tf_op jit(solution)/shard_map/ppermute | solution.py:32
  73.2 1.9 %collective-permute-start.27 = (bf16[32,1536]{1,0:T(8,128)(2,1)S(1)}, bf16[32,1536]{1,0:T(8,128)(2,1)S(1)}, u32[]{:S(2)}, u32[]{:S(2)}) collective-permute-start(bf16[32,1536]{1,0:T(8,128)(2,1)S(1)} %get-tuple-element.56), channel_id=1, source_target_pairs={{0,12},{4,8},{8,4},{12,0},{16,28},{20,24},{24,20},{28,16},{1,13},{... | collective-permute-start | bytes 294920 | tf_op jit(solution)/shard_map/ppermute | solution.py:32
  76.2 1.0 %collective-permute-start.29 = (bf16[32,1536]{1,0:T(8,128)(2,1)S(1)}, bf16[32,1536]{1,0:T(8,128)(2,1)S(1)}, u32[]{:S(2)}, u32[]{:S(2)}) collective-permute-start(bf16[32,1536]{1,0:T(8,128)(2,1)S(1)} %get-tuple-element.58), channel_id=1, source_target_pairs={{0,4},{4,0},{8,12},{12,8},{16,20},{20,16},{24,28},{28,24},{1,5},{5... | collective-permute-start | bytes 294920 | tf_op jit(solution)/shard_map/ppermute | solution.py:32
  78.6 2.2 %collective-permute-start.26 = (bf16[32,1536]{1,0:T(8,128)(2,1)S(1)}, bf16[32,1536]{1,0:T(8,128)(2,1)S(1)}, u32[]{:S(2)}, u32[]{:S(2)}) collective-permute-start(bf16[32,1536]{1,0:T(8,128)(2,1)S(1)} %add_convert_fusion.1), channel_id=1, source_target_pairs={{0,16},{4,20},{8,24},{12,28},{16,0},{20,4},{24,8},{28,12},{1,17},{... | collective-permute-start | bytes 294920 | tf_op jit(solution)/shard_map/ppermute | solution.py:32
  81.7 2.5 %collective-permute-done.26 = bf16[32,1536]{1,0:T(8,128)(2,1)S(1)} collective-permute-done((bf16[32,1536]{1,0:T(8,128)(2,1)S(1)}, bf16[32,1536]{1,0:T(8,128)(2,1)S(1)}, u32[]{:S(2)}, u32[]{:S(2)}) %collective-permute-start.26) | collective-permute-done | bytes 98336 | tf_op jit(solution)/shard_map/ppermute | solution.py:32
  (82 shorter events, 14.1 us)
Async XLA Ops:
  2.8 9.1 %collective-permute-start.3 = (bf16[128,384]{1,0:T(8,128)(2,1)}, bf16[128,384]{1,0:T(8,128)(2,1)S(1)}, u32[]{:S(2)}, u32[]{:S(2)}) collective-permute-start(bf16[128,384]{1,0:T(8,128)(2,1)} %query.1.refs_4_.refs_1_), channel_id=1, source_target_pairs={{0,16},{4,20},{8,24},{12,28},{16,0},{20,4},{24,8},{28,12},{1,17},{... | collective-permute-start | bytes 294920 | tf_op jit(solution)/shard_map/ppermute | solution.py:32
  6.9 8.1 %collective-permute-start.2 = (bf16[128,384]{1,0:T(8,128)(2,1)}, bf16[128,384]{1,0:T(8,128)(2,1)S(1)}, u32[]{:S(2)}, u32[]{:S(2)}) collective-permute-start(bf16[128,384]{1,0:T(8,128)(2,1)} %query.1.refs_4_.refs_1_), channel_id=1, source_target_pairs={{0,12},{4,8},{8,4},{12,0},{16,28},{20,24},{24,20},{28,16},{1,13},{... | collective-permute-start | bytes 294920 | tf_op jit(solution)/shard_map/ppermute | solution.py:32
  9.4 6.8 %collective-permute-start.1 = (bf16[128,384]{1,0:T(8,128)(2,1)}, bf16[128,384]{1,0:T(8,128)(2,1)S(1)}, u32[]{:S(2)}, u32[]{:S(2)}) collective-permute-start(bf16[128,384]{1,0:T(8,128)(2,1)} %query.1.refs_4_.refs_1_), channel_id=1, source_target_pairs={{0,8},{4,12},{8,0},{12,4},{16,24},{20,28},{24,16},{28,20},{1,9},{5... | collective-permute-start | bytes 294920 | tf_op jit(solution)/shard_map/ppermute | solution.py:32
  9.9 6.4 %collective-permute-start = (bf16[128,384]{1,0:T(8,128)(2,1)}, bf16[128,384]{1,0:T(8,128)(2,1)S(1)}, u32[]{:S(2)}, u32[]{:S(2)}) collective-permute-start(bf16[128,384]{1,0:T(8,128)(2,1)} %query.1.refs_4_.refs_1_), channel_id=1, source_target_pairs={{0,4},{4,0},{8,12},{12,8},{16,20},{20,16},{24,28},{28,24},{1,5},{5... | collective-permute-start | bytes 294920 | tf_op jit(solution)/shard_map/ppermute | solution.py:32
  12.0 6.6 %collective-permute-start.6 = (bf16[128,384]{1,0:T(8,128)(2,1)S(1)}, bf16[128,384]{1,0:T(8,128)(2,1)S(1)}, u32[]{:S(2)}, u32[]{:S(2)}) collective-permute-start(bf16[128,384]{1,0:T(8,128)(2,1)S(1)} %collective-permute-done.3.refs_8_), channel_id=1, source_target_pairs={{0,12},{4,8},{8,4},{12,0},{16,28},{20,24},{24,20},{28,16},{1,13},{... | collective-permute-start | bytes 294920 | tf_op jit(solution)/shard_map/ppermute | solution.py:32
  13.9 5.7 %collective-permute-start.5 = (bf16[128,384]{1,0:T(8,128)(2,1)S(1)}, bf16[128,384]{1,0:T(8,128)(2,1)S(1)}, u32[]{:S(2)}, u32[]{:S(2)}) collective-permute-start(bf16[128,384]{1,0:T(8,128)(2,1)S(1)} %collective-permute-done.3.refs_8_), channel_id=1, source_target_pairs={{0,8},{4,12},{8,0},{12,4},{16,24},{20,28},{24,16},{28,20},{1,9},{5... | collective-permute-start | bytes 294920 | tf_op jit(solution)/shard_map/ppermute | solution.py:32
  15.0 4.7 %collective-permute-start.4 = (bf16[128,384]{1,0:T(8,128)(2,1)S(1)}, bf16[128,384]{1,0:T(8,128)(2,1)S(1)}, u32[]{:S(2)}, u32[]{:S(2)}) collective-permute-start(bf16[128,384]{1,0:T(8,128)(2,1)S(1)} %collective-permute-done.3.refs_8_), channel_id=1, source_target_pairs={{0,4},{4,0},{8,12},{12,8},{16,20},{20,16},{24,28},{28,24},{1,5},{5... | collective-permute-start | bytes 294920 | tf_op jit(solution)/shard_map/ppermute | solution.py:32
  19.7 20.0 %copy-start.3 = (bf16[128,1536]{1,0:T(8,128)(2,1)S(1)}, bf16[128,1536]{1,0:T(8,128)(2,1)}, u32[]{:S(2)}) copy-start(bf16[128,1536]{1,0:T(8,128)(2,1)} %key_weight_ref.1) | copy-start | bytes 1179652
  19.8 23.3 %copy-start.2 = (bf16[384,1536]{1,0:T(8,128)(2,1)S(1)}, bf16[384,1536]{1,0:T(8,128)(2,1)}, u32[]{:S(2)}) copy-start(bf16[384,1536]{1,0:T(8,128)(2,1)} %refs_4_.1) | copy-start | bytes 3538948
  28.2 10.0 %collective-permute-start.7 = (bf16[48,512]{1,0:T(8,128)(2,1)S(1)}, bf16[48,512]{1,0:T(8,128)(2,1)S(1)}, u32[]{:S(2)}, u32[]{:S(2)}) collective-permute-start(bf16[48,512]{1,0:T(8,128)(2,1)S(1)} %get-tuple-element.38), channel_id=1, source_target_pairs={{0,28},{4,24},{8,20},{12,16},{16,12},{20,8},{24,4},{28,0},{1,29},{... | collective-permute-start | bytes 147464 | tf_op jit(solution)/shard_map/ppermute | solution.py:32
  32.9 6.1 %collective-permute-start.8 = (bf16[48,512]{1,0:T(8,128)(2,1)S(1)}, bf16[48,512]{1,0:T(8,128)(2,1)S(1)}, u32[]{:S(2)}, u32[]{:S(2)}) collective-permute-start(bf16[48,512]{1,0:T(8,128)(2,1)S(1)} %get-tuple-element.39), channel_id=1, source_target_pairs={{0,24},{4,28},{8,16},{12,20},{16,8},{20,12},{24,0},{28,4},{1,25},{... | collective-permute-start | bytes 147464 | tf_op jit(solution)/shard_map/ppermute | solution.py:32
  32.9 7.8 %collective-permute-start.9 = (bf16[48,512]{1,0:T(8,128)(2,1)S(1)}, bf16[48,512]{1,0:T(8,128)(2,1)S(1)}, u32[]{:S(2)}, u32[]{:S(2)}) collective-permute-start(bf16[48,512]{1,0:T(8,128)(2,1)S(1)} %get-tuple-element.40), channel_id=1, source_target_pairs={{0,20},{4,16},{8,28},{12,24},{16,4},{20,0},{24,12},{28,8},{1,21},{... | collective-permute-start | bytes 147464 | tf_op jit(solution)/shard_map/ppermute | solution.py:32
  33.8 6.9 %collective-permute-start.10 = (bf16[48,512]{1,0:T(8,128)(2,1)S(1)}, bf16[48,512]{1,0:T(8,128)(2,1)S(1)}, u32[]{:S(2)}, u32[]{:S(2)}) collective-permute-start(bf16[48,512]{1,0:T(8,128)(2,1)S(1)} %get-tuple-element.41), channel_id=1, source_target_pairs={{0,16},{4,20},{8,24},{12,28},{16,0},{20,4},{24,8},{28,12},{1,17},{... | collective-permute-start | bytes 147464 | tf_op jit(solution)/shard_map/ppermute | solution.py:32
  36.0 5.7 %collective-permute-start.11 = (bf16[48,512]{1,0:T(8,128)(2,1)S(1)}, bf16[48,512]{1,0:T(8,128)(2,1)S(1)}, u32[]{:S(2)}, u32[]{:S(2)}) collective-permute-start(bf16[48,512]{1,0:T(8,128)(2,1)S(1)} %get-tuple-element.42), channel_id=1, source_target_pairs={{0,12},{4,8},{8,4},{12,0},{16,28},{20,24},{24,20},{28,16},{1,13},{... | collective-permute-start | bytes 147464 | tf_op jit(solution)/shard_map/ppermute | solution.py:32
  38.2 4.1 %collective-permute-start.12 = (bf16[48,512]{1,0:T(8,128)(2,1)S(1)}, bf16[48,512]{1,0:T(8,128)(2,1)S(1)}, u32[]{:S(2)}, u32[]{:S(2)}) collective-permute-start(bf16[48,512]{1,0:T(8,128)(2,1)S(1)} %get-tuple-element.43), channel_id=1, source_target_pairs={{0,8},{4,12},{8,0},{12,4},{16,24},{20,28},{24,16},{28,20},{1,9},{5... | collective-permute-start | bytes 147464 | tf_op jit(solution)/shard_map/ppermute | solution.py:32
  39.0 4.1 %collective-permute-start.13 = (bf16[48,512]{1,0:T(8,128)(2,1)S(1)}, bf16[48,512]{1,0:T(8,128)(2,1)S(1)}, u32[]{:S(2)}, u32[]{:S(2)}) collective-permute-start(bf16[48,512]{1,0:T(8,128)(2,1)S(1)} %get-tuple-element.44), channel_id=1, source_target_pairs={{0,4},{4,0},{8,12},{12,8},{16,20},{20,16},{24,28},{28,24},{1,5},{5... | collective-permute-start | bytes 147464 | tf_op jit(solution)/shard_map/ppermute | solution.py:32
  44.5 1.5 %collective-permute-start.14 = (bf16[64,1536]{1,0:T(8,128)(2,1)S(1)}, bf16[64,1536]{1,0:T(8,128)(2,1)S(1)}, u32[]{:S(2)}, u32[]{:S(2)}) collective-permute-start(bf16[64,1536]{1,0:T(8,128)(2,1)S(1)} %get-tuple-element.46), channel_id=1, source_target_pairs={{0,1},{1,0},{2,3},{3,2},{4,5},{5,4},{6,7},{7,6},{8,9},{9,8},{10,11... | collective-permute-start | bytes 589832 | tf_op jit(solution)/shard_map/ppermute | solution.py:32
  46.1 4.9 %collective-permute-start.15 = (bf16[32,1536]{1,0:T(8,128)(2,1)S(1)}, bf16[32,1536]{1,0:T(8,128)(2,1)S(1)}, u32[]{:S(2)}, u32[]{:S(2)}) collective-permute-start(bf16[32,1536]{1,0:T(8,128)(2,1)S(1)} %add_convert_fusion.2), channel_id=1, source_target_pairs={{0,2},{1,3},{2,0},{3,1},{4,6},{5,7},{6,4},{7,5},{8,10},{9,11},{10,... | collective-permute-start | bytes 294920 | tf_op jit(solution)/shard_map/ppermute | solution.py:32
  51.5 7.3 %collective-permute-start.19 = (bf16[32,1664]{1,0:T(8,128)(2,1)S(1)}, bf16[32,1664]{1,0:T(8,128)(2,1)S(1)}, u32[]{:S(2)}, u32[]{:S(2)}) collective-permute-start(bf16[32,1664]{1,0:T(8,128)(2,1)S(1)} %get-tuple-element.50.order_ref.refs_0_), channel_id=1, source_target_pairs={{0,16},{4,20},{8,24},{12,28},{16,0},{20,4},{24,8},{28,12},{1,17},{... | collective-permute-start | bytes 319496 | tf_op jit(solution)/shard_map/ppermute | solution.py:32
  53.8 7.3 %collective-permute-start.18 = (bf16[32,1664]{1,0:T(8,128)(2,1)S(1)}, bf16[32,1664]{1,0:T(8,128)(2,1)S(1)}, u32[]{:S(2)}, u32[]{:S(2)}) collective-permute-start(bf16[32,1664]{1,0:T(8,128)(2,1)S(1)} %get-tuple-element.50.order_ref.refs_0_), channel_id=1, source_target_pairs={{0,12},{4,8},{8,4},{12,0},{16,28},{20,24},{24,20},{28,16},{1,13},{... | collective-permute-start | bytes 319496 | tf_op jit(solution)/shard_map/ppermute | solution.py:32
  55.9 9.6 %collective-permute-start.17 = (bf16[32,1664]{1,0:T(8,128)(2,1)S(1)}, bf16[32,1664]{1,0:T(8,128)(2,1)S(1)}, u32[]{:S(2)}, u32[]{:S(2)}) collective-permute-start(bf16[32,1664]{1,0:T(8,128)(2,1)S(1)} %get-tuple-element.50.order_ref.refs_0_), channel_id=1, source_target_pairs={{0,8},{4,12},{8,0},{12,4},{16,24},{20,28},{24,16},{28,20},{1,9},{5... | collective-permute-start | bytes 319496 | tf_op jit(solution)/shard_map/ppermute | solution.py:32
  55.9 9.6 %collective-permute-start.16 = (bf16[32,1664]{1,0:T(8,128)(2,1)S(1)}, bf16[32,1664]{1,0:T(8,128)(2,1)S(1)}, u32[]{:S(2)}, u32[]{:S(2)}) collective-permute-start(bf16[32,1664]{1,0:T(8,128)(2,1)S(1)} %get-tuple-element.50.order_ref.refs_0_), channel_id=1, source_target_pairs={{0,4},{4,0},{8,12},{12,8},{16,20},{20,16},{24,28},{28,24},{1,5},{5... | collective-permute-start | bytes 319496 | tf_op jit(solution)/shard_map/ppermute | solution.py:32
  58.8 6.7 %collective-permute-start.22 = (bf16[32,1664]{1,0:T(8,128)(2,1)S(1)}, bf16[32,1664]{1,0:T(8,128)(2,1)S(1)}, u32[]{:S(2)}, u32[]{:S(2)}) collective-permute-start(bf16[32,1664]{1,0:T(8,128)(2,1)S(1)} %collective-permute-done.19.refs_4_), channel_id=1, source_target_pairs={{0,12},{4,8},{8,4},{12,0},{16,28},{20,24},{24,20},{28,16},{1,13},{... | collective-permute-start | bytes 319496 | tf_op jit(solution)/shard_map/ppermute | solution.py:32
  59.7 6.2 %collective-permute-start.21 = (bf16[32,1664]{1,0:T(8,128)(2,1)S(1)}, bf16[32,1664]{1,0:T(8,128)(2,1)S(1)}, u32[]{:S(2)}, u32[]{:S(2)}) collective-permute-start(bf16[32,1664]{1,0:T(8,128)(2,1)S(1)} %collective-permute-done.19.refs_4_), channel_id=1, source_target_pairs={{0,8},{4,12},{8,0},{12,4},{16,24},{20,28},{24,16},{28,20},{1,9},{5... | collective-permute-start | bytes 319496 | tf_op jit(solution)/shard_map/ppermute | solution.py:32
  61.0 5.2 %collective-permute-start.20 = (bf16[32,1664]{1,0:T(8,128)(2,1)S(1)}, bf16[32,1664]{1,0:T(8,128)(2,1)S(1)}, u32[]{:S(2)}, u32[]{:S(2)}) collective-permute-start(bf16[32,1664]{1,0:T(8,128)(2,1)S(1)} %collective-permute-done.19.refs_4_), channel_id=1, source_target_pairs={{0,4},{4,0},{8,12},{12,8},{16,20},{20,16},{24,28},{28,24},{1,5},{5... | collective-permute-start | bytes 319496 | tf_op jit(solution)/shard_map/ppermute | solution.py:32
  69.6 6.7 %collective-permute-start.23 = (bf16[32,1536]{1,0:T(8,128)(2,1)S(1)}, bf16[32,1536]{1,0:T(8,128)(2,1)S(1)}, u32[]{:S(2)}, u32[]{:S(2)}) collective-permute-start(bf16[32,1536]{1,0:T(8,128)(2,1)S(1)} %get-tuple-element.53), channel_id=1, source_target_pairs={{0,12},{4,8},{8,4},{12,0},{16,28},{20,24},{24,20},{28,16},{1,13},{... | collective-permute-start | bytes 294920 | tf_op jit(solution)/shard_map/ppermute | solution.py:32
  71.6 6.3 %collective-permute-start.24 = (bf16[32,1536]{1,0:T(8,128)(2,1)S(1)}, bf16[32,1536]{1,0:T(8,128)(2,1)S(1)}, u32[]{:S(2)}, u32[]{:S(2)}) collective-permute-start(bf16[32,1536]{1,0:T(8,128)(2,1)S(1)} %get-tuple-element.54), channel_id=1, source_target_pairs={{0,8},{4,12},{8,0},{12,4},{16,24},{20,28},{24,16},{28,20},{1,9},{5... | collective-permute-start | bytes 294920 | tf_op jit(solution)/shard_map/ppermute | solution.py:32
  72.2 6.4 %collective-permute-start.25 = (bf16[32,1536]{1,0:T(8,128)(2,1)S(1)}, bf16[32,1536]{1,0:T(8,128)(2,1)S(1)}, u32[]{:S(2)}, u32[]{:S(2)}) collective-permute-start(bf16[32,1536]{1,0:T(8,128)(2,1)S(1)} %get-tuple-element.55), channel_id=1, source_target_pairs={{0,4},{4,0},{8,12},{12,8},{16,20},{20,16},{24,28},{28,24},{1,5},{5... | collective-permute-start | bytes 294920 | tf_op jit(solution)/shard_map/ppermute | solution.py:32
  73.2 7.6 %collective-permute-start.27 = (bf16[32,1536]{1,0:T(8,128)(2,1)S(1)}, bf16[32,1536]{1,0:T(8,128)(2,1)S(1)}, u32[]{:S(2)}, u32[]{:S(2)}) collective-permute-start(bf16[32,1536]{1,0:T(8,128)(2,1)S(1)} %get-tuple-element.56), channel_id=1, source_target_pairs={{0,12},{4,8},{8,4},{12,0},{16,28},{20,24},{24,20},{28,16},{1,13},{... | collective-permute-start | bytes 294920 | tf_op jit(solution)/shard_map/ppermute | solution.py:32
  75.1 6.4 %collective-permute-start.28 = (bf16[32,1536]{1,0:T(8,128)(2,1)S(1)}, bf16[32,1536]{1,0:T(8,128)(2,1)S(1)}, u32[]{:S(2)}, u32[]{:S(2)}) collective-permute-start(bf16[32,1536]{1,0:T(8,128)(2,1)S(1)} %get-tuple-element.57), channel_id=1, source_target_pairs={{0,8},{4,12},{8,0},{12,4},{16,24},{20,28},{24,16},{28,20},{1,9},{5... | collective-permute-start | bytes 294920 | tf_op jit(solution)/shard_map/ppermute | solution.py:32
  76.2 5.4 %collective-permute-start.29 = (bf16[32,1536]{1,0:T(8,128)(2,1)S(1)}, bf16[32,1536]{1,0:T(8,128)(2,1)S(1)}, u32[]{:S(2)}, u32[]{:S(2)}) collective-permute-start(bf16[32,1536]{1,0:T(8,128)(2,1)S(1)} %get-tuple-element.58), channel_id=1, source_target_pairs={{0,4},{4,0},{8,12},{12,8},{16,20},{20,16},{24,28},{28,24},{1,5},{5... | collective-permute-start | bytes 294920 | tf_op jit(solution)/shard_map/ppermute | solution.py:32
  78.6 5.6 %collective-permute-start.26 = (bf16[32,1536]{1,0:T(8,128)(2,1)S(1)}, bf16[32,1536]{1,0:T(8,128)(2,1)S(1)}, u32[]{:S(2)}, u32[]{:S(2)}) collective-permute-start(bf16[32,1536]{1,0:T(8,128)(2,1)S(1)} %add_convert_fusion.1), channel_id=1, source_target_pairs={{0,16},{4,20},{8,24},{12,28},{16,0},{20,4},{24,8},{28,12},{1,17},{... | collective-permute-start | bytes 294920 | tf_op jit(solution)/shard_map/ppermute | solution.py:32
  (17 other events, 185.5 us)
